TPU v7x, 32 devices: a whole 2x2x4 slice. The times are simulated.
32 devices in a mesh: dp: 8 (over y, x, core), seq: 4 (over z).
Axes of the slice: x: 2, y: 2, z: 4, core: 2. Of those that a mesh axis runs over, the one named last changes fastest.
Arguments:
- latents: bfloat16 [64, 256, 1152], P('dp', 'seq'), may hold values from -6 to 6
- condition: bfloat16 [64, 1152], P('dp'), may hold values from -6 to 6
- keep_order: int32 [64, 256], P('dp', 'seq'), may hold values from 0 to 63, as said below
- keep_count: int32 [64, 4], P('dp', 'seq'), may hold values from 16 to 48, as said below
- ada_weight: bfloat16 [1152, 6912], P('dp'), may hold values from -0.1875 to 0.1875
- ada_bias: bfloat16 [6912], replicated, may hold values from -3 to 3
- qkv_weight: bfloat16 [1152, 3456], P('dp'), may hold values from -0.1875 to 0.1875
- out_weight: bfloat16 [1152, 1152], P('dp'), may hold values from -0.75 to 0.75
- fc1_weight: bfloat16 [1152, 4608], P('dp'), may hold values from -0.1875 to 0.1875
- fc1_bias: bfloat16 [4608], replicated, may hold values from -3 to 3
- fc2_weight: bfloat16 [4608, 1152], P('dp'), may hold values from -0.09375 to 0.09375
- cotangent: bfloat16 [64, 256, 1152], P('dp', 'seq'), may hold values from -6 to 6
Outputs:
- block_out: bfloat16 [64, 256, 1152], P('dp', 'seq')
- latents_grad: float32 [64, 256, 1152], P('dp', 'seq')
- condition_grad: float32 [64, 1152], P('dp')
- ada_weight_grad: float32 [1152, 6912], P('dp', 'seq')
- ada_bias_grad: float32 [6912], replicated
- qkv_weight_grad: float32 [1152, 3456], P('dp', 'seq')
- out_weight_grad: float32 [1152, 1152], P('dp', 'seq')
- fc1_weight_grad: float32 [1152, 4608], P('dp', 'seq')
- fc1_bias_grad: float32 [4608], replicated
- fc2_weight_grad: float32 [4608, 1152], P('dp', 'seq')
- kept_total: int32 [1], replicated
Inputs may be any that keep to these rules, and one draw needn't show every extreme that they name: `keep_order`: in each aligned block of 64 tokens of a latent, a permutation of 0 to 63. `keep_count`: every latent has one block with 48 kept tokens and another with 16.
All inputs are finite; a program needn't handle non-finite values.
Results may differ from a plain program's by a relative error of at most 0.014.
The roundings to bfloat16 on the way count: a program that leaves them out, or rounds other values in their place, can miss the bound.
Values may be sent and summed in bfloat16 or wider, within the bound.
No kernel may reach another device: no remote copies, remote signals or barrier semaphores. Data moves between devices by JAX's collectives and lax.ppermute only.
A program may use at most 256 MiB of HBM per device.

v0:
```python
import math

import jax
import jax.numpy as jnp
from jax import lax
from jax.sharding import PartitionSpec as P

HEADS = 16
HEAD = 72


layer_eps = 1e-06
far_below = -1e30


def normalize(rows_in):
    center = rows_in - jnp.mean(rows_in, axis=-1, keepdims=True)
    inverse = lax.rsqrt(jnp.mean(center * center, axis=-1, keepdims=True) + layer_eps)
    return (center * inverse, inverse)


def normalize_back(grad_rows, normed, inverse):
    mean_grad = jnp.mean(grad_rows, axis=-1, keepdims=True)
    mean_proj = jnp.mean(grad_rows * normed, axis=-1, keepdims=True)
    return inverse * (grad_rows - mean_grad - normed * mean_proj)


def kept_rows(order_rows, count_rows):
    live_slot = lax.broadcasted_iota(jnp.int32, order_rows.shape, order_rows.ndim - 1) < count_rows
    positions = lax.broadcasted_iota(
        jnp.int32, order_rows.shape + (order_rows.shape[-1],), order_rows.ndim
    )
    matched = (order_rows[..., None] == positions) & live_slot[..., None]
    return jnp.any(matched, axis=-2)


def inner_rows(left_rows, right_rows):
    return lax.dot_general(
        left_rows, right_rows, (((0,), (0,)), ((), ())), preferred_element_type=jnp.float32
    )


def times_turned(left_rows, weight_full):
    return lax.dot_general(
        left_rows, weight_full, (((1,), (1,)), ((), ())), preferred_element_type=jnp.float32
    )


def scores_of(queries, key_block, mask_block, att_scale):
    raw_scores = (
        jnp.einsum("lqhe,lkhe->lqhk", queries, key_block, preferred_element_type=jnp.float32)
        * att_scale
    )
    return jnp.where(mask_block[:, None, None, :] > 0, raw_scores, far_below)


def body(
    latents,
    condition,
    keep_order,
    keep_count,
    ada_weight,
    ada_bias,
    qkv_weight,
    out_weight,
    fc1_weight,
    fc1_bias,
    fc2_weight,
    cotangent,
):
    latent_count, row_count, model_width = latents.shape
    token_count = latent_count * row_count
    att_scale = 1.0 / math.sqrt(HEAD)
    ada_full, qkv_full, out_full, fc1_full, fc2_full = (
        lax.all_gather(ada_weight, "dp", axis=0, tiled=True),
        lax.all_gather(qkv_weight, "dp", axis=0, tiled=True),
        lax.all_gather(out_weight, "dp", axis=0, tiled=True),
        lax.all_gather(fc1_weight, "dp", axis=0, tiled=True),
        lax.all_gather(fc2_weight, "dp", axis=0, tiled=True),
    )
    kept_mask = kept_rows(keep_order, keep_count)
    cond_wide = condition.astype(jnp.float32)
    silu_cond = jax.nn.silu(cond_wide).astype(jnp.bfloat16)
    modulation = jnp.dot(silu_cond, ada_full, preferred_element_type=jnp.float32) + ada_bias.astype(
        jnp.float32
    )
    shift_attn, scale_attn, gate_attn, shift_mlp, scale_mlp, gate_mlp = [
        part_rows[:, None, :] for part_rows in jnp.split(modulation, 6, axis=1)
    ]
    inputs_wide = latents.astype(jnp.float32)
    normed_one, inverse_one = normalize(inputs_wide)
    mixed_one = (
        (normed_one * (1.0 + scale_attn) + shift_attn)
        .astype(jnp.bfloat16)
        .reshape(token_count, model_width)
    )
    qkv_rows = jnp.dot(mixed_one, qkv_full, preferred_element_type=jnp.float32).astype(jnp.bfloat16)
    qkv_rows = qkv_rows.reshape(latent_count, row_count, 3, HEADS, HEAD)
    queries = qkv_rows[:, :, 0]
    key_rows = qkv_rows[:, :, 1]
    values = qkv_rows[:, :, 2]
    key_mask = kept_mask.astype(jnp.bfloat16)
    start_top = jnp.full((latent_count, row_count, HEADS), far_below, jnp.float32)
    key_block = lax.all_gather(key_rows, "seq", axis=1, tiled=True)
    value_block = lax.all_gather(values, "seq", axis=1, tiled=True)
    mask_block = lax.all_gather(key_mask, "seq", axis=1, tiled=True)
    logits = scores_of(queries, key_block, mask_block, att_scale)
    new_top = jnp.maximum(start_top, jnp.max(logits, axis=-1))
    raised = jnp.exp(logits - new_top[..., None])
    new_total = jnp.sum(raised, axis=-1)
    new_sum = jnp.einsum("lqhk,lkhe->lqhe", raised, value_block.astype(jnp.float32))
    attended = new_sum / new_total[..., None]
    log_sum = new_top + jnp.log(new_total)
    attended_low = attended.reshape(token_count, model_width).astype(jnp.bfloat16)
    projected = jnp.dot(attended_low, out_full, preferred_element_type=jnp.float32).reshape(
        latent_count, row_count, model_width
    )
    hidden_res = inputs_wide + gate_attn * projected
    normed_two, inverse_two = normalize(hidden_res)
    mixed_two = (
        (normed_two * (1.0 + scale_mlp) + shift_mlp)
        .astype(jnp.bfloat16)
        .reshape(token_count, model_width)
    )
    pre_act = jnp.dot(mixed_two, fc1_full, preferred_element_type=jnp.float32) + fc1_bias.astype(
        jnp.float32
    )
    activated = jax.nn.gelu(pre_act, approximate=True).astype(jnp.bfloat16)
    mlp_out = jnp.dot(activated, fc2_full, preferred_element_type=jnp.float32).reshape(
        latent_count, row_count, model_width
    )
    block_res = hidden_res + gate_mlp * mlp_out
    block_out = jnp.where(kept_mask[..., None], block_res, inputs_wide).astype(jnp.bfloat16)
    grad_output = cotangent.astype(jnp.float32)
    grad_block = jnp.where(kept_mask[..., None], grad_output, 0.0)
    grad_gate_mlp = jnp.sum(grad_block * mlp_out, axis=1)
    grad_mlp = (gate_mlp * grad_block).astype(jnp.bfloat16).reshape(token_count, model_width)
    fc2_grad = inner_rows(activated, grad_mlp)
    grad_act = times_turned(grad_mlp, fc2_full)
    gelu_value, gelu_back = jax.vjp(lambda pre_in: jax.nn.gelu(pre_in, approximate=True), pre_act)
    grad_pre = gelu_back(grad_act)[0].astype(jnp.bfloat16)
    fc1_bias_part = jnp.sum(grad_pre.astype(jnp.float32), axis=0)
    fc1_grad = inner_rows(mixed_two, grad_pre)
    grad_mixed_two = times_turned(grad_pre, fc1_full).reshape(latent_count, row_count, model_width)
    grad_scale_mlp = jnp.sum(grad_mixed_two * normed_two, axis=1)
    grad_shift_mlp = jnp.sum(grad_mixed_two, axis=1)
    grad_hidden = grad_block + normalize_back(
        grad_mixed_two * (1.0 + scale_mlp), normed_two, inverse_two
    )
    grad_gate_attn = jnp.sum(grad_hidden * projected, axis=1)
    grad_proj = (gate_attn * grad_hidden).astype(jnp.bfloat16).reshape(token_count, model_width)
    out_grad = inner_rows(attended_low, grad_proj)
    grad_att = (
        times_turned(grad_proj, out_full)
        .astype(jnp.bfloat16)
        .reshape(latent_count, row_count, HEADS, HEAD)
    )
    grad_att_wide = grad_att.astype(jnp.float32)
    row_delta = jnp.sum(grad_att_wide * attended, axis=-1)
    seq_count = lax.axis_size("seq")
    key_block = lax.all_gather(key_rows, "seq", axis=1, tiled=True)
    value_block = lax.all_gather(values, "seq", axis=1, tiled=True)
    mask_block = lax.all_gather(key_mask, "seq", axis=1, tiled=True)
    logits = scores_of(queries, key_block, mask_block, att_scale)
    probabilities = jnp.exp(logits - log_sum[..., None])
    grad_probs = jnp.einsum(
        "lqhe,lkhe->lqhk", grad_att, value_block, preferred_element_type=jnp.float32
    )
    grad_logits = (probabilities * (grad_probs - row_delta[..., None])).astype(jnp.bfloat16)
    grad_queries = (
        jnp.einsum("lqhk,lkhe->lqhe", grad_logits, key_block, preferred_element_type=jnp.float32)
        * att_scale
    )
    grad_keys = (
        jnp.einsum("lqhk,lqhe->lkhe", grad_logits, queries, preferred_element_type=jnp.float32)
        * att_scale
    )
    grad_values = jnp.einsum("lqhk,lqhe->lkhe", probabilities, grad_att_wide)
    block_rows = key_block.shape[1]
    pair_block = jnp.concatenate(
        [
            grad_keys.reshape(latent_count, block_rows, model_width),
            grad_values.reshape(latent_count, block_rows, model_width),
        ],
        axis=2,
    )
    grad_pairs = pair_block
    grad_queries, grad_pairs = (grad_queries, grad_pairs)
    own_pairs = lax.psum_scatter(grad_pairs, "seq", scatter_dimension=1, tiled=True)
    grad_qkv = jnp.concatenate(
        [grad_queries.reshape(latent_count, row_count, model_width), own_pairs], axis=2
    )
    grad_qkv = grad_qkv.astype(jnp.bfloat16).reshape(token_count, 3 * model_width)
    qkv_grad = inner_rows(mixed_one, grad_qkv)
    grad_mixed_one = times_turned(grad_qkv, qkv_full).reshape(latent_count, row_count, model_width)
    grad_scale_attn = jnp.sum(grad_mixed_one * normed_one, axis=1)
    grad_shift_attn = jnp.sum(grad_mixed_one, axis=1)
    grad_block_in = grad_hidden + normalize_back(
        grad_mixed_one * (1.0 + scale_attn), normed_one, inverse_one
    )
    latents_grad = jnp.where(kept_mask[..., None], grad_block_in, grad_output)
    grad_mod = jnp.concatenate(
        [
            grad_shift_attn,
            grad_scale_attn,
            grad_gate_attn,
            grad_shift_mlp,
            grad_scale_mlp,
            grad_gate_mlp,
        ],
        axis=1,
    )
    grad_mod, fc1_bias_seq = lax.psum((grad_mod, fc1_bias_part), "seq")
    grad_mod_low = grad_mod.astype(jnp.bfloat16)
    ada_bias_part = jnp.sum(grad_mod, axis=0)
    silu_value, silu_back = jax.vjp(jax.nn.silu, cond_wide)
    condition_grad = silu_back(times_turned(grad_mod_low, ada_full))[0]
    column_share = 6 * model_width // seq_count
    ada_columns = lax.dynamic_slice_in_dim(
        grad_mod_low, lax.axis_index("seq") * column_share, column_share, 1
    )
    ada_grad = inner_rows(silu_cond, ada_columns)
    ada_bias_grad, fc1_bias_grad = lax.psum((ada_bias_part, fc1_bias_seq), "dp")
    kept_total = lax.psum(jnp.sum(keep_count).reshape(1), ("dp", "seq"))
    ada_grad, qkv_grad, out_grad, fc1_grad, fc2_grad = (
        lax.psum_scatter(ada_grad, "dp", scatter_dimension=0, tiled=True),
        lax.psum_scatter(qkv_grad, "dp", scatter_dimension=0, tiled=True),
        lax.psum_scatter(out_grad, "dp", scatter_dimension=0, tiled=True),
        lax.psum_scatter(fc1_grad, "dp", scatter_dimension=0, tiled=True),
        lax.psum_scatter(fc2_grad, "dp", scatter_dimension=0, tiled=True),
    )
    qkv_grad, out_grad, fc1_grad, fc2_grad = (
        lax.psum_scatter(qkv_grad, "seq", scatter_dimension=1, tiled=True),
        lax.psum_scatter(out_grad, "seq", scatter_dimension=1, tiled=True),
        lax.psum_scatter(fc1_grad, "seq", scatter_dimension=1, tiled=True),
        lax.psum_scatter(fc2_grad, "seq", scatter_dimension=1, tiled=True),
    )
    return (
        block_out,
        latents_grad,
        condition_grad,
        ada_grad,
        ada_bias_grad,
        qkv_grad,
        out_grad,
        fc1_grad,
        fc1_bias_grad,
        fc2_grad,
        kept_total,
    )


def solution(mesh):
    placed = (
        P("dp", "seq", None),
        P("dp", None),
        P("dp", "seq"),
        P("dp", "seq"),
        P("dp", None),
        P(),
        P("dp", None),
        P("dp", None),
        P("dp", None),
        P(),
        P("dp", None),
        P("dp", "seq", None),
    )
    return jax.shard_map(
        body,
        mesh=mesh,
        in_specs=placed,
        out_specs=(
            P("dp", "seq", None),
            P("dp", "seq", None),
            P("dp", None),
            P("dp", "seq"),
            P(),
            P("dp", "seq"),
            P("dp", "seq"),
            P("dp", "seq"),
            P(),
            P("dp", "seq"),
            P(),
        ),
        check_vma=False,
    )
```

profile of v0, /device:TPU:8, one launch (start us, length us, event | category | flops | bytes accessed | tf_op | source)
XLA Modules:
  0.0 1878.0 jit_solution(13488227400705401866)
XLA Ops:
  9.5 87.9 %all-gather.11.cloned.1.call-done = bf16[1152,6912]{1,0:T(8,128)(2,1)} async-done(((bf16[144,6912]{1,0:T(8,128)(2,1)}), bf16[1152,6912]{1,0:T(8,128)(2,1)}) %all-gather.11.cloned.1.call-update) | async-done | bytes 15925264 | tf_op jit(solution)/shard_map/all_gather | solution.py:75
  97.4 7.7 convolution_add_fusion
  106.4 45.5 %all-gather.13.cloned.1.call-done = bf16[1152,3456]{1,0:T(8,128)(2,1)} async-done(((bf16[144,3456]{1,0:T(8,128)(2,1)}), bf16[1152,3456]{1,0:T(8,128)(2,1)}) %all-gather.13.cloned.1.call-update) | async-done | bytes 7962640 | tf_op jit(solution)/shard_map/all_gather | solution.py:76
  151.9 9.5 convolution_convert_fusion
  161.5 13.6 reshape.166
  175.1 5.7 fusion.91
  188.6 12.5 all-gather.2
  204.6 125.1 %all-gather.21.cloned.1.call-done = bf16[8,256,1,16,72]{4,3,2,0,1:T(8,128)(2,1)} async-done(((bf16[8,64,1,16,72]{4,3,2,0,1:T(8,128)(2,1)}), bf16[8,256,1,16,72]{4,3,2,0,1:T(8,128)(2,1)}) %all-gather.21.cloned.1.call-update) | async-done | bytes 4718608 | tf_op jit(solution)/shard_map/all_gather | solution.py:105
  329.6 11.6 copy.73
  341.2 137.8 %all-gather.23.cloned.1.call-done = bf16[8,256,1,16,72]{4,3,2,0,1:T(8,128)(2,1)} async-done(((bf16[8,64,1,16,72]{4,3,2,0,1:T(8,128)(2,1)}), bf16[8,256,1,16,72]{4,3,2,0,1:T(8,128)(2,1)}) %all-gather.23.cloned.1.call-update) | async-done | bytes 4718608 | tf_op jit(solution)/shard_map/all_gather | solution.py:104
  479.0 11.5 copy.76
  490.5 4.0 bitcast_reduce_fusion
  499.9 5.6 fusion.61
  512.2 5.4 fusion.90
  520.3 57.5 %all-gather.17.cloned.1.call-done = bf16[1152,4608]{1,0:T(8,128)(2,1)} async-done(((bf16[144,4608]{1,0:T(8,128)(2,1)}), bf16[1152,4608]{1,0:T(8,128)(2,1)}) %all-gather.17.cloned.1.call-update) | async-done | bytes 10616848 | tf_op jit(solution)/shard_map/all_gather | solution.py:78
  577.8 11.7 fusion.94
  589.5 54.1 %all-gather.19.cloned.1.call-done = bf16[4608,1152]{1,0:T(8,128)(2,1)} async-done(((bf16[576,1152]{1,0:T(8,128)(2,1)}), bf16[4608,1152]{1,0:T(8,128)(2,1)}) %all-gather.19.cloned.1.call-update) | async-done | bytes 10616848 | tf_op jit(solution)/shard_map/all_gather | solution.py:79
  643.5 16.3 convert_reduce_fusion
  659.8 12.4 fusion.57
  678.1 13.5 fusion.87
  700.9 5.0 reshape.172
  707.2 4.1 multiply_reduce_fusion
  711.4 10.6 fusion.13
  722.0 6.2 fusion.8
  728.2 9.9 copy.84
  738.1 7.3 broadcast_multiply_fusion
  745.4 9.7 copy.83
  755.1 12.6 pad_maximum_fusion
  772.6 5.8 fusion.95
  778.5 5.0 fusion.62
  788.5 292.0 %reduce-scatter.17.cloned.1.call-done = f32[8,64,2304]{2,1,0:T(8,128)} async-done(((f32[8,256,2304]{2,1,0:T(8,128)}), f32[8,64,2304]{2,1,0:T(8,128)}) %reduce-scatter.17.cloned.1.call-update) | async-done | bytes 4718608 | tf_op jit(solution)/shard_map/reduce_scatter | solution.py:189
  1083.6 7.9 convolution_bitcast_fusion
  1091.6 15.1 fusion.86
  1106.8 12.2 fusion.96
  1119.7 10.9 fusion.52
  1131.4 12.1 reduce-scatter.23.cloned.1.call-done
  1146.1 113.8 %reduce-scatter.21.cloned.1.call-done = f32[144,3456]{1,0:T(8,128)} async-done(((f32[1152,3456]{1,0:T(8,128)}), f32[144,3456]{1,0:T(8,128)}) %reduce-scatter.21.cloned.1.call-update) | async-done | bytes 1990672 | tf_op jit(solution)/shard_map/reduce_scatter | solution.py:227
  1263.5 137.6 %reduce-scatter.29.cloned.1.call-done = f32[576,1152]{1,0:T(8,128)} async-done(((f32[4608,1152]{1,0:T(8,128)}), f32[576,1152]{1,0:T(8,128)}) %reduce-scatter.29.cloned.1.call-update) | async-done | bytes 2654224 | tf_op jit(solution)/shard_map/reduce_scatter | solution.py:230
  1404.7 137.4 %reduce-scatter.25.cloned.1.call-done = f32[144,4608]{1,0:T(8,128)} async-done(((f32[1152,4608]{1,0:T(8,128)}), f32[144,4608]{1,0:T(8,128)}) %reduce-scatter.25.cloned.1.call-update) | async-done | bytes 2654224 | tf_op jit(solution)/shard_map/reduce_scatter | solution.py:229
  1542.3 38.0 %all-reduce.3.cloned.1.call-done = f32[8,6912]{1,0:T(8,128)} async-done(((f32[8,6912]{1,0:T(8,128)}), f32[8,6912]{1,0:T(8,128)}) %all-reduce.3.cloned.1.call-update) | async-done | bytes 221200 | tf_op jit(solution)/shard_map/psum | solution.py:213
  1582.6 4.5 fusion.75
  1588.4 39.7 %psum.39 = s32[1]{0:T(128)} all-reduce(s32[1]{0:T(128)} %bitcast.25), channel_id=1, replica_groups=mesh['dp'=8,'seq'=4] {'dp','seq'}, use_global_device_ids=true, to_apply=%region_35.36 | all-reduce | flops 1 | bytes 8 | tf_op jit(solution)/shard_map/psum | solution.py:224
  1628.2 21.7 %psum.37 = f32[4608]{0:T(1024)} all-reduce(f32[4608]{0:T(1024)} %get-tuple-element.75), channel_id=1, replica_groups=mesh['dp'=8,'seq'=4] {'seq'}, use_global_device_ids=true, to_apply=%region_30.31 | all-reduce | flops 4608 | bytes 36864 | tf_op jit(solution)/shard_map/psum | solution.py:213
  1656.0 23.9 %all-reduce = (f32[6912]{0:T(1024)}, f32[4608]{0:T(1024)}) all-reduce(f32[6912]{0:T(1024)} %get-tuple-element.86, f32[4608]{0:T(1024)} %psum.37), channel_id=1, replica_groups=mesh['dp'=8,'seq'=4] {'dp'}, use_global_device_ids=true, to_apply=%region_22.23 | all-reduce | flops 11520 | bytes 92160 | tf_op jit(solution)/shard_map/psum | solution.py:223
  1679.8 10.4 fusion.74
  1692.4 47.3 %reduce-scatter.35.cloned.1.call-done = f32[288,576]{1,0:T(8,128)} async-done(((f32[1152,576]{1,0:T(8,128)}), f32[288,576]{1,0:T(8,128)}) %reduce-scatter.35.cloned.1.call-update) | async-done | bytes 663568
  1739.7 55.2 %reduce-scatter.27.cloned.1.call-done = f32[144,1152]{1,0:T(8,128)} async-done(((f32[144,4608]{1,0:T(8,128)}), f32[144,1152]{1,0:T(8,128)}) %reduce-scatter.27.cloned.1.call-update) | async-done | bytes 663568 | tf_op jit(solution)/shard_map/reduce_scatter | solution.py:235
  1794.9 75.8 %reduce-scatter.19.cloned.1.call-done = f32[144,1728]{1,0:T(8,128)} async-done(((f32[1152,1728]{1,0:T(8,128)}), f32[144,1728]{1,0:T(8,128)}) %reduce-scatter.19.cloned.1.call-update) | async-done | bytes 995344 | tf_op jit(solution)/shard_map/reduce_scatter | solution.py:226
  (200 shorter events, 82.2 us)
Async XLA Ops:
  7.2 90.2 %copy-start.30 = (bf16[8,1152]{1,0:T(8,128)(2,1)S(1)}, bf16[8,1152]{1,0:T(8,128)(2,1)}, u32[]{:S(2)}) copy-start(bf16[8,1152]{1,0:T(8,128)(2,1)} %param.13) | copy-start | bytes 55300
  7.2 90.2 %all-gather.11.cloned.1.call-start = ((), (), s32[]{:S(2)}) async-start(), calls=%async_computation.10 | async-start | bytes 17915904 | tf_op jit(solution)/shard_map/all_gather | solution.py:75
  7.9 144.0 %all-gather.13.cloned.1.call-start = ((), (), s32[]{:S(2)}) async-start(), calls=%async_computation.11 | async-start | bytes 8957952 | tf_op jit(solution)/shard_map/all_gather | solution.py:76
  8.7 320.9 %all-gather.21.cloned.1.call-start = ((), (), s32[]{:S(2)}) async-start(), calls=%async_computation.23 | async-start | bytes 10485760 | tf_op jit(solution)/shard_map/all_gather | solution.py:105
  9.0 96.7 %copy-start.40 = (f32[8,64]{1,0:T(8,128)}, f32[8,64]{1,0:T(8,128)S(1)}, u32[]{:S(2)}) copy-start(f32[8,64]{1,0:T(8,128)S(1)} %broadcast_multiply_fusion.5) | copy-start | bytes 6148
  9.5 96.3 %copy-start.42 = (f32[8,64]{1,0:T(8,128)}, f32[8,64]{1,0:T(8,128)S(1)}, u32[]{:S(2)}) copy-start(f32[8,64]{1,0:T(8,128)S(1)} %add_rsqrt_fusion.1) | copy-start | bytes 6148
  105.7 55.7 %copy-start.27 = (f32[8,1152]{1,0:T(8,128)}, f32[8,1152]{1,0:T(8,128)S(1)}, u32[]{:S(2)}) copy-start(f32[8,1152]{1,0:T(8,128)S(1)} %get-tuple-element.92) | copy-start | bytes 110596
  105.7 96.2 %copy-start.28 = (f32[8,1152]{1,0:T(8,128)}, f32[8,1152]{1,0:T(8,128)S(1)}, u32[]{:S(2)}) copy-start(f32[8,1152]{1,0:T(8,128)S(1)} %get-tuple-element.88) | copy-start | bytes 110596
  106.4 55.1 %copy-start.12 = (bf16[8,64,1152]{2,1,0:T(8,128)(2,1)}, bf16[8,64,1152]{2,1,0:T(8,128)(2,1)S(1)}, u32[]{:S(2)}) copy-start(bf16[8,64,1152]{2,1,0:T(8,128)(2,1)S(1)} %fusion.47) | copy-start | bytes 3538948
  180.8 309.7 %copy-start.2 = (bf16[8,64,1,16,72]{4,3,2,1,0:T(8,128)(2,1)}, bf16[8,64,1,16,72]{4,3,2,1,0:T(8,128)(2,1)S(1)}, u32[]{:S(2)}) copy-start(bf16[8,64,1,16,72]{4,3,2,1,0:T(8,128)(2,1)S(1)} %get-tuple-element.82) | copy-start | bytes 3538948
  182.7 296.3 %all-gather.23.cloned.1.call-start = ((), (), s32[]{:S(2)}) async-start(), calls=%async_computation.24 | async-start | bytes 10485760 | tf_op jit(solution)/shard_map/all_gather | solution.py:104
  186.3 15.0 copy-start.47
  186.4 325.8 %all-gather.15.cloned.1.call-start = ((), (), s32[]{:S(2)}) async-start(), calls=%async_computation.12 | async-start | bytes 2985984 | tf_op jit(solution)/shard_map/all_gather | solution.py:77
  187.0 390.8 %all-gather.17.cloned.1.call-start = ((), (), s32[]{:S(2)}) async-start(), calls=%async_computation.13 | async-start | bytes 11943936 | tf_op jit(solution)/shard_map/all_gather | solution.py:78
  187.5 456.0 %all-gather.19.cloned.1.call-start = ((), (), s32[]{:S(2)}) async-start(), calls=%async_computation.14 | async-start | bytes 11943936 | tf_op jit(solution)/shard_map/all_gather | solution.py:79
  188.3 892.2 %reduce-scatter.17.cloned.1.call-start = ((), (), s32[]{:S(2)}) async-start(), calls=%async_computation.15 | async-start | bytes 23592960 | tf_op jit(solution)/shard_map/reduce_scatter | solution.py:189
  512.2 5.8 copy-start.19
  512.2 5.8 copy-start.22
  512.2 6.4 copy-start.23
  512.2 6.4 copy-start.34
  643.5 16.3 copy-start.24
  659.8 12.4 copy-start.14
  678.1 13.6 copy-start.6
  678.1 13.6 copy-start.10
  678.1 13.6 copy-start.17
  678.1 13.6 copy-start.25
  678.1 13.6 copy-start.29
  678.1 13.6 copy-start.45
  700.9 6.4 copy-start.20
  707.2 14.8 slice-start
  711.4 10.7 slice-start.1
  728.2 9.9 copy-start.3
  767.7 375.8 %reduce-scatter.23.cloned.1.call-start = ((), (), s32[]{:S(2)}) async-start(), calls=%async_computation.19 | async-start | bytes 5971968 | tf_op jit(solution)/shard_map/reduce_scatter | solution.py:228
  778.5 481.4 %reduce-scatter.21.cloned.1.call-start = ((), (), s32[]{:S(2)}) async-start(), calls=%async_computation.18 | async-start | bytes 17915904 | tf_op jit(solution)/shard_map/reduce_scatter | solution.py:227
  1091.5 309.6 %reduce-scatter.29.cloned.1.call-start = ((), (), s32[]{:S(2)}) async-start(), calls=%async_computation.22 | async-start | bytes 23887872 | tf_op jit(solution)/shard_map/reduce_scatter | solution.py:230
  1106.7 435.4 %reduce-scatter.25.cloned.1.call-start = ((), (), s32[]{:S(2)}) async-start(), calls=%async_computation.20 | async-start | bytes 23887872 | tf_op jit(solution)/shard_map/reduce_scatter | solution.py:229
  1119.0 461.3 %all-reduce.3.cloned.1.call-start = ((), (), s32[]{:S(2)}) async-start(), calls=%async_computation.16 | async-start | bytes 442368 | tf_op jit(solution)/shard_map/psum | solution.py:213
  1119.6 10.9 copy-start.39
  1119.7 10.9 copy-start.36
  1119.7 11.0 copy-start.35
  1119.7 11.0 copy-start.38
  1131.4 518.5 %reduce-scatter.33.cloned.1.call-start = ((), (), s32[]{:S(2)}) async-start(), calls=%async_computation.26 | async-start | bytes 1474560
  1146.0 544.2 %reduce-scatter.31.cloned.1.call-start = ((), (), s32[]{:S(2)}) async-start(), calls=%async_computation.25 | async-start | bytes 4423680
  1263.5 476.3 %reduce-scatter.35.cloned.1.call-start = ((), (), s32[]{:S(2)}) async-start(), calls=%async_computation.27 | async-start | bytes 3686400
  1404.7 177.9 %copy-start.31 = (bf16[8,1152]{1,0:T(8,128)(2,1)S(1)}, bf16[8,1152]{1,0:T(8,128)(2,1)}, u32[]{:S(2)}) copy-start(bf16[8,1152]{1,0:T(8,128)(2,1)} %param.13) | copy-start | bytes 55300
  1404.7 390.2 %reduce-scatter.27.cloned.1.call-start = ((), (), s32[]{:S(2)}) async-start(), calls=%async_computation.21 | async-start | bytes 3317760 | tf_op jit(solution)/shard_map/reduce_scatter | solution.py:235
  1542.2 328.5 %reduce-scatter.19.cloned.1.call-start = ((), (), s32[]{:S(2)}) async-start(), calls=%async_computation.17 | async-start | bytes 9289728 | tf_op jit(solution)/shard_map/reduce_scatter | solution.py:226
  1587.1 65.2 %copy-start.5 = (f32[8,64,1152]{2,1,0:T(8,128)S(1)}, f32[8,64,1152]{2,1,0:T(8,128)}, u32[]{:S(2)}) copy-start(f32[8,64,1152]{2,1,0:T(8,128)} %copy-done.4) | copy-start | bytes 7077892
  (24 other events, 62.3 us)
Sparse Core Ops, SparseCore 0:
  9.9 87.4 all-gather.10
  99.3 52.5 all-gather.12
  182.8 146.7 all-gather.20
  331.1 147.8 all-gather.22
  480.7 31.4 all-gather.14
  513.9 63.8 all-gather.16
  579.7 63.8 all-gather.18
  767.8 312.6 reduce-scatter.16
  1084.3 59.1 reduce-scatter.22
  1147.0 112.8 reduce-scatter.20
  1263.9 137.1 reduce-scatter.28
  1405.0 137.1 reduce-scatter.24
  1545.2 35.0 all-reduce.2
  1582.4 27.0 reduce-scatter.32
  1611.7 68.1 reduce-scatter.30
  1682.7 57.0 reduce-scatter.34
  1742.6 52.3 reduce-scatter.26
  1799.5 71.1 reduce-scatter.18
where the time goes:
time: 1890 us; the launch traced here: 1880 us
  waiting for transfers between devices  1420 us (75%)
  matrix products  185 us (10%)
  local copies, waits for them, and re-layouts  111 us (6%)
  blocking collectives  97.8 us (5%)
  other arithmetic  45.6 us (2%)
    reduce_scatter x1, waiting for transfers between devices, body(): lax.psum_scatter(grad_pairs, 'seq', scatter_dimension=1, tiled=True)  292 us
    all_gather x1, waiting for transfers between devices, body(): key_block = lax.all_gather(key_rows, 'seq', axis=1, tiled=True)  138 us
    reduce_scatter x1, waiting for transfers between devices, body(): lax.psum_scatter(fc2_grad, 'dp', scatter_dimension=0, tiled=True)  138 us
    reduce_scatter x1, waiting for transfers between devices, body(): lax.psum_scatter(fc1_grad, 'dp', scatter_dimension=0, tiled=True)  137 us
    all_gather x1, waiting for transfers between devices, body(): value_block = lax.all_gather(values, 'seq', axis=1, tiled=True)  125 us
    reduce_scatter x1, waiting for transfers between devices, body(): lax.psum_scatter(qkv_grad, 'dp', scatter_dimension=0, tiled=True)  114 us
    all_gather x1, waiting for transfers between devices, body(): lax.all_gather(ada_weight, 'dp', axis=0, tiled=True)  87.9 us
    reduce_scatter x1, waiting for transfers between devices, body(): lax.psum_scatter(ada_grad, 'dp', scatter_dimension=0, tiled=True)  75.8 us
  transfers between devices with their start and end apart: 18, of which 16 were waited for; matrix products, arithmetic and copies ran while one was open for 10% of the time, Pallas kernels for 0%

commit v1 on v0

v1 whole, which is shorter than its diff:
```python
import functools
import math

import jax
import jax.numpy as jnp
from jax import lax
from jax.experimental import pallas as pl
from jax.experimental.pallas import tpu as pltpu
from jax.sharding import PartitionSpec as P

HEADS = 16
HEAD = 72
LANES = 128
BLOCKS = 8

layer_eps = 1e-06
far_below = -1e30
att_scale = 1.0 / math.sqrt(HEAD)
gelu_c = math.sqrt(2.0 / math.pi)
gelu_k = 0.044715

BF = jnp.bfloat16
F32 = jnp.float32
VMEM = pl.BlockSpec(memory_space=pltpu.VMEM)
SMEM = pl.BlockSpec(memory_space=pltpu.SMEM)
ANY = pl.BlockSpec(memory_space=pl.ANY)
NT = (((1,), (1,)), ((), ()))
TN = (((0,), (0,)), ((), ()))


def swap(value, axis, step):
    return lax.ppermute(value, axis, [(i, i ^ step) for i in range(lax.axis_size(axis))])


def steps_of(axis):
    count = lax.axis_size(axis)
    return [1 << i for i in range(count.bit_length() - 1)]


def bit_set(axis, step):
    return (lax.axis_index(axis) & step) != 0


def gather_all(value, axis):
    value = value[None]
    for step in steps_of(axis):
        other = swap(value, axis, step)
        high = bit_set(axis, step)
        value = jnp.concatenate(
            [jnp.where(high, other, value), jnp.where(high, value, other)], axis=0
        )
    return value


def sum_own(value, axis):
    for step in reversed(steps_of(axis)):
        high = bit_set(axis, step)
        low_half, high_half = value[:step], value[step:]
        kept = jnp.where(high, high_half, low_half)
        value = kept + swap(jnp.where(high, low_half, high_half), axis, step)
    return value[0]


def trade_all(value, axis):
    count = value.shape[0]
    rest = value.shape[1:]
    for step in steps_of(axis):
        high = bit_set(axis, step)
        split = value.reshape((count // (2 * step), 2, step) + rest)
        low_half, high_half = split[:, 0], split[:, 1]
        kept = jnp.where(high, high_half, low_half)
        other = swap(jnp.where(high, low_half, high_half), axis, step)
        value = jnp.stack(
            [jnp.where(high, other, kept), jnp.where(high, kept, other)], axis=1
        ).reshape((count,) + rest)
    return value


def sum_everywhere(value):
    for axis in ("dp", "seq"):
        for step in steps_of(axis):
            value = value + swap(value, axis, step)
    return value


def after(value, *earlier):
    return lax.optimization_barrier((value,) + earlier)[0]


def halves_of(rows):
    first = (rows // 2 + 15) // 16 * 16
    return first, rows - first


def gather_weight(shard, first_after=(), second_after=()):
    rows = shard.shape[0]
    part, _ = halves_of(rows)
    if first_after:
        shard = after(shard, *first_after)
    beside_x = swap(shard, "dp", 2)
    beside_y = swap(shard, "dp", 4)
    own_pair = swap(shard, "dp", 1)
    across_a = swap(beside_y[:part], "dp", 2)
    across_b = swap(beside_x[part:], "dp", 4)
    held = [
        (shard, 0, 0),
        (beside_x, 2, 0),
        (beside_y, 4, 0),
        (across_a, 6, 0),
        (across_b, 6, part),
    ]
    pairs = [
        (own_pair, 1, 0),
        (swap(beside_x, "dp", 1), 3, 0),
        (swap(beside_y, "dp", 1), 5, 0),
        (swap(across_a, "dp", 1), 7, 0),
        (swap(across_b, "dp", 1), 7, part),
    ]
    return held + pairs, (beside_x, beside_y), (across_a, across_b)


def whole_weight(shard):
    full = lax.all_gather(shard, "dp", axis=0, tiled=True)
    rows = full.shape[0] // BLOCKS
    return [(full[k * rows : (k + 1) * rows], k, 0) for k in range(BLOCKS)]


def offsets_of(pieces, position, rows):
    return jnp.stack([position(k) * rows + first for _, k, first in pieces]).astype(jnp.int32)


def call(kernel, outs, ins, specs, scratch, flops, name):
    moved = sum(v.size * v.dtype.itemsize for v in ins) + sum(
        v.size * v.dtype.itemsize for v in jax.tree.leaves(outs)
    )
    return pl.pallas_call(
        kernel,
        out_shape=outs,
        in_specs=specs,
        out_specs=jax.tree.map(lambda _: VMEM, outs),
        scratch_shapes=scratch,
        name=name,
        cost_estimate=pl.CostEstimate(
            flops=int(flops), bytes_accessed=int(moved), transcendentals=0
        ),
        compiler_params=pltpu.CompilerParams(vmem_limit_bytes=56 * 1024 * 1024),
    )(*ins)


def start_pieces(offsets, refs, target, sem, lo, hi):
    copies = []
    for k, ref in enumerate(refs):
        rows = ref.shape[0]
        copies.append(
            pltpu.make_async_copy(
                ref.at[:, pl.ds(lo, hi - lo)],
                target.at[pl.ds(pl.multiple_of(offsets[k], 16), rows), :],
                sem.at[k],
            )
        )
    for one in copies:
        one.start()
    return copies


def wait_all(copies):
    for one in copies:
        one.wait()


def normal(rows_in):
    center = rows_in - jnp.mean(rows_in, axis=-1, keepdims=True)
    inverse = lax.rsqrt(jnp.mean(center * center, axis=-1, keepdims=True) + layer_eps)
    return center * inverse, inverse


def normal_back(grad_rows, normed, inverse):
    mean_grad = jnp.mean(grad_rows, axis=-1, keepdims=True)
    mean_proj = jnp.mean(grad_rows * normed, axis=-1, keepdims=True)
    return inverse * (grad_rows - mean_grad - normed * mean_proj)


def dot(left, right, dims=None):
    if dims is None:
        return jnp.dot(left, right, preferred_element_type=F32)
    return lax.dot_general(left, right, dims, preferred_element_type=F32)


def spans(total, width):
    return [(lo, min(lo + width, total)) for lo in range(0, total, width)]


def pack_rows(place_ref, piece_refs, latent, rows_out):
    gathered = jnp.concatenate([ref[latent] for ref in piece_refs], axis=0)
    slots = lax.broadcasted_iota(jnp.int32, (rows_out, gathered.shape[0]), 0)
    chosen = jnp.where(place_ref[latent] == slots, 1.0, 0.0).astype(BF)
    return dot(chosen, gathered)


def unpack_rows(place_ref, piece_refs, latent, packed, out_refs):
    rows_out = packed.shape[0]
    place = place_ref[latent]
    slots = lax.broadcasted_iota(jnp.int32, (place.shape[0], rows_out), 1)
    chosen = jnp.where(place == slots, 1.0, 0.0).astype(BF)
    spread = dot(chosen, packed)
    block = piece_refs[0].shape[1]
    for k, (piece, out) in enumerate(zip(piece_refs, out_refs)):
        here = slice(k * block, (k + 1) * block)
        out[latent] = jnp.where(
            place[here] >= 0, spread[here], piece[latent].astype(F32)
        ).astype(BF)


def split_parity(rows_low, order_ref, own_ref, other_ref):
    moved = dot(rows_low, order_ref[...]).astype(BF)
    width = own_ref.shape[1]
    own_ref[...] = moved[:, :width]
    other_ref[...] = moved[:, width:]


def enter_kernel(pieces, blocks, cap, *refs):
    (offsets, place, mod, order), refs = refs[:4], refs[4:]
    latents, refs = refs[:blocks], refs[blocks:]
    weights, refs = refs[:pieces], refs[pieces:]
    packed_out, qkv_out, own_out, other_out, weight, mixed, sem = refs
    width = qkv_out.shape[1]
    copies = start_pieces(offsets, weights, weight, sem, 0, width)
    for latent in range(mod.shape[0]):
        here = pl.ds(latent * cap, cap)
        rows = pack_rows(place, latents, latent, cap)
        packed_out[here, :] = rows.astype(BF)
        normed, _ = normal(rows)
        mixed[here, :] = (normed * (1.0 + mod[latent, 1:2, :]) + mod[latent, 0:1, :]).astype(BF)
    split_parity(mixed[...], order, own_out, other_out)
    wait_all(copies)
    for lo, hi in spans(width, 768):
        qkv_out[:, lo:hi] = dot(mixed[...], weight[:, lo:hi]).astype(BF)


def cot_kernel(blocks, cap, *refs):
    place, mod = refs[:2]
    cots = refs[2 : 2 + blocks]
    packed_out, mlp_out = refs[2 + blocks :]
    for latent in range(mod.shape[0]):
        here = pl.ds(latent * cap, cap)
        rows = pack_rows(place, cots, latent, cap)
        packed_out[here, :] = rows.astype(BF)
        mlp_out[here, :] = (mod[latent, 5:6, :] * rows).astype(BF)


def windows():
    found = []
    for head in range(HEADS):
        first = head * HEAD
        base = first // LANES * LANES
        width = LANES if first + HEAD <= base + LANES else 2 * LANES
        found.append((base, width, first - base))
    return found


def head_mask(width, first, dtype):
    lane = lax.broadcasted_iota(jnp.int32, (1, width), 1)
    return jnp.where((lane >= first) & (lane < first + HEAD), 1.0, 0.0).astype(dtype)


def attend_kernel(pieces, cap, model, *refs):
    (offsets, live, qkv, packed, mod, order), refs = refs[:6], refs[6:]
    weights, refs = refs[:pieces], refs[pieces:]
    (own_att, other_att, proj_out, hidden_out, mixed_out, own_mix, other_mix), refs = (
        refs[:7],
        refs[7:],
    )
    weight, attended, sem = refs
    copies = start_pieces(offsets, weights, weight, sem, 3 * model, 4 * model)
    attended[...] = jnp.zeros_like(attended)

    def one_latent(latent, carry):
        here = pl.ds(pl.multiple_of(latent * cap, 16), cap)
        count = live[latent]
        seen = lax.broadcasted_iota(jnp.int32, (cap, cap), 1) < count
        for base, width, first in windows():
            low_mask = head_mask(width, first, BF)
            query = qkv[here, base : base + width] * low_mask
            key = qkv[here, model + base : model + base + width]
            value = qkv[here, 2 * model + base : 2 * model + base + width]
            scores = jnp.where(seen, dot(query, key, NT) * att_scale, far_below)
            raised = jnp.exp(scores - jnp.max(scores, axis=-1, keepdims=True))
            total = jnp.sum(raised, axis=-1, keepdims=True)
            mixed = dot(raised.astype(BF), value) / total
            attended[here, base : base + width] += mixed * head_mask(width, first, F32)
        return carry

    lax.fori_loop(0, mod.shape[0], one_latent, 0)
    att_low = attended[...].astype(BF)
    split_parity(att_low, order, own_att, other_att)
    wait_all(copies)
    projected = dot(att_low, weight[...])
    proj_out[...] = projected
    for latent in range(mod.shape[0]):
        rows = slice(latent * cap, (latent + 1) * cap)
        hidden = packed[rows, :].astype(F32) + mod[latent, 2:3, :] * projected[rows]
        hidden_out[rows, :] = hidden
        normed, _ = normal(hidden)
        mixed_out[rows, :] = (
            normed * (1.0 + mod[latent, 4:5, :]) + mod[latent, 3:4, :]
        ).astype(BF)
    split_parity(mixed_out[...], order, own_mix, other_mix)


def first_kernel(pieces, *refs):
    (offsets, parity, mixed, bias), refs = refs[:4], refs[4:]
    weights, refs = refs[:pieces], refs[pieces:]
    own_act, other_act, own_slope, other_slope, weight, sem = refs
    copies = start_pieces(offsets, weights, weight, sem, 0, weight.shape[1])
    half = own_act.shape[1]
    wait_all(copies)
    for side, (act_out, slope_out) in enumerate(
        ((own_act, own_slope), (other_act, other_slope))
    ):
        base = (parity[0] ^ side) * half
        for lo, hi in spans(half, 768):
            cols = pl.ds(pl.multiple_of(base + lo, LANES), hi - lo)
            pre = dot(mixed[...], weight[:, cols]) + bias[:, cols]
            square = pre * pre
            curve = jnp.tanh(gelu_c * pre * (1.0 + gelu_k * square))
            cdf = 0.5 * (1.0 + curve)
            act_out[:, lo:hi] = (pre * cdf).astype(BF)
            slope = cdf + pre * (0.5 * gelu_c) * (1.0 - curve * curve) * (
                1.0 + 3.0 * gelu_k * square
            )
            slope_out[:, lo:hi] = slope.astype(BF)


def second_kernel(pieces, blocks, cap, *refs):
    (
        offsets,
        own_act,
        other_act,
        own_slope,
        other_slope,
        grad_mlp,
        grad_out,
        hidden,
        mod,
        place,
    ), refs = refs[:10], refs[10:]
    latents, refs = refs[:blocks], refs[blocks:]
    weights, refs = refs[:pieces], refs[pieces:]
    outs, refs = refs[:blocks], refs[blocks:]
    own_pre, other_pre, own_bias, other_bias, gate_grad, weight, sem = refs
    copies = start_pieces(offsets, weights, weight, sem, 0, weight.shape[1])
    half = own_act.shape[1]
    wait_all(copies)
    for side, (slope, pre_out, bias_out) in enumerate(
        ((own_slope, own_pre, own_bias), (other_slope, other_pre, other_bias))
    ):
        for lo, hi in spans(half, 768):
            grad_act = dot(grad_mlp[...], weight[side * half + lo : side * half + hi, :], NT)
            grad_pre = (grad_act * slope[:, lo:hi].astype(F32)).astype(BF)
            pre_out[:, lo:hi] = grad_pre
            bias_out[:, lo:hi] = jnp.sum(grad_pre.astype(F32), axis=0, keepdims=True)
    mlp = dot(own_act[...], weight[:half, :]) + dot(other_act[...], weight[half:, :])
    for latent in range(mod.shape[0]):
        rows = slice(latent * cap, (latent + 1) * cap)
        gate_grad[latent, :, :] = jnp.sum(
            grad_out[rows, :].astype(F32) * mlp[rows], axis=0, keepdims=True
        )
        block = (hidden[rows, :] + mod[latent, 5:6, :] * mlp[rows]).astype(BF)
        unpack_rows(place, latents, latent, block, outs)


def hidden_kernel(pieces, first_pieces, cap, model, *refs):
    (
        first_offsets,
        offsets,
        parity,
        own_pre,
        other_pre,
        hidden_in,
        projected,
        grad_out,
        mod,
    ), refs = refs[:9], refs[9:]
    first_weights, refs = refs[:first_pieces], refs[first_pieces:]
    out_weights, refs = refs[:pieces], refs[pieces:]
    grad_hidden, grad_proj, grad_att, mod_grads, first, out_weight, first_sem, out_sem = refs
    copies = start_pieces(first_offsets, first_weights, first, first_sem, 0, first.shape[1])
    later = start_pieces(offsets, out_weights, out_weight, out_sem, 3 * model, 4 * model)
    half = own_pre.shape[1]
    wait_all(copies)
    total = None
    for side, pre in enumerate((own_pre, other_pre)):
        base = (parity[0] ^ side) * half
        for lo, hi in spans(half, 768):
            cols = pl.ds(pl.multiple_of(base + lo, LANES), hi - lo)
            part = dot(pre[:, lo:hi], first[:, cols], NT)
            total = part if total is None else total + part
    for latent in range(mod.shape[0]):
        rows = slice(latent * cap, (latent + 1) * cap)
        normed, inverse = normal(hidden_in[rows, :])
        grad_mixed = total[rows]
        mod_grads[latent, 0:1, :] = jnp.sum(grad_mixed, axis=0, keepdims=True)
        mod_grads[latent, 1:2, :] = jnp.sum(grad_mixed * normed, axis=0, keepdims=True)
        grad = grad_out[rows, :].astype(F32) + normal_back(
            grad_mixed * (1.0 + mod[latent, 4:5, :]), normed, inverse
        )
        grad_hidden[rows, :] = grad
        mod_grads[latent, 2:3, :] = jnp.sum(grad * projected[rows, :], axis=0, keepdims=True)
        grad_proj[rows, :] = (mod[latent, 2:3, :] * grad).astype(BF)
    wait_all(later)
    grad_att[...] = dot(grad_proj[...], out_weight[...], NT).astype(BF)


def attend_back_kernel(cap, model, *refs):
    live, qkv, grad_att, grad_qkv, sums = refs
    sums[...] = jnp.zeros_like(sums)

    def one_latent(latent, carry):
        here = pl.ds(pl.multiple_of(latent * cap, 16), cap)
        count = live[latent]
        seen = lax.broadcasted_iota(jnp.int32, (cap, cap), 0) < count
        for base, width, first in windows():
            low_mask = head_mask(width, first, BF)
            wide_mask = head_mask(width, first, F32)
            cols = slice(base, base + width)
            key_cols = slice(model + base, model + base + width)
            value_cols = slice(2 * model + base, 2 * model + base + width)
            query, key, value = qkv[here, cols], qkv[here, key_cols], qkv[here, value_cols]
            grad = grad_att[here, cols]
            scores = jnp.where(seen, dot(key * low_mask, query, NT) * att_scale, far_below)
            raised = jnp.exp(scores - jnp.max(scores, axis=0, keepdims=True))
            probs = raised / jnp.sum(raised, axis=0, keepdims=True)
            grad_probs = dot(value * low_mask, grad, NT)
            delta = jnp.sum(probs * grad_probs, axis=0, keepdims=True)
            grad_scores = (probs * (grad_probs - delta)).astype(BF)
            scaled = wide_mask * att_scale
            sums[here, cols] += dot(grad_scores, key, TN) * scaled
            sums[here, key_cols] += dot(grad_scores, query) * scaled
            sums[here, value_cols] += dot(probs.astype(BF), grad) * wide_mask
        return carry

    lax.fori_loop(0, live.shape[0], one_latent, 0)
    grad_qkv[...] = sums[...].astype(BF)


def leave_kernel(pieces, blocks, cap, *refs):
    (offsets, grad_qkv, packed, grad_hidden, mod, place), refs = refs[:6], refs[6:]
    cots, refs = refs[:blocks], refs[blocks:]
    weights, refs = refs[:pieces], refs[pieces:]
    outs, refs = refs[:blocks], refs[blocks:]
    mod_grads, weight, sem = refs
    copies = start_pieces(offsets, weights, weight, sem, 0, weight.shape[1])
    wait_all(copies)
    total = None
    for lo, hi in spans(weight.shape[1], 768):
        part = dot(grad_qkv[:, lo:hi], weight[:, lo:hi], NT)
        total = part if total is None else total + part
    for latent in range(mod.shape[0]):
        rows = slice(latent * cap, (latent + 1) * cap)
        normed, inverse = normal(packed[rows, :].astype(F32))
        grad_mixed = total[rows]
        mod_grads[latent, 0:1, :] = jnp.sum(grad_mixed, axis=0, keepdims=True)
        mod_grads[latent, 1:2, :] = jnp.sum(grad_mixed * normed, axis=0, keepdims=True)
        grad = grad_hidden[rows, :] + normal_back(
            grad_mixed * (1.0 + mod[latent, 1:2, :]), normed, inverse
        )
        unpack_rows(place, cots, latent, grad.astype(BF), outs)


def outer_kernel(rows, used, sides, *refs):
    (block_at, own_left, pair_left), refs = refs[:3], refs[3:]
    own_rights, refs = refs[:sides], refs[sides:]
    pair_rights, refs = refs[:sides], refs[sides:]
    (send_x, send_y, keep, keep_x, keep_y), refs = refs[:5], refs[5:]
    result, sem = refs
    part, rest = halves_of(rows)
    left = jnp.concatenate([own_left[:, :used], pair_left[:, :used]], axis=0)
    base = 0
    for own, pair in zip(own_rights, pair_rights):
        width = own.shape[1]
        for lo, hi in spans(width, 768):
            right = jnp.concatenate([own[:, lo:hi], pair[:, lo:hi]], axis=0)
            result[:, base + lo : base + hi] = dot(left, right, TN).astype(BF)
        base += width

    def rows_at(k, first, count):
        return result.at[pl.ds(pl.multiple_of(block_at[k] * rows + first, 16), count), :]

    moves = [
        (rows_at(1, 0, part), send_x.at[0]),
        (rows_at(3, 0, part), send_x.at[1]),
        (rows_at(2, part, rest), send_y.at[0]),
        (rows_at(3, part, rest), send_y.at[1]),
        (rows_at(0, 0, rows), keep),
        (rows_at(1, part, rest), keep_x),
        (rows_at(2, 0, part), keep_y),
    ]
    copies = [pltpu.make_async_copy(a, b, sem.at[i]) for i, (a, b) in enumerate(moves)]
    for one in copies:
        one.start()
    wait_all(copies)


def outer_pair(own_left, pair_left, own_rights, pair_rights, rows, name):
    used = 4 * rows
    part, rest = halves_of(rows)
    width = sum(v.shape[1] for v in own_rights)
    block_at = jnp.stack([(lax.axis_index("dp") ^ (2 * k)) // 2 for k in range(4)]).astype(jnp.int32)
    ins = [block_at, own_left, pair_left, *own_rights, *pair_rights]
    specs = [SMEM] + [VMEM] * (len(ins) - 1)
    outs = (
        jax.ShapeDtypeStruct((2, part, width), BF),
        jax.ShapeDtypeStruct((2, rest, width), BF),
        jax.ShapeDtypeStruct((rows, width), BF),
        jax.ShapeDtypeStruct((rest, width), BF),
        jax.ShapeDtypeStruct((part, width), BF),
    )
    return pl.pallas_call(
        functools.partial(outer_kernel, rows, used, len(own_rights)),
        out_shape=outs,
        in_specs=specs,
        out_specs=tuple(ANY for _ in outs),
        scratch_shapes=[pltpu.VMEM((used, width), BF), pltpu.SemaphoreType.DMA((7,))],
        name=name,
        cost_estimate=pl.CostEstimate(
            flops=2 * used * width * own_left.shape[0] * 2,
            bytes_accessed=2 * (2 * used * width),
            transcendentals=0,
        ),
        compiler_params=pltpu.CompilerParams(vmem_limit_bytes=56 * 1024 * 1024),
    )(*ins)


def spread_blocks(cut, rows):
    send_x, send_y, keep, keep_x, keep_y = cut
    part, _ = halves_of(rows)
    from_x = swap(send_x, "dp", 2)
    from_y = swap(send_y, "dp", 4)
    on_y = (keep_y.astype(F32) + from_x[1].astype(F32)).astype(BF)
    on_x = (keep_x.astype(F32) + from_y[1].astype(F32)).astype(BF)
    last_y = swap(on_y, "dp", 4)
    last_x = swap(on_x, "dp", 2)
    near = jnp.concatenate([from_x[0], from_y[0]], axis=0).astype(F32)
    far = jnp.concatenate([last_y, last_x], axis=0).astype(F32)
    return keep.astype(F32) + near + far


def spread_columns(block, cut_columns):
    count = lax.axis_size("seq")
    at = lax.axis_index("seq")
    parts = jnp.stack([cut_columns(block, j) for j in range(count)])
    low_parts = parts.astype(BF)
    total = lax.dynamic_index_in_dim(parts, at, 0, keepdims=False)
    for step in range(1, count):
        piece = lax.dynamic_index_in_dim(low_parts, at ^ step, 0, keepdims=False)
        total = total + swap(piece, "seq", step).astype(F32)
    return total


def plain_columns(block, j):
    width = block.shape[1] // lax.axis_size("seq")
    return block[:, j * width : (j + 1) * width]


def spread_plain(grad):
    grad = lax.psum_scatter(grad, "dp", scatter_dimension=0, tiled=True)
    return lax.psum_scatter(grad, "seq", scatter_dimension=1, tiled=True)


def body(
    latents,
    condition,
    keep_order,
    keep_count,
    ada_weight,
    ada_bias,
    qkv_weight,
    out_weight,
    fc1_weight,
    fc1_bias,
    fc2_weight,
    cotangent,
):
    latent_count, block_rows, model = latents.shape
    hidden_units = fc1_weight.shape[1]
    half_units = hidden_units // 2
    unit_rows = hidden_units // BLOCKS
    model_rows = model // BLOCKS
    dp_count, seq_count = lax.axis_size("dp"), lax.axis_size("seq")
    dp_at, seq_at = lax.axis_index("dp"), lax.axis_index("seq")
    group = latent_count // seq_count
    cap = (seq_count - 1) * (block_rows * 3 // 4) + block_rows // 4
    rows_all = group * cap
    paired = dp_count == BLOCKS
    parity = (dp_at & 1) if paired else jnp.zeros_like(dp_at)
    parity_in = parity.reshape(1).astype(jnp.int32)

    joint = jnp.concatenate([qkv_weight, out_weight], axis=1)
    unit_order = lambda v: jnp.swapaxes(
        v.reshape(v.shape[0], BLOCKS // 2, 2, unit_rows), 1, 2
    ).reshape(v.shape[0], hidden_units)
    first_shard = unit_order(fc1_weight)
    if paired:
        joint_pieces, mark_a, mark_b = gather_weight(joint)
        first_pieces, mark_c, mark_d = gather_weight(first_shard, mark_a)
        second_pieces, _, _ = gather_weight(fc2_weight, mark_c)
        whose = lambda k: dp_at ^ k
    else:
        joint_pieces = whole_weight(joint)
        first_pieces = whole_weight(first_shard)
        second_pieces = whole_weight(fc2_weight)
        whose = lambda k: jnp.int32(k)
    joint_at = offsets_of(joint_pieces, whose, model_rows)
    first_at = offsets_of(first_pieces, whose, model_rows)
    second_at = offsets_of(
        second_pieces,
        lambda k: ((whose(k) & 1) ^ parity) * (BLOCKS // 2) + whose(k) // 2,
        unit_rows,
    )
    joint_w = [v for v, _, _ in joint_pieces]
    first_w = [v for v, _, _ in first_pieces]
    second_w = [v for v, _, _ in second_pieces]
    n_joint, n_first, n_second = len(joint_w), len(first_w), len(second_w)

    slot = lax.broadcasted_iota(jnp.int32, (1, block_rows, 1), 1)
    token = lax.broadcasted_iota(jnp.int32, (1, 1, block_rows), 2)
    found = (keep_order[:, :, None] == token) & (slot < keep_count[:, :, None])
    rank = jnp.max(jnp.where(found, slot, -1), axis=1)
    ranks = gather_all(rank, "seq")
    ranks = lax.dynamic_slice_in_dim(ranks, seq_at * group, group, 1)
    ranks = jnp.stack(
        [lax.dynamic_index_in_dim(ranks, seq_at ^ k, 0, keepdims=False) for k in range(seq_count)],
        axis=1,
    )
    counts = jnp.sum((ranks >= 0).astype(jnp.int32), axis=2)
    starts = jnp.cumsum(counts, axis=1) - counts
    live = jnp.sum(counts, axis=1).astype(jnp.int32)
    place = jnp.where(ranks >= 0, ranks + starts[:, :, None], -1).reshape(
        group, seq_count * block_rows
    )
    place_row = place[:, None, :]
    place_col = place[:, :, None]

    def to_whole(blocks_in):
        pieces = []
        for k in range(seq_count):
            piece = lax.dynamic_slice_in_dim(blocks_in, (seq_at ^ k) * group, group, 0)
            pieces.append(swap(piece, "seq", k) if k else piece)
        return pieces

    def to_blocks(pieces, dtype):
        result = jnp.zeros((latent_count, block_rows, model), dtype)
        for k, piece in enumerate(pieces):
            piece = swap(piece, "seq", k) if k else piece
            result = lax.dynamic_update_slice_in_dim(
                result, piece.astype(dtype), (seq_at ^ k) * group, 0
            )
        return result

    latent_pieces = to_whole(latents)
    cot_pieces = to_whole(cotangent)

    cond_wide = condition.astype(F32)
    silu_cond = jax.nn.silu(cond_wide).astype(BF)
    silu_mine = lax.dynamic_slice_in_dim(silu_cond, seq_at * group, group, 0)
    share = model // dp_count
    silu_rows = trade_all(
        jnp.swapaxes(silu_mine.reshape(group, dp_count, share), 0, 1), "dp"
    )
    partial = jnp.dot(
        silu_rows.reshape(dp_count * group, share), ada_weight, preferred_element_type=F32
    ).reshape(dp_count, group, 6 * model)
    mod = sum_own(partial, "dp") + ada_bias.astype(F32)
    mod = mod.reshape(group, 6, model)
    silu_all = gather_all(silu_rows, "seq")

    pad = -(-(model // 2) // LANES) * LANES
    column = lax.broadcasted_iota(jnp.int32, (1, 2 * pad), 1)
    side, inner = column // pad, column % pad
    source = (2 * (inner // model_rows) + (parity ^ side)) * model_rows + inner % model_rows
    source = jnp.where(inner < model // 2, source, -1)
    order = (lax.broadcasted_iota(jnp.int32, (model, 1), 0) == source).astype(BF)

    sds = jax.ShapeDtypeStruct
    flops = 2 * rows_all * model
    dma = lambda n: pltpu.SemaphoreType.DMA((n,))
    half_width = pad
    packed, qkv, mixa_own, mixa_other = call(
        functools.partial(enter_kernel, n_joint, seq_count, cap),
        (
            sds((rows_all, model), BF),
            sds((rows_all, 3 * model), BF),
            sds((rows_all, half_width), BF),
            sds((rows_all, half_width), BF),
        ),
        [joint_at, place_row, mod, order, *latent_pieces, *joint_w],
        [SMEM, VMEM, VMEM, VMEM] + [VMEM] * seq_count + [ANY] * n_joint,
        [pltpu.VMEM((model, 3 * model), BF), pltpu.VMEM((rows_all, model), BF), dma(n_joint)],
        flops * 4 * model,
        "enter",
    )
    grad_out, grad_mlp = call(
        functools.partial(cot_kernel, seq_count, cap),
        (sds((rows_all, model), BF), sds((rows_all, model), BF)),
        [place_row, mod, *cot_pieces],
        [VMEM] * (2 + seq_count),
        [],
        flops * 256,
        "cotangent",
    )
    att_own, att_other, projected, hidden, mixed, mixm_own, mixm_other = call(
        functools.partial(attend_kernel, n_joint, cap, model),
        (
            sds((rows_all, half_width), BF),
            sds((rows_all, half_width), BF),
            sds((rows_all, model), F32),
            sds((rows_all, model), F32),
            sds((rows_all, model), BF),
            sds((rows_all, half_width), BF),
            sds((rows_all, half_width), BF),
        ),
        [joint_at, live, qkv, packed, mod, order, *joint_w],
        [SMEM, SMEM, VMEM, VMEM, VMEM, VMEM] + [ANY] * n_joint,
        [pltpu.VMEM((model, model), BF), pltpu.VMEM((rows_all, model), F32), dma(n_joint)],
        flops * 6 * model,
        "attend",
    )
    bias_row = unit_order(fc1_bias.astype(F32)[None])
    act_own, act_other, slope_own, slope_other = call(
        functools.partial(first_kernel, n_first),
        tuple(sds((rows_all, half_units), BF) for _ in range(4)),
        [first_at, parity_in, mixed, bias_row, *first_w],
        [SMEM, SMEM, VMEM, VMEM] + [ANY] * n_first,
        [pltpu.VMEM((model, hidden_units), BF), dma(n_first)],
        flops * hidden_units,
        "first",
    )

    def weight_grad(left_own, left_other, rights, rows, name):
        pair_left = swap(left_other, "dp", 1)
        pair_rights = [swap(v, "dp", 1) for v in rights]
        if len(rights) == 2:
            pair_rights = pair_rights[::-1]
        cut = outer_pair(left_own, pair_left, rights, pair_rights, rows, name)
        return spread_blocks(cut, rows)

    join_left = lambda a, b: jnp.stack(
        [a[:, : model // 2].reshape(rows_all, 4, model_rows), b[:, : model // 2].reshape(rows_all, 4, model_rows)],
        axis=2,
    ).reshape(rows_all, model)
    inner = lambda a, b: dot(a, b, TN)

    if paired:
        fc2_grad = weight_grad(act_own, act_other, [grad_mlp], unit_rows, "fc2_grad")
        fc2_grad = spread_columns(fc2_grad, plain_columns)
    else:
        act = jnp.concatenate([act_own, act_other], axis=1)
        act = jnp.swapaxes(act.reshape(rows_all, 2, 4, unit_rows), 1, 2).reshape(
            rows_all, hidden_units
        )
        fc2_grad = spread_plain(inner(act, grad_mlp))

    result = call(
        functools.partial(second_kernel, n_second, seq_count, cap),
        tuple(sds((group, block_rows, model), BF) for _ in range(seq_count))
        + (
            sds((rows_all, half_units), BF),
            sds((rows_all, half_units), BF),
            sds((1, half_units), F32),
            sds((1, half_units), F32),
            sds((group, 1, model), F32),
        ),
        [
            second_at,
            act_own,
            act_other,
            slope_own,
            slope_other,
            grad_mlp,
            grad_out,
            hidden,
            mod,
            place_col,
            *latent_pieces,
            *second_w,
        ],
        [SMEM] + [VMEM] * (9 + seq_count) + [ANY] * n_second,
        [pltpu.VMEM((hidden_units, model), BF), dma(n_second)],
        flops * 2 * hidden_units,
        "second",
    )
    block_pieces = result[:seq_count]
    pre_own, pre_other, bias_own, bias_other, gate_m_grad = result[seq_count:]
    block_out = to_blocks(block_pieces, BF)

    if paired:
        fc1_grad = weight_grad(mixm_own, mixm_other, [pre_own, pre_other], model_rows, "fc1_grad")

        def unit_columns(block, j):
            a = block[:, j * unit_rows : (j + 1) * unit_rows]
            b = block[:, half_units + j * unit_rows : half_units + (j + 1) * unit_rows]
            return jnp.concatenate([a, b], axis=1)

        fc1_grad = spread_columns(fc1_grad, unit_columns)
        fc1_grad = jnp.where(
            parity == 1,
            jnp.concatenate([fc1_grad[:, unit_rows:], fc1_grad[:, :unit_rows]], axis=1),
            fc1_grad,
        )
    else:
        pre = jnp.concatenate([pre_own, pre_other], axis=1)
        pre = jnp.swapaxes(pre.reshape(rows_all, 2, 4, unit_rows), 1, 2).reshape(
            rows_all, hidden_units
        )
        fc1_grad = spread_plain(inner(join_left(mixm_own, mixm_other), pre))

    grad_hidden, grad_proj, grad_att, mod_grads = call(
        functools.partial(hidden_kernel, n_joint, n_first, cap, model),
        (
            sds((rows_all, model), F32),
            sds((rows_all, model), BF),
            sds((rows_all, model), BF),
            sds((group, 3, model), F32),
        ),
        [
            first_at,
            joint_at,
            parity_in,
            pre_own,
            pre_other,
            hidden,
            projected,
            grad_out,
            mod,
            *first_w,
            *joint_w,
        ],
        [SMEM, SMEM, SMEM] + [VMEM] * 6 + [ANY] * (n_first + n_joint),
        [
            pltpu.VMEM((model, hidden_units), BF),
            pltpu.VMEM((model, model), BF),
            dma(n_first),
            dma(n_joint),
        ],
        flops * 5 * model,
        "hidden_back",
    )
    grad_qkv = call(
        functools.partial(attend_back_kernel, cap, model),
        sds((rows_all, 3 * model), BF),
        [live, qkv, grad_att],
        [SMEM, VMEM, VMEM],
        [pltpu.VMEM((rows_all, 3 * model), F32)],
        flops * 8 * model,
        "attend_back",
    )
    if paired:
        out_grad = weight_grad(att_own, att_other, [grad_proj], model_rows, "out_grad")
        out_grad = spread_columns(out_grad, plain_columns)
        qkv_grad = weight_grad(mixa_own, mixa_other, [grad_qkv], model_rows, "qkv_grad")
        qkv_grad = spread_columns(qkv_grad, plain_columns)
    else:
        out_grad = spread_plain(inner(join_left(att_own, att_other), grad_proj))
        qkv_grad = spread_plain(inner(join_left(mixa_own, mixa_other), grad_qkv))

    result = call(
        functools.partial(leave_kernel, n_joint, seq_count, cap),
        tuple(sds((group, block_rows, model), BF) for _ in range(seq_count))
        + (sds((group, 2, model), F32),),
        [joint_at, grad_qkv, packed, grad_hidden, mod, place_col, *cot_pieces, *joint_w],
        [SMEM] + [VMEM] * (5 + seq_count) + [ANY] * n_joint,
        [pltpu.VMEM((model, 3 * model), BF), dma(n_joint)],
        flops * 3 * model,
        "leave",
    )
    latents_grad = to_blocks(result[:seq_count], F32)
    mod_first = result[seq_count]

    grad_mod = jnp.concatenate(
        [mod_first, mod_grads[:, 2:3], mod_grads[:, :2], gate_m_grad], axis=1
    ).reshape(group, 6 * model)
    bias_pair = jnp.where(
        parity == 1,
        jnp.concatenate([bias_other, bias_own], axis=0),
        jnp.concatenate([bias_own, bias_other], axis=0),
    )
    bias_part = jnp.swapaxes(bias_pair.reshape(2, BLOCKS // 2, unit_rows), 0, 1).reshape(
        hidden_units
    )
    kept_part = jnp.sum(keep_count).astype(F32).reshape(1)
    sums = sum_everywhere(jnp.concatenate([jnp.sum(grad_mod, axis=0), bias_part, kept_part]))
    ada_bias_grad = sums[: 6 * model]
    fc1_bias_grad = sums[6 * model : 6 * model + hidden_units]
    kept_total = sums[6 * model + hidden_units :].astype(jnp.int32)

    grad_mod_all = gather_all(grad_mod.astype(BF), "dp")
    column_share = 6 * model // seq_count
    by_column = jnp.stack(
        [grad_mod_all[:, :, j * column_share : (j + 1) * column_share] for j in range(seq_count)]
    )
    by_column = trade_all(by_column, "seq")
    ada_grad = dot(
        silu_all.reshape(seq_count * dp_count * group, share),
        by_column.reshape(seq_count * dp_count * group, column_share),
        TN,
    )
    cond_part = dot(grad_mod_all.reshape(dp_count * group, 6 * model), ada_weight, NT)
    cond_cols = trade_all(cond_part.reshape(dp_count, group, share), "dp")
    cond_mine = jnp.swapaxes(cond_cols, 0, 1).reshape(group, model)
    cond_rows = gather_all(cond_mine, "seq").reshape(latent_count, model)
    _, silu_back = jax.vjp(jax.nn.silu, cond_wide)
    condition_grad = silu_back(cond_rows)[0]
    return (
        block_out,
        latents_grad,
        condition_grad,
        ada_grad,
        ada_bias_grad,
        qkv_grad,
        out_grad,
        fc1_grad,
        fc1_bias_grad,
        fc2_grad,
        kept_total,
    )


def solution(mesh):
    placed = (
        P("dp", "seq", None),
        P("dp", None),
        P("dp", "seq"),
        P("dp", "seq"),
        P("dp", None),
        P(),
        P("dp", None),
        P("dp", None),
        P("dp", None),
        P(),
        P("dp", None),
        P("dp", "seq", None),
    )
    return jax.shard_map(
        body,
        mesh=mesh,
        in_specs=placed,
        out_specs=(
            P("dp", "seq", None),
            P("dp", "seq", None),
            P("dp", None),
            P("dp", "seq"),
            P(),
            P("dp", "seq"),
            P("dp", "seq"),
            P("dp", "seq"),
            P(),
            P("dp", "seq"),
            P(),
        ),
        check_vma=False,
    )
```

time: 1890 us -> 653 us (0.35)
  waiting for transfers between devices: 1420 us -> 314 us
  matrix products: 185 us -> 3.32 us
  Pallas kernels: 0 us -> 131 us
  blocking collectives: 97.8 us -> 0 us
  starting transfers between devices: 0.98 us -> 96 us
  local copies, waits for them, and re-layouts: 111 us -> 62.5 us
    reduce_scatter x7 -> x0, waiting for transfers between devices: 824 us -> none  [the longest x1 292 us: body(): lax.psum_scatter(grad_pairs, 'seq', scatter_dimension=1, tiled=True)]
    all_gather x7 -> x0, waiting for transfers between devices: 510 us -> none  [the longest x1 138 us: body(): key_block = lax.all_gather(key_rows, 'seq', axis=1, tiled=True)]
    ppermute x0 -> x101, waiting for transfers between devices: none -> 314 us  [swap(): lax.ppermute(value, axis, [(i, i ^ step) for i in range(lax.axis_size(axi...]
    dot_general x21 -> x3, matrix products: 185 us -> 3.32 us  [the longest x2 2.94 us: dot(): return lax.dot_general(left, right, dims, preferred_element_type=F32)]
    pallas_call x0 -> x12, Pallas kernels: none -> 131 us  [the longest x8 99.8 us: call(): pl.pallas_call(kernel, out_shape=outs, in_specs=specs, out_specs=jax.tree...]
    ppermute x0 -> x101, starting transfers between devices: none -> 96 us  [swap(): lax.ppermute(value, axis, [(i, i ^ step) for i in range(lax.axis_size(axi...]
    psum x3 -> x0, blocking collectives: 85.3 us -> none  [the longest x1 39.7 us: body(): kept_total = lax.psum(jnp.sum(keep_count).reshape(1), ('dp', 'seq'))]
    unnamed x21 -> x0, waiting for transfers between devices: 50.7 us -> none
  transfers between devices with their start and end apart: 18 -> 101, of which waited for: 16 -> 47; matrix products, arithmetic and copies ran while one was open for 10% -> 13% of each run, Pallas kernels for 0% -> 11%
where the time goes in v1:
time: 653 us; the launch traced here: 646 us
  waiting for transfers between devices  314 us (48%)
  Pallas kernels  131 us (20%)
  starting transfers between devices  96 us (15%)
  local copies, waits for them, and re-layouts  62.5 us (10%)
  other arithmetic  34.2 us (5%)
    ppermute x101, waiting for transfers between devices, swap(): lax.ppermute(value, axis, [(i, i ^ step) for i in range(lax.axis_size(axi...  314 us
    pallas_call x8, Pallas kernels, call(): pl.pallas_call(kernel, out_shape=outs, in_specs=specs, out_specs=jax.tree...  99.8 us
    ppermute x101, starting transfers between devices, swap(): lax.ppermute(value, axis, [(i, i ^ step) for i in range(lax.axis_size(axi...  96 us
    pallas_call x4, Pallas kernels, outer_pair(): pl.pallas_call(functools.partial(outer_kernel, rows, used, len(own_rights...  31.5 us
  transfers between devices with their start and end apart: 101, of which 47 were waited for; matrix products, arithmetic and copies ran while one was open for 13% of the time, Pallas kernels for 11%

profile of v1, /device:TPU:8, one launch (start us, length us, event | category | flops | bytes accessed | tf_op | source)
XLA Modules:
  0.0 646.3 jit_solution(17799361890726610135)
XLA Ops:
  13.4 21.2 %collective-permute-done.3 = bf16[2,2,2,144]{3,2,0,1:T(2,128)(2,1)S(1)} collective-permute-done((bf16[2,2,2,144]{3,2,0,1:T(2,128)(2,1)S(1)}, bf16[2,2,2,144]{3,2,0,1:T(2,128)(2,1)S(1)}, u32[]{:S(2)}, u32[]{:S(2)}) %collective-permute-start.3) | collective-permute-done | bytes 2336 | tf_op jit(solution)/shard_map/ppermute | solution.py:32
  44.5 4.2 collective-permute-done.5
  59.8 4.9 reshape.590
  64.7 3.2 copy.202
  67.8 4.2 reshape.591.refs_4_.refs_9_
  80.5 16.6 %collective-permute-done.9.refs_6_.refs_12_ = bf16[2,64,1152]{2,1,0:T(8,128)(2,1)S(1)} collective-permute-done((bf16[2,64,1152]{2,1,0:T(8,128)(2,1)}, bf16[2,64,1152]{2,1,0:T(8,128)(2,1)S(1)}, u32[]{:S(2)}, u32[]{:S(2)}) %collective-permute-start.9) | collective-permute-done | bytes 294944 | tf_op jit(solution)/shard_map/ppermute | solution.py:32
  97.7 5.7 collective-permute-done.30.refs_4_.refs_8_
  104.0 5.2 collective-permute-done.31.refs_5_.refs_9_
  109.8 19.2 %collective-permute-done.21.refs_6_.refs_11_ = bf16[144,4608]{1,0:T(8,128)(2,1)} collective-permute-done((bf16[144,4608]{1,0:T(8,128)(2,1)}, bf16[144,4608]{1,0:T(8,128)(2,1)}, u32[]{:S(2)}, u32[]{:S(2)}) %collective-permute-start.21) | collective-permute-done | bytes 1327136 | tf_op jit(solution)/shard_map/ppermute | solution.py:32
  129.0 6.8 %collective-permute-done.20.refs_5_.refs_10_ = bf16[144,4608]{1,0:T(8,128)(2,1)} collective-permute-done((bf16[144,4608]{1,0:T(8,128)(2,1)}, bf16[144,4608]{1,0:T(8,128)(2,1)}, u32[]{:S(2)}, u32[]{:S(2)}) %collective-permute-start.20) | collective-permute-done | bytes 1327136 | tf_op jit(solution)/shard_map/ppermute | solution.py:32
  137.6 7.8 %collective-permute-done.13.refs_11_.refs_9_.refs_22_.refs_13_ = bf16[80,4608]{1,0:T(8,128)(2,1)} collective-permute-done((bf16[80,4608]{1,0:T(8,128)(2,1)S(1)}, bf16[80,4608]{1,0:T(8,128)(2,1)}, u32[]{:S(2)}, u32[]{:S(2)}) %collective-permute-start.13) | collective-permute-done | bytes 737312 | tf_op jit(solution)/shard_map/ppermute | solution.py:32
  165.8 17.5 %collective-permute-done.23.refs_8_.refs_13_ = bf16[64,4608]{1,0:T(8,128)(2,1)} collective-permute-done((bf16[64,4608]{1,0:T(8,128)(2,1)}, bf16[64,4608]{1,0:T(8,128)(2,1)}, u32[]{:S(2)}, u32[]{:S(2)}) %collective-permute-start.23) | collective-permute-done | bytes 589856 | tf_op jit(solution)/shard_map/ppermute | solution.py:32
  183.4 5.9 collective-permute-done.22.refs_7_.refs_12_
  199.6 10.2 %enter.1 = (bf16[320,1152]{1,0:T(8,128)(2,1)}, bf16[320,3456]{1,0:T(8,128)(2,1)}, bf16[320,640]{1,0:T(8,128)(2,1)}, bf16[320,640]{1,0:T(8,128)(2,1)}) custom-call(s32[10]{0:T(128)} %stack.290.refs_0_.refs_1_, s32[2,1,256]{2,1,0:T(1,128)} %select_n.693.refs_1_.refs_0_, f32[2,6,1152]{2,1,0:T(8,128)} %broadcast_add_fusion.refs_2_.refs_4_.refs_1_.refs_8_, ...), custom_call_target="tpu_custom_call" | custom-call | flops 3397386240 | bytes 18571304 | tf_op jit(solution)/shard_map/enter/pallas_call | solution.py:136
  211.0 11.9 %attend.1 = (bf16[320,640]{1,0:T(8,128)(2,1)}, bf16[320,640]{1,0:T(8,128)(2,1)}, f32[320,1152]{1,0:T(8,128)}, f32[320,1152]{1,0:T(8,128)}, bf16[320,1152]{1,0:T(...) custom-call(s32[10]{0:T(128)} %stack.290.refs_0_.refs_1_, s32[2]{0:T(128)} %get-tuple-element.126.refs_1_.refs_0_, ...), custom_call_target="tpu_custom_call" | custom-call | flops 5096079360 | bytes 21895216 | tf_op jit(solution)/shard_map/attend/pallas_call | solution.py:136
  223.0 13.7 %first.1 = (bf16[320,2304]{1,0:T(8,128)(2,1)}, bf16[320,2304]{1,0:T(8,128)(2,1)}, bf16[320,2304]{1,0:T(8,128)(2,1)}, bf16[320,2304]{1,0:T(8,128)(2,1)}) custom-call(s32[10]{0:T(128)} %stack.290.refs_0_.refs_1_, s32[1]{0:T(128)} %bitcast.20.refs_1_.refs_2_, bf16[320,1152]{1,0:T(8,128)(2,1)} %get-tuple-element.70.refs_2_, f32[1,4608]{1,0:T(1,128)} %reshape.601.refs_3_, ...), custom_call_target="tpu_custom_call" | custom-call | flops 3397386240 | bytes 17270828 | tf_op jit(solution)/shard_map/first/pallas_call | solution.py:136
  239.1 18.4 %second.1 = (bf16[2,64,1152]{2,1,0:T(8,128)(2,1)}, bf16[2,64,1152]{2,1,0:T(8,128)(2,1)}, bf16[2,64,1152]{2,1,0:T(8,128)(2,1)}, bf16[2,64,1152]{2,1,0:T(8,128)(2,...) custom-call(s32[10]{0:T(128)} %stack.279.refs_0_, ...), custom_call_target="tpu_custom_call" | custom-call | flops 6794772480 | bytes 24857640 | tf_op jit(solution)/shard_map/second/pallas_call | solution.py:136
  257.5 16.1 %hidden_back.1 = (f32[320,1152]{1,0:T(8,128)}, bf16[320,1152]{1,0:T(8,128)(2,1)}, bf16[320,1152]{1,0:T(8,128)(2,1)}, f32[2,3,1152]{2,1,0:T(4,128)}) custom-call(s32[10]{0:T(128)} %stack.290.refs_0_.refs_1_, s32[10]{0:T(128)} %stack.290.refs_0_.refs_1_, s32[1]{0:T(128)} %bitcast.20.refs_1_.refs_2_, bf16[320,2304]{1,0:T(8,128)(2,1)} %get-tuple-element.84.refs_3_, ...), custom_call_target="tpu_custom_call" | custom-call | flops 4246732800 | bytes 30901332 | tf_op jit(solution)/shard_map/hidden_back/pallas_call | solution.py:136
  275.3 14.9 %attend_back.1.refs_1_.refs_3_ = bf16[320,3456]{1,0:T(8,128)(2,1)} custom-call(s32[2]{0:T(128)} %get-tuple-element.126.refs_1_.refs_0_, bf16[320,3456]{1,0:T(8,128)(2,1)} %get-tuple-element.68.refs_2_.refs_1_, bf16[320,1152]{1,0:T(8,128)(2,1)} %get-tuple-element.87.refs_2_), custom_call_target="tpu_custom_call" | custom-call | flops 6794772480 | bytes 5160968 | tf_op jit(solution)/shard_map/attend_back/pallas_call | solution.py:136
  290.2 11.8 %leave.1 = (bf16[2,64,1152]{2,1,0:T(8,128)(2,1)}, bf16[2,64,1152]{2,1,0:T(8,128)(2,1)}, bf16[2,64,1152]{2,1,0:T(8,128)(2,1)}, bf16[2,64,1152]{2,1,0:T(8,128)(2,1)}, f32[2,2,1152]{2,1,0:T(2,128)}) custom-call(s32[10]{0:T(128)} %stack.290.refs_0_.refs_1_, bf16[320,3456]{1,0:T(8,128)(2,1)} %attend_back.1.refs_1_.refs_3_, ...), custom_call_target="tpu_custom_call" | custom-call | flops 2548039680 | bytes 17475624 | tf_op jit(solution)/shard_map/leave/pallas_call | solution.py:136
  317.0 4.4 collective-permute-start.62
  333.1 3.0 collective-permute-start.54
  341.8 4.6 collective-permute-done.44
  352.2 6.9 %collective-permute-done.41 = bf16[2,64,1152]{2,1,0:T(8,128)(2,1)S(1)} collective-permute-done((bf16[2,64,1152]{2,1,0:T(8,128)(2,1)}, bf16[2,64,1152]{2,1,0:T(8,128)(2,1)S(1)}, u32[]{:S(2)}, u32[]{:S(2)}) %collective-permute-start.41) | collective-permute-done | bytes 294944 | tf_op jit(solution)/shard_map/ppermute | solution.py:32
  362.8 8.0 %collective-permute-done.42 = bf16[2,64,1152]{2,1,0:T(8,128)(2,1)S(1)} collective-permute-done((bf16[2,64,1152]{2,1,0:T(8,128)(2,1)}, bf16[2,64,1152]{2,1,0:T(8,128)(2,1)S(1)}, u32[]{:S(2)}, u32[]{:S(2)}) %collective-permute-start.42) | collective-permute-done | bytes 294944 | tf_op jit(solution)/shard_map/ppermute | solution.py:32
  371.5 5.8 collective-permute-done.46
  378.4 9.5 %fc2_grad.1 = (bf16[2,288,1152]{2,1,0:T(8,128)(2,1)}, bf16[2,288,1152]{2,1,0:T(8,128)(2,1)}, bf16[576,1152]{1,0:T(8,128)(2,1)}, bf16[288,1152]{1,0:T(8,128)(2,1)}, bf16[288,1152]{1,0:T(8,128)(2,1)}) custom-call(s32[4]{0:T(128)} %pad_add_fusion.2.refs_0_, bf16[320,2304]{1,0:T(8,128)(2,1)} %get-tuple-element.72.refs_1_, ...), custom_call_target="tpu_custom_call" | custom-call | flops 3397386240 | bytes 10616832 | tf_op jit(solution)/shard_map/fc2_grad/pallas_call | solution.py:518
  388.0 4.6 collective-permute-done.43
  393.3 4.3 collective-permute-done.57
  399.7 4.0 out_grad.1
  406.9 5.0 collective-permute-done.76
  414.3 23.3 %collective-permute-done.75 = bf16[2,80,1152]{2,1,0:T(8,128)(2,1)S(1)} collective-permute-done((bf16[2,80,1152]{2,1,0:T(8,128)(2,1)}, bf16[2,80,1152]{2,1,0:T(8,128)(2,1)S(1)}, u32[]{:S(2)}, u32[]{:S(2)}) %collective-permute-start.75) | collective-permute-done | bytes 368672 | tf_op jit(solution)/shard_map/ppermute | solution.py:32
  440.2 3.9 collective-permute-done.77
  460.8 9.7 %fc1_grad.1 = (bf16[2,80,4608]{2,1,0:T(8,128)(2,1)}, bf16[2,64,4608]{2,1,0:T(8,128)(2,1)}, bf16[144,4608]{1,0:T(8,128)(2,1)}, bf16[64,4608]{1,0:T(8,128)(2,1)}, bf16[80,4608]{1,0:T(8,128)(2,1)}) custom-call(s32[4]{0:T(128)} %pad_add_fusion.2.refs_0_, bf16[320,640]{1,0:T(8,128)(2,1)} %get-tuple-element.113.refs_1_, bf16[320,640]{1,0:T(8,128)(2,1)} %copy-done.62, ...), custom_call_target="tpu_custom_call" | custom-call | flops 3397386240 | bytes 10616832 | tf_op jit(solution)/shard_map/fc1_grad/pallas_call | solution.py:518
  472.0 15.6 %collective-permute-done.95 = bf16[2,288,1152]{2,1,0:T(8,128)(2,1)S(1)} collective-permute-done((bf16[2,288,1152]{2,1,0:T(8,128)(2,1)}, bf16[2,288,1152]{2,1,0:T(8,128)(2,1)S(1)}, u32[]{:S(2)}, u32[]{:S(2)}) %collective-permute-start.95) | collective-permute-done | bytes 1327136 | tf_op jit(solution)/shard_map/ppermute | solution.py:32
  490.9 8.2 %qkv_grad.1 = (bf16[2,80,3456]{2,1,0:T(8,128)(2,1)}, bf16[2,64,3456]{2,1,0:T(8,128)(2,1)}, bf16[144,3456]{1,0:T(8,128)(2,1)}, bf16[64,3456]{1,0:T(8,128)(2,1)}, bf16[80,3456]{1,0:T(8,128)(2,1)}) custom-call(s32[4]{0:T(128)} %pad_add_fusion.2.refs_0_, bf16[320,640]{1,0:T(8,128)(2,1)} %get-tuple-element.98.refs_1_, ...), custom_call_target="tpu_custom_call" | custom-call | flops 2548039680 | bytes 7962624 | tf_op jit(solution)/shard_map/qkv_grad/pallas_call | solution.py:518
  501.8 17.9 %collective-permute-done.97 = bf16[288,1152]{1,0:T(8,128)(2,1)S(1)} collective-permute-done((bf16[288,1152]{1,0:T(8,128)(2,1)}, bf16[288,1152]{1,0:T(8,128)(2,1)S(1)}, u32[]{:S(2)}, u32[]{:S(2)}) %collective-permute-start.97) | collective-permute-done | bytes 663584 | tf_op jit(solution)/shard_map/ppermute | solution.py:32
  534.0 10.0 %collective-permute-done.100 = bf16[576,288]{0,1:T(8,128)(2,1)} collective-permute-done((bf16[576,288]{0,1:T(8,128)(2,1)}, bf16[576,288]{0,1:T(8,128)(2,1)}, u32[]{:S(2)}, u32[]{:S(2)}) %collective-permute-start.100) | collective-permute-done | bytes 331808 | tf_op jit(solution)/shard_map/ppermute | solution.py:32
  544.7 3.7 collective-permute-done.98
  548.4 3.2 collective-permute-start.67
  551.6 5.9 collective-permute-done.99
  566.7 5.5 collective-permute-done.67
  575.4 8.6 %collective-permute-done.88 = bf16[64,4608]{1,0:T(8,128)(2,1)S(1)} collective-permute-done((bf16[64,4608]{1,0:T(8,128)(2,1)S(1)}, bf16[64,4608]{1,0:T(8,128)(2,1)S(1)}, u32[]{:S(2)}, u32[]{:S(2)}) %collective-permute-start.88) | collective-permute-done | bytes 589856 | tf_op jit(solution)/shard_map/ppermute | solution.py:32
  584.0 4.0 collective-permute-done.87
  594.2 5.1 collective-permute-done.68
  604.8 10.0 %collective-permute-done.90 = bf16[144,1152]{1,0:T(8,128)(2,1)S(1)} collective-permute-done((bf16[144,1152]{1,0:T(8,128)(2,1)S(1)}, bf16[144,1152]{1,0:T(8,128)(2,1)S(1)}, u32[]{:S(2)}, u32[]{:S(2)}) %collective-permute-start.90) | collective-permute-done | bytes 331808 | tf_op jit(solution)/shard_map/ppermute | solution.py:32
  614.8 19.8 %collective-permute-done.91 = bf16[144,1152]{1,0:T(8,128)(2,1)S(1)} collective-permute-done((bf16[144,1152]{1,0:T(8,128)(2,1)S(1)}, bf16[144,1152]{1,0:T(8,128)(2,1)S(1)}, u32[]{:S(2)}, u32[]{:S(2)}) %collective-permute-start.91) | collective-permute-done | bytes 331808 | tf_op jit(solution)/shard_map/ppermute | solution.py:32
  638.6 5.4 collective-permute-done.72
  (479 shorter events, 202.2 us)
Async XLA Ops:
  2.2 75.6 %collective-permute-start.12 = (bf16[144,4608]{1,0:T(8,128)(2,1)S(1)}, bf16[144,4608]{1,0:T(8,128)(2,1)}, u32[]{:S(2)}, u32[]{:S(2)}) collective-permute-start(bf16[144,4608]{1,0:T(8,128)(2,1)S(1)} %constant_dynamic-update-slice_fusion.4.refs_8_.refs_6_.refs_19_.refs_10_), channel_id=1, source_target_pairs={{0,16},{4,20},{8,24},{12,28},{16,0},{20,4},{24,8},{28,12},{1,17},{... | collective-permute-start | bytes 3981320 | tf_op jit(solution)/shard_map/ppermute | solution.py:32
  3.8 52.3 %collective-permute-start.11 = (bf16[144,4608]{1,0:T(8,128)(2,1)S(1)}, bf16[144,4608]{1,0:T(8,128)(2,1)}, u32[]{:S(2)}, u32[]{:S(2)}) collective-permute-start(bf16[144,4608]{1,0:T(8,128)(2,1)S(1)} %constant_dynamic-update-slice_fusion.4.refs_8_.refs_6_.refs_19_.refs_10_), channel_id=1, source_target_pairs={{0,8},{4,12},{8,0},{12,4},{16,24},{20,28},{24,16},{28,20},{1,9},{5... | collective-permute-start | bytes 3981320 | tf_op jit(solution)/shard_map/ppermute | solution.py:32
  8.6 64.9 %collective-permute-start.10 = (bf16[2,64,1152]{2,1,0:T(8,128)(2,1)}, bf16[2,64,1152]{2,1,0:T(8,128)(2,1)}, u32[]{:S(2)}, u32[]{:S(2)}) collective-permute-start(bf16[2,64,1152]{2,1,0:T(8,128)(2,1)} %get-tuple-element.156), channel_id=1, source_target_pairs={{0,3},{1,2},{2,1},{3,0},{4,7},{5,6},{6,5},{7,4},{8,11},{9,10},{10,... | collective-permute-start | bytes 884744 | tf_op jit(solution)/shard_map/ppermute | solution.py:32
  11.3 63.8 %collective-permute-start.8 = (bf16[2,64,1152]{2,1,0:T(8,128)(2,1)}, bf16[2,64,1152]{2,1,0:T(8,128)(2,1)}, u32[]{:S(2)}, u32[]{:S(2)}) collective-permute-start(bf16[2,64,1152]{2,1,0:T(8,128)(2,1)} %get-tuple-element.157), channel_id=1, source_target_pairs={{0,1},{1,0},{2,3},{3,2},{4,5},{5,4},{6,7},{7,6},{8,9},{9,8},{10,11... | collective-permute-start | bytes 884744 | tf_op jit(solution)/shard_map/ppermute | solution.py:32
  73.2 24.0 %collective-permute-start.9 = (bf16[2,64,1152]{2,1,0:T(8,128)(2,1)}, bf16[2,64,1152]{2,1,0:T(8,128)(2,1)S(1)}, u32[]{:S(2)}, u32[]{:S(2)}) collective-permute-start(bf16[2,64,1152]{2,1,0:T(8,128)(2,1)} %get-tuple-element.159), channel_id=1, source_target_pairs={{0,2},{1,3},{2,0},{3,1},{4,6},{5,7},{6,4},{7,5},{8,10},{9,11},{10,... | collective-permute-start | bytes 884744 | tf_op jit(solution)/shard_map/ppermute | solution.py:32
  75.2 28.3 %collective-permute-start.30 = (bf16[2,64,1152]{2,1,0:T(8,128)(2,1)}, bf16[2,64,1152]{2,1,0:T(8,128)(2,1)S(1)}, u32[]{:S(2)}, u32[]{:S(2)}) collective-permute-start(bf16[2,64,1152]{2,1,0:T(8,128)(2,1)} %get-tuple-element.155), channel_id=1, source_target_pairs={{0,2},{1,3},{2,0},{3,1},{4,6},{5,7},{6,4},{7,5},{8,10},{9,11},{10,... | collective-permute-start | bytes 884744 | tf_op jit(solution)/shard_map/ppermute | solution.py:32
  77.7 31.5 %collective-permute-start.31 = (bf16[2,64,1152]{2,1,0:T(8,128)(2,1)}, bf16[2,64,1152]{2,1,0:T(8,128)(2,1)S(1)}, u32[]{:S(2)}, u32[]{:S(2)}) collective-permute-start(bf16[2,64,1152]{2,1,0:T(8,128)(2,1)} %get-tuple-element.152), channel_id=1, source_target_pairs={{0,3},{1,2},{2,1},{3,0},{4,7},{5,6},{6,5},{7,4},{8,11},{9,10},{10,... | collective-permute-start | bytes 884744 | tf_op jit(solution)/shard_map/ppermute | solution.py:32
  77.8 32.0 %collective-permute-start.14 = (bf16[64,4608]{1,0:T(8,128)(2,1)S(1)}, bf16[64,4608]{1,0:T(8,128)(2,1)S(1)}, u32[]{:S(2)}, u32[]{:S(2)}) collective-permute-start(bf16[64,4608]{1,0:T(8,128)(2,1)S(1)} %slice.315), channel_id=1, source_target_pairs={{0,16},{4,20},{8,24},{12,28},{16,0},{20,4},{24,8},{28,12},{1,17},{... | collective-permute-start | bytes 1769480 | tf_op jit(solution)/shard_map/ppermute | solution.py:32
  97.2 39.4 %collective-permute-start.15 = (bf16[144,4608]{1,0:T(8,128)(2,1)S(1)}, bf16[144,4608]{1,0:T(8,128)(2,1)S(1)}, u32[]{:S(2)}, u32[]{:S(2)}) collective-permute-start(bf16[144,4608]{1,0:T(8,128)(2,1)S(1)} %constant_dynamic-update-slice_fusion.4.refs_8_.refs_6_.refs_19_.refs_10_), channel_id=1, source_target_pairs={{0,4},{4,0},{8,12},{12,8},{16,20},{20,16},{24,28},{28,24},{1,5},{5... | collective-permute-start | bytes 3981320 | tf_op jit(solution)/shard_map/ppermute | solution.py:32
  97.2 31.9 %collective-permute-start.21 = (bf16[144,4608]{1,0:T(8,128)(2,1)}, bf16[144,4608]{1,0:T(8,128)(2,1)}, u32[]{:S(2)}, u32[]{:S(2)}) collective-permute-start(bf16[144,4608]{1,0:T(8,128)(2,1)} %reshape.591.refs_4_.refs_9_), channel_id=1, source_target_pairs={{0,16},{4,20},{8,24},{12,28},{16,0},{20,4},{24,8},{28,12},{1,17},{... | collective-permute-start | bytes 3981320 | tf_op jit(solution)/shard_map/ppermute | solution.py:32
  103.5 32.4 %collective-permute-start.20 = (bf16[144,4608]{1,0:T(8,128)(2,1)}, bf16[144,4608]{1,0:T(8,128)(2,1)}, u32[]{:S(2)}, u32[]{:S(2)}) collective-permute-start(bf16[144,4608]{1,0:T(8,128)(2,1)} %reshape.591.refs_4_.refs_9_), channel_id=1, source_target_pairs={{0,8},{4,12},{8,0},{12,4},{16,24},{20,28},{24,16},{28,20},{1,9},{5... | collective-permute-start | bytes 3981320 | tf_op jit(solution)/shard_map/ppermute | solution.py:32
  109.3 36.2 %collective-permute-start.13 = (bf16[80,4608]{1,0:T(8,128)(2,1)S(1)}, bf16[80,4608]{1,0:T(8,128)(2,1)}, u32[]{:S(2)}, u32[]{:S(2)}) collective-permute-start(bf16[80,4608]{1,0:T(8,128)(2,1)S(1)} %slice.314), channel_id=1, source_target_pairs={{0,8},{4,12},{8,0},{12,4},{16,24},{20,28},{24,16},{28,20},{1,9},{5... | collective-permute-start | bytes 2211848 | tf_op jit(solution)/shard_map/ppermute | solution.py:32
  109.8 38.4 %collective-permute-start.19 = (bf16[64,4608]{1,0:T(8,128)(2,1)S(1)}, bf16[64,4608]{1,0:T(8,128)(2,1)S(1)}, u32[]{:S(2)}, u32[]{:S(2)}) collective-permute-start(bf16[64,4608]{1,0:T(8,128)(2,1)S(1)} %collective-permute-done.14.refs_12_.refs_10_.refs_23_.refs_14_), channel_id=1, source_target_pairs={{0,4},{4,0},{8,12},{12,8},{16,20},{20,16},{24,28},{28,24},{1,5},{5... | collective-permute-start | bytes 1769480 | tf_op jit(solution)/shard_map/ppermute | solution.py:32
  135.9 29.9 %collective-permute-start.24 = (bf16[144,4608]{1,0:T(8,128)(2,1)}, bf16[144,4608]{1,0:T(8,128)(2,1)}, u32[]{:S(2)}, u32[]{:S(2)}) collective-permute-start(bf16[144,4608]{1,0:T(8,128)(2,1)} %reshape.591.refs_4_.refs_9_), channel_id=1, source_target_pairs={{0,4},{4,0},{8,12},{12,8},{16,20},{20,16},{24,28},{28,24},{1,5},{5... | collective-permute-start | bytes 3981320 | tf_op jit(solution)/shard_map/ppermute | solution.py:32
  137.6 24.3 %collective-permute-start.17 = (bf16[144,4608]{1,0:T(8,128)(2,1)}, bf16[144,4608]{1,0:T(8,128)(2,1)S(1)}, u32[]{:S(2)}, u32[]{:S(2)}) collective-permute-start(bf16[144,4608]{1,0:T(8,128)(2,1)} %collective-permute-done.12.refs_10_.refs_8_.refs_21_.refs_12_), channel_id=1, source_target_pairs={{0,4},{4,0},{8,12},{12,8},{16,20},{20,16},{24,28},{28,24},{1,5},{5... | collective-permute-start | bytes 3981320 | tf_op jit(solution)/shard_map/ppermute | solution.py:32
  145.4 43.9 %collective-permute-start.33 = (bf16[576,1152]{1,0:T(8,128)(2,1)}, bf16[576,1152]{1,0:T(8,128)(2,1)}, u32[]{:S(2)}, u32[]{:S(2)}) collective-permute-start(bf16[576,1152]{1,0:T(8,128)(2,1)} %refs_14_), channel_id=1, source_target_pairs={{0,16},{4,20},{8,24},{12,28},{16,0},{20,4},{24,8},{28,12},{1,17},{... | collective-permute-start | bytes 3981320 | tf_op jit(solution)/shard_map/ppermute | solution.py:32
  149.1 40.8 %collective-permute-start.32 = (bf16[576,1152]{1,0:T(8,128)(2,1)}, bf16[576,1152]{1,0:T(8,128)(2,1)}, u32[]{:S(2)}, u32[]{:S(2)}) collective-permute-start(bf16[576,1152]{1,0:T(8,128)(2,1)} %refs_14_), channel_id=1, source_target_pairs={{0,8},{4,12},{8,0},{12,4},{16,24},{20,28},{24,16},{28,20},{1,9},{5... | collective-permute-start | bytes 3981320 | tf_op jit(solution)/shard_map/ppermute | solution.py:32
  158.4 30.9 %collective-permute-start.22 = (bf16[80,4608]{1,0:T(8,128)(2,1)}, bf16[80,4608]{1,0:T(8,128)(2,1)}, u32[]{:S(2)}, u32[]{:S(2)}) collective-permute-start(bf16[80,4608]{1,0:T(8,128)(2,1)} %slice.316), channel_id=1, source_target_pairs={{0,8},{4,12},{8,0},{12,4},{16,24},{20,28},{24,16},{28,20},{1,9},{5... | collective-permute-start | bytes 2211848 | tf_op jit(solution)/shard_map/ppermute | solution.py:32
  165.8 27.3 %collective-permute-start.18 = (bf16[80,4608]{1,0:T(8,128)(2,1)}, bf16[80,4608]{1,0:T(8,128)(2,1)}, u32[]{:S(2)}, u32[]{:S(2)}) collective-permute-start(bf16[80,4608]{1,0:T(8,128)(2,1)} %collective-permute-done.13.refs_11_.refs_9_.refs_22_.refs_13_), channel_id=1, source_target_pairs={{0,4},{4,0},{8,12},{12,8},{16,20},{20,16},{24,28},{28,24},{1,5},{5... | collective-permute-start | bytes 2211848 | tf_op jit(solution)/shard_map/ppermute | solution.py:32
  193.1 43.6 %collective-permute-start.36 = (bf16[576,1152]{1,0:T(8,128)(2,1)}, bf16[576,1152]{1,0:T(8,128)(2,1)S(1)}, u32[]{:S(2)}, u32[]{:S(2)}) collective-permute-start(bf16[576,1152]{1,0:T(8,128)(2,1)} %refs_14_), channel_id=1, source_target_pairs={{0,4},{4,0},{8,12},{12,8},{16,20},{20,16},{24,28},{28,24},{1,5},{5... | collective-permute-start | bytes 3981320 | tf_op jit(solution)/shard_map/ppermute | solution.py:32
  195.7 41.1 %collective-permute-start.37 = (bf16[576,1152]{1,0:T(8,128)(2,1)}, bf16[576,1152]{1,0:T(8,128)(2,1)S(1)}, u32[]{:S(2)}, u32[]{:S(2)}) collective-permute-start(bf16[576,1152]{1,0:T(8,128)(2,1)} %collective-permute-done.32.refs_15_), channel_id=1, source_target_pairs={{0,4},{4,0},{8,12},{12,8},{16,20},{20,16},{24,28},{28,24},{1,5},{5... | collective-permute-start | bytes 3981320 | tf_op jit(solution)/shard_map/ppermute | solution.py:32
  195.7 41.1 %collective-permute-start.38 = (bf16[576,1152]{1,0:T(8,128)(2,1)}, bf16[576,1152]{1,0:T(8,128)(2,1)S(1)}, u32[]{:S(2)}, u32[]{:S(2)}) collective-permute-start(bf16[576,1152]{1,0:T(8,128)(2,1)} %collective-permute-done.33.refs_16_), channel_id=1, source_target_pairs={{0,4},{4,0},{8,12},{12,8},{16,20},{20,16},{24,28},{28,24},{1,5},{5... | collective-permute-start | bytes 3981320 | tf_op jit(solution)/shard_map/ppermute | solution.py:32
  210.5 26.2 %collective-permute-start.39 = (bf16[288,1152]{1,0:T(8,128)(2,1)S(1)}, bf16[288,1152]{1,0:T(8,128)(2,1)S(1)}, u32[]{:S(2)}, u32[]{:S(2)}) collective-permute-start(bf16[288,1152]{1,0:T(8,128)(2,1)S(1)} %collective-permute-done.34.refs_17_), channel_id=1, source_target_pairs={{0,4},{4,0},{8,12},{12,8},{16,20},{20,16},{24,28},{28,24},{1,5},{5... | collective-permute-start | bytes 1990664 | tf_op jit(solution)/shard_map/ppermute | solution.py:32
  210.7 26.0 %collective-permute-start.40 = (bf16[288,1152]{1,0:T(8,128)(2,1)}, bf16[288,1152]{1,0:T(8,128)(2,1)S(1)}, u32[]{:S(2)}, u32[]{:S(2)}) collective-permute-start(bf16[288,1152]{1,0:T(8,128)(2,1)} %collective-permute-done.35.refs_18_), channel_id=1, source_target_pairs={{0,4},{4,0},{8,12},{12,8},{16,20},{20,16},{24,28},{28,24},{1,5},{5... | collective-permute-start | bytes 1990664 | tf_op jit(solution)/shard_map/ppermute | solution.py:32
  312.2 65.2 %collective-permute-start.93 = (bf16[320,1152]{1,0:T(8,128)(2,1)}, bf16[320,1152]{1,0:T(8,128)(2,1)}, u32[]{:S(2)}, u32[]{:S(2)}) collective-permute-start(bf16[320,1152]{1,0:T(8,128)(2,1)} %get-tuple-element.76.refs_5_.refs_3_), channel_id=1, source_target_pairs={{0,4},{4,0},{8,12},{12,8},{16,20},{20,16},{24,28},{28,24},{1,5},{5... | collective-permute-start | bytes 2211848 | tf_op jit(solution)/shard_map/ppermute | solution.py:32
  312.2 86.7 %collective-permute-start.73 = (bf16[320,640]{1,0:T(8,128)(2,1)}, bf16[320,640]{1,0:T(8,128)(2,1)}, u32[]{:S(2)}, u32[]{:S(2)}) collective-permute-start(bf16[320,640]{1,0:T(8,128)(2,1)} %get-tuple-element.106), channel_id=1, source_target_pairs={{0,4},{4,0},{8,12},{12,8},{16,20},{20,16},{24,28},{28,24},{1,5},{5... | collective-permute-start | bytes 1228808 | tf_op jit(solution)/shard_map/ppermute | solution.py:32
  312.7 65.3 %collective-permute-start.92 = (bf16[320,2304]{1,0:T(8,128)(2,1)}, bf16[320,2304]{1,0:T(8,128)(2,1)}, u32[]{:S(2)}, u32[]{:S(2)}) collective-permute-start(bf16[320,2304]{1,0:T(8,128)(2,1)} %get-tuple-element.73.refs_2_), channel_id=1, source_target_pairs={{0,4},{4,0},{8,12},{12,8},{16,20},{20,16},{24,28},{28,24},{1,5},{5... | collective-permute-start | bytes 4423688 | tf_op jit(solution)/shard_map/ppermute | solution.py:32
  370.8 89.1 %collective-permute-start.83 = (bf16[320,2304]{1,0:T(8,128)(2,1)}, bf16[320,2304]{1,0:T(8,128)(2,1)}, u32[]{:S(2)}, u32[]{:S(2)}) collective-permute-start(bf16[320,2304]{1,0:T(8,128)(2,1)} %get-tuple-element.85.refs_4_), channel_id=1, source_target_pairs={{0,4},{4,0},{8,12},{12,8},{16,20},{20,16},{24,28},{28,24},{1,5},{5... | collective-permute-start | bytes 4423688 | tf_op jit(solution)/shard_map/ppermute | solution.py:32
  377.3 83.5 %collective-permute-start.84 = (bf16[320,2304]{1,0:T(8,128)(2,1)}, bf16[320,2304]{1,0:T(8,128)(2,1)}, u32[]{:S(2)}, u32[]{:S(2)}) collective-permute-start(bf16[320,2304]{1,0:T(8,128)(2,1)} %get-tuple-element.84.refs_3_), channel_id=1, source_target_pairs={{0,4},{4,0},{8,12},{12,8},{16,20},{20,16},{24,28},{28,24},{1,5},{5... | collective-permute-start | bytes 4423688 | tf_op jit(solution)/shard_map/ppermute | solution.py:32
  397.7 73.5 %collective-permute-start.94 = (bf16[2,288,1152]{2,1,0:T(8,128)(2,1)}, bf16[2,288,1152]{2,1,0:T(8,128)(2,1)S(1)}, u32[]{:S(2)}, u32[]{:S(2)}) collective-permute-start(bf16[2,288,1152]{2,1,0:T(8,128)(2,1)} %get-tuple-element.121), channel_id=1, source_target_pairs={{0,8},{4,12},{8,0},{12,4},{16,24},{20,28},{24,16},{28,20},{1,9},{5... | collective-permute-start | bytes 3981320 | tf_op jit(solution)/shard_map/ppermute | solution.py:32
  405.5 32.1 %collective-permute-start.75 = (bf16[2,80,1152]{2,1,0:T(8,128)(2,1)}, bf16[2,80,1152]{2,1,0:T(8,128)(2,1)S(1)}, u32[]{:S(2)}, u32[]{:S(2)}) collective-permute-start(bf16[2,80,1152]{2,1,0:T(8,128)(2,1)} %get-tuple-element.109), channel_id=1, source_target_pairs={{0,8},{4,12},{8,0},{12,4},{16,24},{20,28},{24,16},{28,20},{1,9},{5... | collective-permute-start | bytes 1105928 | tf_op jit(solution)/shard_map/ppermute | solution.py:32
  412.8 27.3 %collective-permute-start.78 = (bf16[64,1152]{1,0:T(8,128)(2,1)S(1)}, bf16[64,1152]{1,0:T(8,128)(2,1)S(1)}, u32[]{:S(2)}, u32[]{:S(2)}) collective-permute-start(bf16[64,1152]{1,0:T(8,128)(2,1)S(1)} %fusion.19), channel_id=1, source_target_pairs={{0,8},{4,12},{8,0},{12,4},{16,24},{20,28},{24,16},{28,20},{1,9},{5... | collective-permute-start | bytes 442376 | tf_op jit(solution)/shard_map/ppermute | solution.py:32
  455.3 32.3 %collective-permute-start.95 = (bf16[2,288,1152]{2,1,0:T(8,128)(2,1)}, bf16[2,288,1152]{2,1,0:T(8,128)(2,1)S(1)}, u32[]{:S(2)}, u32[]{:S(2)}) collective-permute-start(bf16[2,288,1152]{2,1,0:T(8,128)(2,1)} %get-tuple-element.122), channel_id=1, source_target_pairs={{0,16},{4,20},{8,24},{12,28},{16,0},{20,4},{24,8},{28,12},{1,17},{... | collective-permute-start | bytes 3981320 | tf_op jit(solution)/shard_map/ppermute | solution.py:32
  459.9 29.5 %collective-permute-start.64 = (bf16[320,640]{1,0:T(8,128)(2,1)}, bf16[320,640]{1,0:T(8,128)(2,1)}, u32[]{:S(2)}, u32[]{:S(2)}) collective-permute-start(bf16[320,640]{1,0:T(8,128)(2,1)} %get-tuple-element.99), channel_id=1, source_target_pairs={{0,4},{4,0},{8,12},{12,8},{16,20},{20,16},{24,28},{28,24},{1,5},{5... | collective-permute-start | bytes 1228808 | tf_op jit(solution)/shard_map/ppermute | solution.py:32
  460.8 30.2 %collective-permute-start.65 = (bf16[320,3456]{1,0:T(8,128)(2,1)S(1)}, bf16[320,3456]{1,0:T(8,128)(2,1)}, u32[]{:S(2)}, u32[]{:S(2)}) collective-permute-start(bf16[320,3456]{1,0:T(8,128)(2,1)S(1)} %copy-done.8), channel_id=1, source_target_pairs={{0,4},{4,0},{8,12},{12,8},{16,20},{20,16},{24,28},{28,24},{1,5},{5... | collective-permute-start | bytes 6635528 | tf_op jit(solution)/shard_map/ppermute | solution.py:32
  470.5 92.3 %collective-permute-start.85 = (bf16[2,80,4608]{2,1,0:T(8,128)(2,1)}, bf16[2,80,4608]{2,1,0:T(8,128)(2,1)}, u32[]{:S(2)}, u32[]{:S(2)}) collective-permute-start(bf16[2,80,4608]{2,1,0:T(8,128)(2,1)} %get-tuple-element.116), channel_id=1, source_target_pairs={{0,8},{4,12},{8,0},{12,4},{16,24},{20,28},{24,16},{28,20},{1,9},{5... | collective-permute-start | bytes 4423688 | tf_op jit(solution)/shard_map/ppermute | solution.py:32
  471.3 30.5 %collective-permute-start.96 = (bf16[288,1152]{1,0:T(8,128)(2,1)S(1)}, bf16[288,1152]{1,0:T(8,128)(2,1)S(1)}, u32[]{:S(2)}, u32[]{:S(2)}) collective-permute-start(bf16[288,1152]{1,0:T(8,128)(2,1)S(1)} %fusion.5), channel_id=1, source_target_pairs={{0,16},{4,20},{8,24},{12,28},{16,0},{20,4},{24,8},{28,12},{1,17},{... | collective-permute-start | bytes 1990664 | tf_op jit(solution)/shard_map/ppermute | solution.py:32
  488.6 31.0 %collective-permute-start.97 = (bf16[288,1152]{1,0:T(8,128)(2,1)}, bf16[288,1152]{1,0:T(8,128)(2,1)S(1)}, u32[]{:S(2)}, u32[]{:S(2)}) collective-permute-start(bf16[288,1152]{1,0:T(8,128)(2,1)} %fusion.4), channel_id=1, source_target_pairs={{0,8},{4,12},{8,0},{12,4},{16,24},{20,28},{24,16},{28,20},{1,9},{5... | collective-permute-start | bytes 1990664 | tf_op jit(solution)/shard_map/ppermute | solution.py:32
  489.4 70.2 %collective-permute-start.86 = (bf16[2,64,4608]{2,1,0:T(8,128)(2,1)}, bf16[2,64,4608]{2,1,0:T(8,128)(2,1)}, u32[]{:S(2)}, u32[]{:S(2)}) collective-permute-start(bf16[2,64,4608]{2,1,0:T(8,128)(2,1)} %get-tuple-element.117), channel_id=1, source_target_pairs={{0,16},{4,20},{8,24},{12,28},{16,0},{20,4},{24,8},{28,12},{1,17},{... | collective-permute-start | bytes 3538952 | tf_op jit(solution)/shard_map/ppermute | solution.py:32
  531.2 26.2 %collective-permute-start.99 = (bf16[576,288]{0,1:T(8,128)(2,1)}, bf16[576,288]{0,1:T(8,128)(2,1)}, u32[]{:S(2)}, u32[]{:S(2)}) collective-permute-start(bf16[576,288]{0,1:T(8,128)(2,1)} %bitcast.442), channel_id=1, source_target_pairs={{0,2},{1,3},{2,0},{3,1},{4,6},{5,7},{6,4},{7,5},{8,10},{9,11},{10,... | collective-permute-start | bytes 995336 | tf_op jit(solution)/shard_map/ppermute | solution.py:32
  544.1 29.0 %collective-permute-start.66 = (bf16[2,80,3456]{2,1,0:T(8,128)(2,1)S(1)}, bf16[2,80,3456]{2,1,0:T(8,128)(2,1)S(1)}, u32[]{:S(2)}, u32[]{:S(2)}) collective-permute-start(bf16[2,80,3456]{2,1,0:T(8,128)(2,1)S(1)} %copy-done.56), channel_id=1, source_target_pairs={{0,8},{4,12},{8,0},{12,4},{16,24},{20,28},{24,16},{28,20},{1,9},{5... | collective-permute-start | bytes 3317768 | tf_op jit(solution)/shard_map/ppermute | solution.py:32
  548.4 23.8 %collective-permute-start.67 = (bf16[2,64,3456]{2,1,0:T(8,128)(2,1)}, bf16[2,64,3456]{2,1,0:T(8,128)(2,1)S(1)}, u32[]{:S(2)}, u32[]{:S(2)}) collective-permute-start(bf16[2,64,3456]{2,1,0:T(8,128)(2,1)} %get-tuple-element.102), channel_id=1, source_target_pairs={{0,16},{4,20},{8,24},{12,28},{16,0},{20,4},{24,8},{28,12},{1,17},{... | collective-permute-start | bytes 2654216 | tf_op jit(solution)/shard_map/ppermute | solution.py:32
  564.2 23.9 %collective-permute-start.87 = (bf16[80,4608]{1,0:T(8,128)(2,1)S(1)}, bf16[80,4608]{1,0:T(8,128)(2,1)S(1)}, u32[]{:S(2)}, u32[]{:S(2)}) collective-permute-start(bf16[80,4608]{1,0:T(8,128)(2,1)S(1)} %fusion.3), channel_id=1, source_target_pairs={{0,16},{4,20},{8,24},{12,28},{16,0},{20,4},{24,8},{28,12},{1,17},{... | collective-permute-start | bytes 2211848 | tf_op jit(solution)/shard_map/ppermute | solution.py:32
  573.3 26.0 %collective-permute-start.68 = (bf16[80,3456]{1,0:T(8,128)(2,1)S(1)}, bf16[80,3456]{1,0:T(8,128)(2,1)S(1)}, u32[]{:S(2)}, u32[]{:S(2)}) collective-permute-start(bf16[80,3456]{1,0:T(8,128)(2,1)S(1)} %fusion.10), channel_id=1, source_target_pairs={{0,16},{4,20},{8,24},{12,28},{16,0},{20,4},{24,8},{28,12},{1,17},{... | collective-permute-start | bytes 1658888 | tf_op jit(solution)/shard_map/ppermute | solution.py:32
  592.4 42.2 %collective-permute-start.91 = (bf16[144,1152]{1,0:T(8,128)(2,1)S(1)}, bf16[144,1152]{1,0:T(8,128)(2,1)S(1)}, u32[]{:S(2)}, u32[]{:S(2)}) collective-permute-start(bf16[144,1152]{1,0:T(8,128)(2,1)S(1)} %get-tuple-element.150), channel_id=1, source_target_pairs={{0,3},{1,2},{2,1},{3,0},{4,7},{5,6},{6,5},{7,4},{8,11},{9,10},{10,... | collective-permute-start | bytes 995336 | tf_op jit(solution)/shard_map/ppermute | solution.py:32
  600.5 35.5 %collective-permute-start.70 = (bf16[144,864]{1,0:T(8,128)(2,1)S(1)}, bf16[144,864]{1,0:T(8,128)(2,1)S(1)}, u32[]{:S(2)}, u32[]{:S(2)}) collective-permute-start(bf16[144,864]{1,0:T(8,128)(2,1)S(1)} %get-tuple-element.160), channel_id=1, source_target_pairs={{0,1},{1,0},{2,3},{3,2},{4,5},{5,4},{6,7},{7,6},{8,9},{9,8},{10,11... | collective-permute-start | bytes 746504 | tf_op jit(solution)/shard_map/ppermute | solution.py:32
  603.0 35.6 %collective-permute-start.71 = (bf16[144,864]{1,0:T(8,128)(2,1)S(1)}, bf16[144,864]{1,0:T(8,128)(2,1)S(1)}, u32[]{:S(2)}, u32[]{:S(2)}) collective-permute-start(bf16[144,864]{1,0:T(8,128)(2,1)S(1)} %get-tuple-element.162), channel_id=1, source_target_pairs={{0,2},{1,3},{2,0},{3,1},{4,6},{5,7},{6,4},{7,5},{8,10},{9,11},{10,... | collective-permute-start | bytes 746504 | tf_op jit(solution)/shard_map/ppermute | solution.py:32
  603.2 40.9 %collective-permute-start.72 = (bf16[144,864]{1,0:T(8,128)(2,1)S(1)}, bf16[144,864]{1,0:T(8,128)(2,1)S(1)}, u32[]{:S(2)}, u32[]{:S(2)}) collective-permute-start(bf16[144,864]{1,0:T(8,128)(2,1)S(1)} %get-tuple-element.161), channel_id=1, source_target_pairs={{0,3},{1,2},{2,1},{3,0},{4,7},{5,6},{6,5},{7,4},{8,11},{9,10},{10,... | collective-permute-start | bytes 746504 | tf_op jit(solution)/shard_map/ppermute | solution.py:32
  (120 other events, 1627.2 us)

commit v2 on v1

v2 whole, which is shorter than its diff:
```python
import functools
import math

import jax
import jax.numpy as jnp
from jax import lax
from jax.experimental import pallas as pl
from jax.experimental.pallas import tpu as pltpu
from jax.sharding import PartitionSpec as P

HEADS = 16
HEAD = 72
LANES = 128
BLOCKS = 8

layer_eps = 1e-06
far_below = -1e30
att_scale = 1.0 / math.sqrt(HEAD)
gelu_c = math.sqrt(2.0 / math.pi)
gelu_k = 0.044715

BF = jnp.bfloat16
F32 = jnp.float32
VMEM = pl.BlockSpec(memory_space=pltpu.VMEM)
SMEM = pl.BlockSpec(memory_space=pltpu.SMEM)
ANY = pl.BlockSpec(memory_space=pl.ANY)
NT = (((1,), (1,)), ((), ()))
TN = (((0,), (0,)), ((), ()))


def swap(value, axis, step):
    return lax.ppermute(value, axis, [(i, i ^ step) for i in range(lax.axis_size(axis))])


def steps_of(axis):
    count = lax.axis_size(axis)
    return [1 << i for i in range(count.bit_length() - 1)]


def bit_set(axis, step):
    return (lax.axis_index(axis) & step) != 0


def gather_all(value, axis):
    value = value[None]
    for step in steps_of(axis):
        value = jnp.concatenate([value, swap(value, axis, step)], axis=0)
    return value


def sum_own(value, axis):
    for step in reversed(steps_of(axis)):
        value = value[:step] + swap(value[step:], axis, step)
    return value[0]


def trade_all(value, axis):
    count = value.shape[0]
    rest = value.shape[1:]
    for step in steps_of(axis):
        split = value.reshape((count // (2 * step), 2, step) + rest)
        value = jnp.stack([split[:, 0], swap(split[:, 1], axis, step)], axis=1).reshape(
            (count,) + rest
        )
    return value


def in_order(value, axis):
    count = value.shape[0]
    rest = value.shape[1:]
    for step in steps_of(axis):
        split = value.reshape((count // (2 * step), 2, step) + rest)
        value = jnp.where(bit_set(axis, step), split[:, ::-1], split).reshape((count,) + rest)
    return value


def sum_everywhere(value):
    for axis in ("dp", "seq"):
        for step in steps_of(axis):
            value = value + swap(value, axis, step)
    return value


def after(value, *earlier):
    return lax.optimization_barrier((value,) + earlier)[0]


def halves_of(rows):
    first = (rows // 2 + 15) // 16 * 16
    return first, rows - first


def pieces_of(own, own_pair, beside, beside_pair, across, across_pair, part):
    return [
        (own, 0, 0),
        (own_pair, 1, 0),
        (beside[0], 2, 0),
        (beside_pair[0], 3, 0),
        (beside[1], 4, 0),
        (beside_pair[1], 5, 0),
        (across[0], 6, 0),
        (across[1], 6, part),
        (across_pair[0], 7, 0),
        (across_pair[1], 7, part),
    ]


def beside_of(shard):
    return swap(shard, "dp", 2), swap(shard, "dp", 4)


def across_of(beside, part):
    return swap(beside[1][:part], "dp", 2), swap(beside[0][part:], "dp", 4)


def pair_of(values):
    return tuple(swap(v, "dp", 1) for v in values)


def whole_weight(shard):
    full = lax.all_gather(shard, "dp", axis=0, tiled=True)
    rows = full.shape[0] // BLOCKS
    return [(full[k * rows : (k + 1) * rows], k, 0) for k in range(BLOCKS)]


def offsets_of(pieces, position, rows):
    return jnp.stack([position(k) * rows + first for _, k, first in pieces]).astype(jnp.int32)


def call(kernel, outs, ins, specs, scratch, name):
    return pl.pallas_call(
        kernel,
        out_shape=outs,
        in_specs=specs,
        out_specs=jax.tree.map(lambda _: VMEM, outs),
        scratch_shapes=scratch,
        name=name,
        compiler_params=pltpu.CompilerParams(vmem_limit_bytes=56 * 1024 * 1024),
    )(*ins)


def start_pieces(offsets, refs, target, sem, lo, hi):
    copies = []
    for k, ref in enumerate(refs):
        rows = ref.shape[0]
        copies.append(
            pltpu.make_async_copy(
                ref.at[:, pl.ds(lo, hi - lo)],
                target.at[pl.ds(pl.multiple_of(offsets[k], 16), rows), :],
                sem.at[k],
            )
        )
    for one in copies:
        one.start()
    return copies


def wait_all(copies):
    for one in copies:
        one.wait()


def normal(rows_in):
    center = rows_in - jnp.mean(rows_in, axis=-1, keepdims=True)
    inverse = lax.rsqrt(jnp.mean(center * center, axis=-1, keepdims=True) + layer_eps)
    return center * inverse, inverse


def normal_back(grad_rows, normed, inverse):
    mean_grad = jnp.mean(grad_rows, axis=-1, keepdims=True)
    mean_proj = jnp.mean(grad_rows * normed, axis=-1, keepdims=True)
    return inverse * (grad_rows - mean_grad - normed * mean_proj)


def dot(left, right, dims=None):
    if dims is None:
        return jnp.dot(left, right, preferred_element_type=F32)
    return lax.dot_general(left, right, dims, preferred_element_type=F32)


def spans(total, width):
    return [(lo, min(lo + width, total)) for lo in range(0, total, width)]


def pack_rows(place_ref, piece_refs, latent, rows_out):
    gathered = jnp.concatenate([ref[latent] for ref in piece_refs], axis=0)
    slots = lax.broadcasted_iota(jnp.int32, (rows_out, gathered.shape[0]), 0)
    chosen = jnp.where(place_ref[latent] == slots, 1.0, 0.0).astype(BF)
    return dot(chosen, gathered)


def unpack_rows(place_ref, piece_refs, latent, packed, out_refs):
    rows_out = packed.shape[0]
    place = place_ref[latent]
    slots = lax.broadcasted_iota(jnp.int32, (place.shape[0], rows_out), 1)
    chosen = jnp.where(place == slots, 1.0, 0.0).astype(BF)
    spread = dot(chosen, packed)
    block = piece_refs[0].shape[1]
    for k, (piece, out) in enumerate(zip(piece_refs, out_refs)):
        here = slice(k * block, (k + 1) * block)
        out[latent] = jnp.where(
            place[here] >= 0, spread[here], piece[latent].astype(F32)
        ).astype(BF)


def split_parity(rows_low, order_ref, own_ref, other_ref):
    moved = dot(rows_low, order_ref[...]).astype(BF)
    width = own_ref.shape[1]
    own_ref[...] = moved[:, :width]
    other_ref[...] = moved[:, width:]


def enter_kernel(pieces, blocks, cap, *refs):
    (offsets, place, mod, order), refs = refs[:4], refs[4:]
    latents, refs = refs[:blocks], refs[blocks:]
    weights, refs = refs[:pieces], refs[pieces:]
    packed_out, qkv_out, own_out, other_out, weight, mixed, sem = refs
    width = qkv_out.shape[1]
    copies = start_pieces(offsets, weights, weight, sem, 0, width)
    for latent in range(mod.shape[0]):
        here = pl.ds(latent * cap, cap)
        rows = pack_rows(place, latents, latent, cap)
        packed_out[here, :] = rows.astype(BF)
        normed, _ = normal(rows)
        mixed[here, :] = (normed * (1.0 + mod[latent, 1:2, :]) + mod[latent, 0:1, :]).astype(BF)
    split_parity(mixed[...], order, own_out, other_out)
    wait_all(copies)
    for lo, hi in spans(width, 768):
        qkv_out[:, lo:hi] = dot(mixed[...], weight[:, lo:hi]).astype(BF)


def cot_kernel(blocks, cap, *refs):
    place, mod = refs[:2]
    cots = refs[2 : 2 + blocks]
    packed_out, mlp_out = refs[2 + blocks :]
    for latent in range(mod.shape[0]):
        here = pl.ds(latent * cap, cap)
        rows = pack_rows(place, cots, latent, cap)
        packed_out[here, :] = rows.astype(BF)
        mlp_out[here, :] = (mod[latent, 5:6, :] * rows).astype(BF)


def windows():
    found = []
    for head in range(HEADS):
        first = head * HEAD
        base = first // LANES * LANES
        width = LANES if first + HEAD <= base + LANES else 2 * LANES
        found.append((base, width, first - base))
    return found


def head_mask(width, first, dtype):
    lane = lax.broadcasted_iota(jnp.int32, (1, width), 1)
    return jnp.where((lane >= first) & (lane < first + HEAD), 1.0, 0.0).astype(dtype)


def attend_kernel(pieces, cap, model, *refs):
    (offsets, live, qkv, packed, mod, order), refs = refs[:6], refs[6:]
    weights, refs = refs[:pieces], refs[pieces:]
    (own_att, other_att, proj_out, hidden_out, mixed_out, own_mix, other_mix), refs = (
        refs[:7],
        refs[7:],
    )
    weight, attended, sem = refs
    copies = start_pieces(offsets, weights, weight, sem, 3 * model, 4 * model)
    attended[...] = jnp.zeros_like(attended)

    def one_latent(latent, carry):
        here = pl.ds(pl.multiple_of(latent * cap, 16), cap)
        count = live[latent]
        seen = lax.broadcasted_iota(jnp.int32, (cap, cap), 1) < count
        for base, width, first in windows():
            low_mask = head_mask(width, first, BF)
            query = qkv[here, base : base + width] * low_mask
            key = qkv[here, model + base : model + base + width]
            value = qkv[here, 2 * model + base : 2 * model + base + width]
            scores = jnp.where(seen, dot(query, key, NT) * att_scale, far_below)
            raised = jnp.exp(scores - jnp.max(scores, axis=-1, keepdims=True))
            total = jnp.sum(raised, axis=-1, keepdims=True)
            mixed = dot(raised.astype(BF), value) / total
            attended[here, base : base + width] += mixed * head_mask(width, first, F32)
        return carry

    lax.fori_loop(0, mod.shape[0], one_latent, 0)
    att_low = attended[...].astype(BF)
    split_parity(att_low, order, own_att, other_att)
    wait_all(copies)
    projected = dot(att_low, weight[...])
    proj_out[...] = projected
    for latent in range(mod.shape[0]):
        rows = slice(latent * cap, (latent + 1) * cap)
        hidden = packed[rows, :].astype(F32) + mod[latent, 2:3, :] * projected[rows]
        hidden_out[rows, :] = hidden
        normed, _ = normal(hidden)
        mixed_out[rows, :] = (
            normed * (1.0 + mod[latent, 4:5, :]) + mod[latent, 3:4, :]
        ).astype(BF)
    split_parity(mixed_out[...], order, own_mix, other_mix)


def first_kernel(pieces, *refs):
    (offsets, parity, mixed, bias), refs = refs[:4], refs[4:]
    weights, refs = refs[:pieces], refs[pieces:]
    own_act, other_act, own_slope, other_slope, weight, sem = refs
    copies = start_pieces(offsets, weights, weight, sem, 0, weight.shape[1])
    half = own_act.shape[1]
    wait_all(copies)
    for side, (act_out, slope_out) in enumerate(
        ((own_act, own_slope), (other_act, other_slope))
    ):
        base = (parity[0] ^ side) * half
        for lo, hi in spans(half, 768):
            cols = pl.ds(pl.multiple_of(base + lo, LANES), hi - lo)
            pre = dot(mixed[...], weight[:, cols]) + bias[:, cols]
            square = pre * pre
            curve = jnp.tanh(gelu_c * pre * (1.0 + gelu_k * square))
            cdf = 0.5 * (1.0 + curve)
            act_out[:, lo:hi] = (pre * cdf).astype(BF)
            slope = cdf + pre * (0.5 * gelu_c) * (1.0 - curve * curve) * (
                1.0 + 3.0 * gelu_k * square
            )
            slope_out[:, lo:hi] = slope.astype(BF)


def second_kernel(pieces, blocks, cap, *refs):
    (
        offsets,
        own_act,
        other_act,
        own_slope,
        other_slope,
        grad_mlp,
        grad_out,
        hidden,
        mod,
        place,
    ), refs = refs[:10], refs[10:]
    latents, refs = refs[:blocks], refs[blocks:]
    weights, refs = refs[:pieces], refs[pieces:]
    outs, refs = refs[:blocks], refs[blocks:]
    own_pre, other_pre, own_bias, other_bias, gate_grad, weight, sem = refs
    copies = start_pieces(offsets, weights, weight, sem, 0, weight.shape[1])
    half = own_act.shape[1]
    wait_all(copies)
    for side, (slope, pre_out, bias_out) in enumerate(
        ((own_slope, own_pre, own_bias), (other_slope, other_pre, other_bias))
    ):
        for lo, hi in spans(half, 768):
            grad_act = dot(grad_mlp[...], weight[side * half + lo : side * half + hi, :], NT)
            grad_pre = (grad_act * slope[:, lo:hi].astype(F32)).astype(BF)
            pre_out[:, lo:hi] = grad_pre
            bias_out[:, lo:hi] = jnp.sum(grad_pre.astype(F32), axis=0, keepdims=True)
    mlp = dot(own_act[...], weight[:half, :]) + dot(other_act[...], weight[half:, :])
    for latent in range(mod.shape[0]):
        rows = slice(latent * cap, (latent + 1) * cap)
        gate_grad[latent, :, :] = jnp.sum(
            grad_out[rows, :].astype(F32) * mlp[rows], axis=0, keepdims=True
        )
        block = (hidden[rows, :] + mod[latent, 5:6, :] * mlp[rows]).astype(BF)
        unpack_rows(place, latents, latent, block, outs)


def hidden_kernel(pieces, first_pieces, cap, model, *refs):
    (
        first_offsets,
        offsets,
        parity,
        own_pre,
        other_pre,
        hidden_in,
        projected,
        grad_out,
        mod,
    ), refs = refs[:9], refs[9:]
    first_weights, refs = refs[:first_pieces], refs[first_pieces:]
    out_weights, refs = refs[:pieces], refs[pieces:]
    grad_hidden, grad_proj, grad_att, mod_grads, first, out_weight, first_sem, out_sem = refs
    copies = start_pieces(first_offsets, first_weights, first, first_sem, 0, first.shape[1])
    later = start_pieces(offsets, out_weights, out_weight, out_sem, 3 * model, 4 * model)
    half = own_pre.shape[1]
    wait_all(copies)
    total = None
    for side, pre in enumerate((own_pre, other_pre)):
        base = (parity[0] ^ side) * half
        for lo, hi in spans(half, 768):
            cols = pl.ds(pl.multiple_of(base + lo, LANES), hi - lo)
            part = dot(pre[:, lo:hi], first[:, cols], NT)
            total = part if total is None else total + part
    for latent in range(mod.shape[0]):
        rows = slice(latent * cap, (latent + 1) * cap)
        normed, inverse = normal(hidden_in[rows, :])
        grad_mixed = total[rows]
        mod_grads[latent, 0:1, :] = jnp.sum(grad_mixed, axis=0, keepdims=True)
        mod_grads[latent, 1:2, :] = jnp.sum(grad_mixed * normed, axis=0, keepdims=True)
        grad = grad_out[rows, :].astype(F32) + normal_back(
            grad_mixed * (1.0 + mod[latent, 4:5, :]), normed, inverse
        )
        grad_hidden[rows, :] = grad
        mod_grads[latent, 2:3, :] = jnp.sum(grad * projected[rows, :], axis=0, keepdims=True)
        grad_proj[rows, :] = (mod[latent, 2:3, :] * grad).astype(BF)
    wait_all(later)
    grad_att[...] = dot(grad_proj[...], out_weight[...], NT).astype(BF)


def attend_back_kernel(cap, model, *refs):
    live, qkv, grad_att, grad_qkv, sums = refs
    sums[...] = jnp.zeros_like(sums)

    def one_latent(latent, carry):
        here = pl.ds(pl.multiple_of(latent * cap, 16), cap)
        count = live[latent]
        seen = lax.broadcasted_iota(jnp.int32, (cap, cap), 0) < count
        for base, width, first in windows():
            low_mask = head_mask(width, first, BF)
            wide_mask = head_mask(width, first, F32)
            cols = slice(base, base + width)
            key_cols = slice(model + base, model + base + width)
            value_cols = slice(2 * model + base, 2 * model + base + width)
            query, key, value = qkv[here, cols], qkv[here, key_cols], qkv[here, value_cols]
            grad = grad_att[here, cols]
            scores = jnp.where(seen, dot(key * low_mask, query, NT) * att_scale, far_below)
            raised = jnp.exp(scores - jnp.max(scores, axis=0, keepdims=True))
            probs = raised / jnp.sum(raised, axis=0, keepdims=True)
            grad_probs = dot(value * low_mask, grad, NT)
            delta = jnp.sum(probs * grad_probs, axis=0, keepdims=True)
            grad_scores = (probs * (grad_probs - delta)).astype(BF)
            scaled = wide_mask * att_scale
            sums[here, cols] += dot(grad_scores, key, TN) * scaled
            sums[here, key_cols] += dot(grad_scores, query) * scaled
            sums[here, value_cols] += dot(probs.astype(BF), grad) * wide_mask
        return carry

    lax.fori_loop(0, live.shape[0], one_latent, 0)
    grad_qkv[...] = sums[...].astype(BF)


def leave_kernel(pieces, blocks, cap, *refs):
    (offsets, grad_qkv, packed, grad_hidden, mod, place), refs = refs[:6], refs[6:]
    cots, refs = refs[:blocks], refs[blocks:]
    weights, refs = refs[:pieces], refs[pieces:]
    outs, refs = refs[:blocks], refs[blocks:]
    mod_grads, weight, sem = refs
    copies = start_pieces(offsets, weights, weight, sem, 0, weight.shape[1])
    wait_all(copies)
    total = None
    for lo, hi in spans(weight.shape[1], 768):
        part = dot(grad_qkv[:, lo:hi], weight[:, lo:hi], NT)
        total = part if total is None else total + part
    for latent in range(mod.shape[0]):
        rows = slice(latent * cap, (latent + 1) * cap)
        normed, inverse = normal(packed[rows, :].astype(F32))
        grad_mixed = total[rows]
        mod_grads[latent, 0:1, :] = jnp.sum(grad_mixed, axis=0, keepdims=True)
        mod_grads[latent, 1:2, :] = jnp.sum(grad_mixed * normed, axis=0, keepdims=True)
        grad = grad_hidden[rows, :] + normal_back(
            grad_mixed * (1.0 + mod[latent, 1:2, :]), normed, inverse
        )
        unpack_rows(place, cots, latent, grad.astype(BF), outs)


def outer_kernel(rows, used, sides, *refs):
    block_at, refs = refs[0], refs[1:]
    total = sum(sides)
    lefts, refs = refs[: 2 * len(sides)], refs[2 * len(sides) :]
    rights, refs = refs[: 2 * total], refs[2 * total :]
    (send_x, send_y, keep, keep_x, keep_y), refs = refs[:5], refs[5:]
    result, sem = refs
    part, rest = halves_of(rows)
    base, at = 0, 0
    for group, count in enumerate(sides):
        own_left, pair_left = lefts[2 * group : 2 * group + 2]
        left = jnp.concatenate([own_left[:, :used], pair_left[:, :used]], axis=0)
        for own, pair in zip(rights[2 * at : 2 * (at + count) : 2], rights[2 * at + 1 : 2 * (at + count) : 2]):
            width = own.shape[1]
            for lo, hi in spans(width, 768):
                right = jnp.concatenate([own[:, lo:hi], pair[:, lo:hi]], axis=0)
                result[:, base + lo : base + hi] = dot(left, right, TN).astype(BF)
            base += width
        at += count

    def rows_at(k, first, count):
        return result.at[pl.ds(pl.multiple_of(block_at[k] * rows + first, 16), count), :]

    moves = [
        (rows_at(1, 0, part), send_x.at[0]),
        (rows_at(3, 0, part), send_x.at[1]),
        (rows_at(2, part, rest), send_y.at[0]),
        (rows_at(3, part, rest), send_y.at[1]),
        (rows_at(0, 0, rows), keep),
        (rows_at(1, part, rest), keep_x),
        (rows_at(2, 0, part), keep_y),
    ]
    copies = [pltpu.make_async_copy(a, b, sem.at[i]) for i, (a, b) in enumerate(moves)]
    for one in copies:
        one.start()
    wait_all(copies)


def reorder_kernel(unit, shard, whole):
    count = shard.shape[1] // unit
    for block in range(count):
        to = (block % 2) * (count // 2) + block // 2
        whole[:, to * unit : (to + 1) * unit] = shard[:, block * unit : (block + 1) * unit]


def fold_kernel(cuts, *refs):
    (at, keep, near_top, near_bottom, far_top, far_bottom), refs = refs[:6], refs[6:]
    count = len(cuts[0])
    outs, refs = refs[: count * len(cuts)], refs[count * len(cuts) :]
    scratch, sem = refs[:-1], refs[-1]
    part = far_top.shape[0]
    wide = lambda ref: ref[...].astype(F32)
    top = keep[:part, :].astype(F32) + wide(near_top) + wide(far_top)
    bottom = keep[part:, :].astype(F32) + wide(near_bottom) + wide(far_bottom)
    copies = []
    for group, parts in zip(cuts, scratch):
        for j, pieces in enumerate(group):
            first = 0
            for lo, hi in pieces:
                parts[j, :part, first : first + hi - lo] = top[:, lo:hi].astype(BF)
                parts[j, part:, first : first + hi - lo] = bottom[:, lo:hi].astype(BF)
                first += hi - lo
        for k in range(count):
            i = len(copies)
            copies.append(pltpu.make_async_copy(parts.at[at[0] ^ k], outs[i], sem.at[i]))
    for one in copies:
        one.start()
    wait_all(copies)


def outer_pair(groups, rows, name):
    used = 4 * rows
    part, rest = halves_of(rows)
    lefts = [v for left, _ in groups for v in left]
    rights = [v for _, pairs in groups for pair in pairs for v in pair]
    width = sum(v.shape[1] for v in rights) // 2
    sides = tuple(len(pairs) for _, pairs in groups)
    block_at = jnp.stack([(lax.axis_index("dp") ^ (2 * k)) // 2 for k in range(4)]).astype(jnp.int32)
    ins = [block_at, *lefts, *rights]
    outs = (
        jax.ShapeDtypeStruct((2, part, width), BF),
        jax.ShapeDtypeStruct((2, rest, width), BF),
        jax.ShapeDtypeStruct((rows, width), BF),
        jax.ShapeDtypeStruct((rest, width), BF),
        jax.ShapeDtypeStruct((part, width), BF),
    )
    return pl.pallas_call(
        functools.partial(outer_kernel, rows, used, sides),
        out_shape=outs,
        in_specs=[SMEM] + [VMEM] * (len(ins) - 1),
        out_specs=tuple(ANY for _ in outs),
        scratch_shapes=[pltpu.VMEM((used, width), BF), pltpu.SemaphoreType.DMA((7,))],
        name=name,
        compiler_params=pltpu.CompilerParams(vmem_limit_bytes=56 * 1024 * 1024),
    )(*ins)


def near_sums(cut, from_x, from_y):
    _, _, _, keep_x, keep_y = cut
    on_y = (keep_y.astype(F32) + from_x[1].astype(F32)).astype(BF)
    on_x = (keep_x.astype(F32) + from_y[1].astype(F32)).astype(BF)
    return on_x, on_y


def fold(keep, from_x, from_y, far_top, far_bottom, cuts, name):
    rows = keep.shape[0]
    count = lax.axis_size("seq")
    at = lax.axis_index("seq").reshape(1).astype(jnp.int32)
    widths = tuple(sum(hi - lo for lo, hi in group[0]) for group in cuts)
    outs = tuple(jax.ShapeDtypeStruct((rows, w), BF) for w in widths for _ in range(count))
    return pl.pallas_call(
        functools.partial(fold_kernel, cuts),
        out_shape=outs,
        in_specs=[SMEM] + [VMEM] * 5,
        out_specs=tuple(ANY for _ in outs),
        scratch_shapes=[pltpu.VMEM((count, rows, w), BF) for w in widths]
        + [pltpu.SemaphoreType.DMA((len(outs),))],
        name=name,
        compiler_params=pltpu.CompilerParams(vmem_limit_bytes=40 * 1024 * 1024),
    )(at, keep, from_x[0], from_y[0], far_top, far_bottom)


def plain_cuts(first, width, count):
    share = width // count
    return tuple(((first + j * share, first + (j + 1) * share),) for j in range(count))


def spread_plain(grad):
    grad = lax.psum_scatter(grad, "dp", scatter_dimension=0, tiled=True)
    return lax.psum_scatter(grad, "seq", scatter_dimension=1, tiled=True)


def body(
    latents,
    condition,
    keep_order,
    keep_count,
    ada_weight,
    ada_bias,
    qkv_weight,
    out_weight,
    fc1_weight,
    fc1_bias,
    fc2_weight,
    cotangent,
):
    latent_count, block_rows, model = latents.shape
    hidden_units = fc1_weight.shape[1]
    half_units = hidden_units // 2
    unit_rows = hidden_units // BLOCKS
    model_rows = model // BLOCKS
    dp_count, seq_count = lax.axis_size("dp"), lax.axis_size("seq")
    dp_at, seq_at = lax.axis_index("dp"), lax.axis_index("seq")
    group = latent_count // seq_count
    cap = (seq_count - 1) * (block_rows * 3 // 4) + block_rows // 4
    rows_all = group * cap
    share = model // dp_count
    column_share = 6 * model // seq_count
    paired = dp_count == BLOCKS and seq_count == 4
    parity = (dp_at & 1) if paired else jnp.zeros_like(dp_at)
    parity_in = parity.reshape(1).astype(jnp.int32)
    part, _ = halves_of(model_rows)
    unit_part, _ = halves_of(unit_rows)
    whose = (lambda k: dp_at ^ k) if paired else (lambda k: jnp.int32(k))
    sds = jax.ShapeDtypeStruct
    dma = lambda n: pltpu.SemaphoreType.DMA((n,))
    fence = lambda *values: lax.optimization_barrier(values)

    def rank_of():
        slot = lax.broadcasted_iota(jnp.int32, (1, block_rows, 1), 1)
        token = lax.broadcasted_iota(jnp.int32, (1, 1, block_rows), 2)
        found = (keep_order[:, :, None] == token) & (slot < keep_count[:, :, None])
        return jnp.max(jnp.where(found, slot, -1), axis=1)

    def places_of(ranks):
        ranks = lax.dynamic_slice_in_dim(ranks, seq_at * group, group, 1)
        ranks = jnp.swapaxes(ranks, 0, 1)
        counts = jnp.sum((ranks >= 0).astype(jnp.int32), axis=2)
        starts = jnp.cumsum(counts, axis=1) - counts
        live = jnp.sum(counts, axis=1).astype(jnp.int32)
        place = jnp.where(ranks >= 0, ranks + starts[:, :, None], -1).reshape(
            group, seq_count * block_rows
        )
        return live, place[:, None, :], place[:, :, None]

    def whole_slice(blocks_in, k):
        return lax.dynamic_slice_in_dim(blocks_in, (seq_at ^ k) * group, group, 0)

    def put_slices(pieces, dtype):
        result = jnp.zeros((latent_count, block_rows, model), dtype)
        for k, piece in enumerate(pieces):
            result = lax.dynamic_update_slice_in_dim(
                result, piece.astype(dtype), (seq_at ^ k) * group, 0
            )
        return result

    cond_wide = condition.astype(F32)
    silu_cond = jax.nn.silu(cond_wide).astype(BF)
    silu_mine = lax.dynamic_slice_in_dim(silu_cond, seq_at * group, group, 0)
    silu_mine = in_order(jnp.swapaxes(silu_mine.reshape(group, dp_count, share), 0, 1), "dp")

    def partial_mod(silu_rows):
        return jnp.dot(
            silu_rows.reshape(dp_count * group, share), ada_weight, preferred_element_type=F32
        ).reshape(dp_count, group, 6 * model)

    def whole_mod(total):
        return (total + ada_bias.astype(F32)).reshape(group, 6, model)

    unit_order = lambda v: jnp.swapaxes(
        v.reshape(v.shape[0], BLOCKS // 2, 2, unit_rows), 1, 2
    ).reshape(v.shape[0], hidden_units)
    bias_row = unit_order(fc1_bias.astype(F32)[None])

    pad = -(-(model // 2) // LANES) * LANES
    column = lax.broadcasted_iota(jnp.int32, (1, 2 * pad), 1)
    side, inner = column // pad, column % pad
    source = (2 * (inner // model_rows) + (parity ^ side)) * model_rows + inner % model_rows
    source = jnp.where(inner < model // 2, source, -1)
    order = (lax.broadcasted_iota(jnp.int32, (model, 1), 0) == source).astype(BF)

    model_position = lambda k: whose(k)
    unit_position = lambda k: ((whose(k) & 1) ^ parity) * (BLOCKS // 2) + whose(k) // 2

    def run_enter(joint, place_row, mod, latent_pieces):
        weights = [v for v, _, _ in joint]
        return call(
            functools.partial(enter_kernel, len(weights), seq_count, cap),
            (
                sds((rows_all, model), BF),
                sds((rows_all, 3 * model), BF),
                sds((rows_all, pad), BF),
                sds((rows_all, pad), BF),
            ),
            [
                offsets_of(joint, model_position, model_rows),
                place_row,
                mod,
                order,
                *latent_pieces,
                *weights,
            ],
            [SMEM, VMEM, VMEM, VMEM] + [VMEM] * seq_count + [ANY] * len(weights),
            [
                pltpu.VMEM((model, 3 * model), BF),
                pltpu.VMEM((rows_all, model), BF),
                dma(len(weights)),
            ],
            "enter",
        )

    def run_cot(place_row, mod, cot_pieces):
        return call(
            functools.partial(cot_kernel, seq_count, cap),
            (sds((rows_all, model), BF), sds((rows_all, model), BF)),
            [place_row, mod, *cot_pieces],
            [VMEM] * (2 + seq_count),
            [],
            "cotangent",
        )

    def run_attend(joint, live, qkv, packed, mod):
        weights = [v for v, _, _ in joint]
        return call(
            functools.partial(attend_kernel, len(weights), cap, model),
            (
                sds((rows_all, pad), BF),
                sds((rows_all, pad), BF),
                sds((rows_all, model), F32),
                sds((rows_all, model), F32),
                sds((rows_all, model), BF),
                sds((rows_all, pad), BF),
                sds((rows_all, pad), BF),
            ),
            [
                offsets_of(joint, model_position, model_rows),
                live,
                qkv,
                packed,
                mod,
                order,
                *weights,
            ],
            [SMEM, SMEM, VMEM, VMEM, VMEM, VMEM] + [ANY] * len(weights),
            [
                pltpu.VMEM((model, model), BF),
                pltpu.VMEM((rows_all, model), F32),
                dma(len(weights)),
            ],
            "attend",
        )

    def run_first(first, mixed):
        weights = [v for v, _, _ in first]
        return call(
            functools.partial(first_kernel, len(weights)),
            tuple(sds((rows_all, half_units), BF) for _ in range(4)),
            [
                offsets_of(first, model_position, model_rows),
                parity_in,
                mixed,
                bias_row,
                *weights,
            ],
            [SMEM, SMEM, VMEM, VMEM] + [ANY] * len(weights),
            [pltpu.VMEM((model, hidden_units), BF), dma(len(weights))],
            "first",
        )

    def run_second(second, acts, grad_mlp, grad_out, hidden, mod, place_col, latent_pieces):
        weights = [v for v, _, _ in second]
        result = call(
            functools.partial(second_kernel, len(weights), seq_count, cap),
            tuple(sds((group, block_rows, model), BF) for _ in range(seq_count))
            + (
                sds((rows_all, half_units), BF),
                sds((rows_all, half_units), BF),
                sds((1, half_units), F32),
                sds((1, half_units), F32),
                sds((group, 1, model), F32),
            ),
            [
                offsets_of(second, unit_position, unit_rows),
                *acts,
                grad_mlp,
                grad_out,
                hidden,
                mod,
                place_col,
                *latent_pieces,
                *weights,
            ],
            [SMEM] + [VMEM] * (9 + seq_count) + [ANY] * len(weights),
            [pltpu.VMEM((hidden_units, model), BF), dma(len(weights))],
            "second",
        )
        return result[:seq_count], result[seq_count:]

    def run_hidden(first, joint, pres, hidden, projected, grad_out, mod):
        first_w = [v for v, _, _ in first]
        joint_w = [v for v, _, _ in joint]
        return call(
            functools.partial(hidden_kernel, len(joint_w), len(first_w), cap, model),
            (
                sds((rows_all, model), F32),
                sds((rows_all, model), BF),
                sds((rows_all, model), BF),
                sds((group, 3, model), F32),
            ),
            [
                offsets_of(first, model_position, model_rows),
                offsets_of(joint, model_position, model_rows),
                parity_in,
                *pres,
                hidden,
                projected,
                grad_out,
                mod,
                *first_w,
                *joint_w,
            ],
            [SMEM, SMEM, SMEM] + [VMEM] * 6 + [ANY] * (len(first_w) + len(joint_w)),
            [
                pltpu.VMEM((model, hidden_units), BF),
                pltpu.VMEM((model, model), BF),
                dma(len(first_w)),
                dma(len(joint_w)),
            ],
            "hidden_back",
        )

    def run_attend_back(live, qkv, grad_att):
        return call(
            functools.partial(attend_back_kernel, cap, model),
            sds((rows_all, 3 * model), BF),
            [live, qkv, grad_att],
            [SMEM, VMEM, VMEM],
            [pltpu.VMEM((rows_all, 3 * model), F32)],
            "attend_back",
        )

    def run_leave(joint, grad_qkv, packed, grad_hidden, mod, place_col, cot_pieces):
        weights = [v for v, _, _ in joint]
        result = call(
            functools.partial(leave_kernel, len(weights), seq_count, cap),
            tuple(sds((group, block_rows, model), BF) for _ in range(seq_count))
            + (sds((group, 2, model), F32),),
            [
                offsets_of(joint, model_position, model_rows),
                grad_qkv,
                packed,
                grad_hidden,
                mod,
                place_col,
                *cot_pieces,
                *weights,
            ],
            [SMEM] + [VMEM] * (5 + seq_count) + [ANY] * len(weights),
            [pltpu.VMEM((model, 3 * model), BF), dma(len(weights))],
            "leave",
        )
        return result[:seq_count], result[seq_count]

    def join_mod(mod_first, mod_grads, gate_m_grad):
        return jnp.concatenate(
            [mod_first, mod_grads[:, 2:3], mod_grads[:, :2], gate_m_grad], axis=1
        ).reshape(group, 6 * model)

    def join_sums(grad_mod, bias_own, bias_other):
        bias_pair = jnp.where(
            parity == 1,
            jnp.concatenate([bias_other, bias_own], axis=0),
            jnp.concatenate([bias_own, bias_other], axis=0),
        )
        bias_part = jnp.swapaxes(bias_pair.reshape(2, BLOCKS // 2, unit_rows), 0, 1)
        kept_part = jnp.sum(keep_count).astype(F32).reshape(1)
        return jnp.concatenate(
            [jnp.sum(grad_mod, axis=0), bias_part.reshape(hidden_units), kept_part]
        )

    def by_columns(grad_mod_all):
        return in_order(
            jnp.stack(
                [
                    grad_mod_all[:, :, j * column_share : (j + 1) * column_share]
                    for j in range(seq_count)
                ]
            ),
            "seq",
        )

    def cond_product(grad_mod_all):
        return dot(grad_mod_all.reshape(dp_count * group, 6 * model), ada_weight, NT).reshape(
            dp_count, group, share
        )

    def ada_product(silu_all, columns):
        return dot(
            silu_all.reshape(seq_count * dp_count * group, share),
            columns.reshape(seq_count * dp_count * group, column_share),
            TN,
        )

    def cond_end(rows):
        rows = in_order(rows, "seq").reshape(latent_count, model)
        _, silu_back = jax.vjp(jax.nn.silu, cond_wide)
        return silu_back(rows)[0]

    def cond_mine_of(cols):
        return jnp.swapaxes(in_order(cols, "dp"), 0, 1).reshape(group, model)

    def split_sums(sums):
        return (
            sums[: 6 * model],
            sums[6 * model : 6 * model + hidden_units],
            sums[6 * model + hidden_units :].astype(jnp.int32),
        )

    if not paired:
        live, place_row, place_col = places_of(gather_all(rank_of(), "seq"))
        silu_rows = trade_all(silu_mine, "dp")
        mod = whole_mod(sum_own(partial_mod(silu_rows), "dp"))
        to_whole = lambda v: [
            swap(whole_slice(v, k), "seq", k) if k else whole_slice(v, k)
            for k in range(seq_count)
        ]
        latent_pieces, cot_pieces = to_whole(latents), to_whole(cotangent)
        joint = whole_weight(jnp.concatenate([qkv_weight, out_weight], axis=1))
        first = whole_weight(unit_order(fc1_weight))
        second = whole_weight(fc2_weight)
        packed, qkv, *mixa = run_enter(joint, place_row, mod, latent_pieces)
        grad_out, grad_mlp = run_cot(place_row, mod, cot_pieces)
        att_own, att_other, projected, hidden, mixed, *mixm = run_attend(
            joint, live, qkv, packed, mod
        )
        acts = run_first(first, mixed)
        block_pieces, (*pres, bias_own, bias_other, gate_m_grad) = run_second(
            second, acts, grad_mlp, grad_out, hidden, mod, place_col, latent_pieces
        )
        grad_hidden, grad_proj, grad_att, mod_grads = run_hidden(
            first, joint, pres, hidden, projected, grad_out, mod
        )
        grad_qkv = run_attend_back(live, qkv, grad_att)
        latent_grads, mod_first = run_leave(
            joint, grad_qkv, packed, grad_hidden, mod, place_col, cot_pieces
        )
        grad_mod = join_mod(mod_first, mod_grads, gate_m_grad)
        sums = sum_everywhere(join_sums(grad_mod, bias_own, bias_other))
        grad_mod_all = gather_all(grad_mod.astype(BF), "dp")
        ada_grad = ada_product(
            gather_all(silu_rows, "seq"), trade_all(by_columns(grad_mod_all), "seq")
        )
        cond_cols = trade_all(cond_product(grad_mod_all), "dp")
        condition_grad = cond_end(gather_all(cond_mine_of(cond_cols), "seq"))

        def mixed_sides(own, other, width):
            both = jnp.stack([own[:, : 4 * width], other[:, : 4 * width]], axis=1)
            return jnp.swapaxes(both.reshape(rows_all, 2, 4, width), 1, 2).reshape(
                rows_all, BLOCKS * width
            )

        product = lambda a, b: spread_plain(dot(a, b, TN))
        fc2_grad = product(mixed_sides(acts[0], acts[1], unit_rows), grad_mlp)
        fc1_grad = product(
            mixed_sides(*mixm, model_rows), mixed_sides(pres[0], pres[1], unit_rows)
        )
        out_grad = product(mixed_sides(att_own, att_other, model_rows), grad_proj)
        qkv_grad = product(mixed_sides(*mixa, model_rows), grad_qkv)
        home = lambda pieces: [swap(v, "seq", k) if k else v for k, v in enumerate(pieces)]
        block_out = put_slices(home(block_pieces), BF)
        latents_grad = put_slices(home(latent_grads), F32)
        return (
            block_out,
            latents_grad,
            condition_grad,
            ada_grad,
            *split_sums(sums)[:1],
            qkv_grad,
            out_grad,
            fc1_grad,
            split_sums(sums)[1],
            fc2_grad,
            split_sums(sums)[2],
        )

    trade = lambda value, axis, step: jnp.stack(
        [
            (lambda split: split[:, 0])(value.reshape((-1, 2, step) + value.shape[1:])),
            swap(value.reshape((-1, 2, step) + value.shape[1:])[:, 1], axis, step),
        ],
        axis=1,
    ).reshape(value.shape)
    grow = lambda value, axis, step: jnp.concatenate([value, swap(value, axis, step)], axis=0)

    joint_own = jnp.concatenate([qkv_weight, out_weight], axis=1)
    first_own = pl.pallas_call(
        functools.partial(reorder_kernel, unit_rows),
        out_shape=sds(fc1_weight.shape, BF),
        in_specs=[VMEM],
        out_specs=VMEM,
        name="reorder",
        compiler_params=pltpu.CompilerParams(vmem_limit_bytes=40 * 1024 * 1024),
    )(fc1_weight)

    ranks = rank_of()[None]
    ranks = grow(ranks, "seq", 1)
    silu_rows = trade(silu_mine, "dp", 2)
    (joint_pair,) = pair_of((joint_own,))
    ranks, silu_rows, joint_pair, joint_own = fence(ranks, silu_rows, joint_pair, joint_own)
    ranks = grow(ranks, "seq", 2)
    silu_rows = trade(silu_rows, "dp", 4)
    ranks, silu_rows, joint_own, latents_in = fence(ranks, silu_rows, joint_own, latents)

    live, place_row, place_col = places_of(ranks)
    latent_pieces = [whole_slice(latents_in, k) for k in range(seq_count)]
    joint_beside = beside_of(joint_own)
    latent_1 = swap(latent_pieces[1], "seq", 1)
    latent_2 = swap(latent_pieces[2], "seq", 2)
    silu_rows = trade(silu_rows, "dp", 1)
    partial = partial_mod(silu_rows)
    pairs = partial.reshape(4, 2, group, 6 * model)
    chip_sum = pairs[:, 0] + swap(pairs[:, 1], "dp", 1)
    latent_3 = latent_pieces[3]
    joint_beside, latent_1, latent_2, chip_sum, silu_rows, latent_3 = fence(
        joint_beside, latent_1, latent_2, chip_sum, silu_rows, latent_3
    )

    joint_beside_pair = pair_of(joint_beside)
    cut = 3 * model
    corners = chip_sum.reshape(2, 2, group, 6 * model)
    sum_a = corners[:, 0, :, :cut] + swap(corners[:, 1, :, :cut], "dp", 2)
    sum_b = corners[0, :, :, cut:] + swap(corners[1, :, :, cut:], "dp", 4)
    joint_tails = (joint_beside[1][:part], joint_beside[0][part:])
    joint_beside_pair, sum_a, sum_b, joint_tails, latent_3 = fence(
        joint_beside_pair, sum_a, sum_b, joint_tails, latent_3
    )
    sum_a = sum_a[0] + swap(sum_a[1], "dp", 4)
    sum_b = sum_b[0] + swap(sum_b[1], "dp", 2)
    mod = whole_mod(jnp.concatenate([sum_a, sum_b], axis=1))
    mod, joint_tails, latent_3 = fence(mod, joint_tails, latent_3)

    latent_3 = swap(latent_3, "seq", 3)
    joint_across = (swap(joint_tails[0], "dp", 2), swap(joint_tails[1], "dp", 4))
    joint_across, latent_3, first_own, cot_in = fence(
        joint_across, latent_3, first_own, cotangent
    )

    first_beside = beside_of(first_own)
    joint_across_pair = pair_of(joint_across)
    joint = pieces_of(
        joint_own, joint_pair, joint_beside, joint_beside_pair, joint_across, joint_across_pair, part
    )
    latent_pieces = [latent_pieces[0], latent_1, latent_2, latent_3]
    packed, qkv, mixa_own, mixa_other = run_enter(joint, place_row, mod, latent_pieces)
    cot_pieces = [whole_slice(cot_in, k) for k in range(seq_count)]
    cot_1 = swap(cot_pieces[1], "seq", 1)
    first_beside, packed, qkv, mixa_own, mixa_other, cot_1, cot_2, cot_3 = fence(
        first_beside, packed, qkv, mixa_own, mixa_other, cot_1, cot_pieces[2], cot_pieces[3]
    )

    first_across = across_of(first_beside, part)
    first_beside_pair = pair_of(first_beside)
    (first_pair,) = pair_of((first_own,))
    cot_2 = swap(cot_2, "seq", 2)
    att_own, att_other, projected, hidden, mixed, mixm_own, mixm_other = run_attend(
        joint, live, qkv, packed, mod
    )
    first_across, first_beside_pair, first_pair, cot_2, mixed, att_own, second_own, cot_3 = fence(
        first_across, first_beside_pair, first_pair, cot_2, mixed, att_own, fc2_weight, cot_3
    )

    second_beside = beside_of(second_own)
    first_across_pair = pair_of(first_across)
    cot_3 = swap(cot_3, "seq", 3)
    first = pieces_of(
        first_own, first_pair, first_beside, first_beside_pair, first_across, first_across_pair, part
    )
    acts = run_first(first, mixed)
    second_beside, acts, cot_3 = fence(second_beside, acts, cot_3)

    second_across = across_of(second_beside, unit_part)
    second_beside_pair = pair_of(second_beside)
    (second_pair,) = pair_of((second_own,))
    cot_pieces = [cot_pieces[0], cot_1, cot_2, cot_3]
    grad_out, grad_mlp = run_cot(place_row, mod, cot_pieces)
    act_pair, grad_mlp_pair = pair_of((acts[1], grad_mlp))
    fc2_cut = outer_pair(
        [((acts[0], act_pair), [(grad_mlp, grad_mlp_pair)])], unit_rows, "fc2_grad"
    )
    second_across, second_beside_pair, second_pair, fc2_cut, grad_out, grad_mlp = fence(
        second_across, second_beside_pair, second_pair, fc2_cut, grad_out, grad_mlp
    )

    fc2_x, fc2_y = swap(fc2_cut[0], "dp", 2), swap(fc2_cut[1], "dp", 4)
    second_across_pair = pair_of(second_across)
    second = pieces_of(
        second_own,
        second_pair,
        second_beside,
        second_beside_pair,
        second_across,
        second_across_pair,
        unit_part,
    )
    block_pieces, (pre_own, pre_other, bias_own, bias_other, gate_m_grad) = run_second(
        second, acts, grad_mlp, grad_out, hidden, mod, place_col, latent_pieces
    )
    fc2_x, fc2_y, block_pieces, pre_own, pre_other, mixm_other, att_other, mixa_other = fence(
        fc2_x, fc2_y, block_pieces, pre_own, pre_other, mixm_other, att_other, mixa_other
    )

    on_x, on_y = near_sums(fc2_cut, fc2_x, fc2_y)
    fc2_far = (swap(on_y, "dp", 4), swap(on_x, "dp", 2))
    pre_other_pair, pre_own_pair, mixm_pair = pair_of((pre_own, pre_other, mixm_other))
    grad_hidden, grad_proj, grad_att, mod_grads = run_hidden(
        first, joint, (pre_own, pre_other), hidden, projected, grad_out, mod
    )
    fc1_cut = outer_pair(
        [((mixm_own, mixm_pair), [(pre_own, pre_own_pair), (pre_other, pre_other_pair)])],
        model_rows,
        "fc1_grad",
    )
    block_1 = swap(block_pieces[1], "seq", 1)
    fc2_far, grad_att, grad_proj, fc1_cut, block_1, block_2, block_3 = fence(
        fc2_far, grad_att, grad_proj, fc1_cut, block_1, block_pieces[2], block_pieces[3]
    )

    fc1_x, fc1_y = swap(fc1_cut[0], "dp", 2), swap(fc1_cut[1], "dp", 4)
    fc2_parts = fold(
        fc2_cut[2],
        fc2_x,
        fc2_y,
        *fc2_far,
        (plain_cuts(0, model, seq_count),),
        "fc2_fold",
    )
    fc2_1 = swap(fc2_parts[1], "seq", 1)
    block_2 = swap(block_2, "seq", 2)
    grad_qkv = run_attend_back(live, qkv, grad_att)
    latent_grads, mod_first = run_leave(
        joint, grad_qkv, packed, grad_hidden, mod, place_col, cot_pieces
    )
    proj_pair, att_pair, mixa_pair, qkv_pair = pair_of((grad_proj, att_other, mixa_other, grad_qkv))
    grad_mod = join_mod(mod_first, mod_grads, gate_m_grad)
    sums = join_sums(grad_mod, bias_own, bias_other)
    grad_mod_all = grad_mod.astype(BF)[None]
    (
        fc1_x,
        fc1_y,
        fc2_1,
        fc2_2,
        fc2_3,
        block_2,
        block_3,
        latent_grads,
        grad_qkv,
        proj_pair,
        att_pair,
        mixa_pair,
        qkv_pair,
        sums,
        grad_mod_all,
    ) = fence(
        fc1_x,
        fc1_y,
        fc2_1,
        fc2_parts[2],
        fc2_parts[3],
        block_2,
        block_3,
        latent_grads,
        grad_qkv,
        proj_pair,
        att_pair,
        mixa_pair,
        qkv_pair,
        sums,
        grad_mod_all,
    )

    on_x, on_y = near_sums(fc1_cut, fc1_x, fc1_y)
    fc1_far = (swap(on_y, "dp", 4), swap(on_x, "dp", 2))
    block_3 = swap(block_3, "seq", 3)
    last_cut = outer_pair(
        [
            ((mixa_own, mixa_pair), [(grad_qkv, qkv_pair)]),
            ((att_own, att_pair), [(grad_proj, proj_pair)]),
        ],
        model_rows,
        "last_grad",
    )
    sums = sums + swap(sums, "dp", 1)
    grad_mod_all = grow(grad_mod_all, "dp", 1)
    fc1_far, block_3, last_cut, sums, grad_mod_all, fc2_2, fc2_3, latent_grads = fence(
        fc1_far, block_3, last_cut, sums, grad_mod_all, fc2_2, fc2_3, latent_grads
    )
    block_out = put_slices((block_pieces[0], block_1, block_2, block_3), BF)
    sums = sums + swap(sums, "dp", 4)
    grad_mod_all = grow(grad_mod_all, "dp", 2)
    sums, grad_mod_all, last_cut = fence(sums, grad_mod_all, last_cut)
    sums = sums + swap(sums, "dp", 2)
    grad_mod_all = grow(grad_mod_all, "dp", 4)
    sums, grad_mod_all, last_cut, fc2_2, fc2_3, latent_grads = fence(
        sums, grad_mod_all, last_cut, fc2_2, fc2_3, latent_grads
    )

    last_x, last_y = swap(last_cut[0], "dp", 2), swap(last_cut[1], "dp", 4)
    fc1_cuts = tuple(
        tuple((lo, lo + unit_rows) for lo in (j * unit_rows, half_units + j * unit_rows))
        for j in range(seq_count)
    )
    fc1_parts = fold(fc1_cut[2], fc1_x, fc1_y, *fc1_far, (fc1_cuts,), "fc1_fold")
    fc2_2 = swap(fc2_2, "seq", 2)
    fc2_3 = swap(fc2_3, "seq", 3)
    cond_cols = trade(cond_product(grad_mod_all), "dp", 1)
    columns = by_columns(grad_mod_all)
    latent_1 = swap(latent_grads[1], "seq", 1)
    sums = sums + swap(sums, "seq", 1)
    last_x, last_y, fc2_2, fc2_3, cond_cols, columns, latent_1, sums, fc1_parts = fence(
        last_x, last_y, fc2_2, fc2_3, cond_cols, columns, latent_1, sums, fc1_parts
    )
    cond_cols = trade(cond_cols, "dp", 2)
    columns = trade(columns, "seq", 1)
    cond_cols, columns, last_x, last_y = fence(cond_cols, columns, last_x, last_y)
    cond_cols = trade(cond_cols, "dp", 4)
    columns = trade(columns, "seq", 2)
    cond_cols, columns, last_x, last_y, latent_2, latent_3, fc1_parts = fence(
        cond_cols, columns, last_x, last_y, latent_grads[2], latent_grads[3], fc1_parts
    )

    on_x, on_y = near_sums(last_cut, last_x, last_y)
    last_far = (swap(on_y, "dp", 4), swap(on_x, "dp", 2))
    fc2_grad = (
        fc2_parts[0].astype(F32)
        + fc2_1.astype(F32)
        + fc2_2.astype(F32)
        + fc2_3.astype(F32)
    )
    cond_rows = grow(cond_mine_of(cond_cols)[None], "seq", 1)
    silu_all = gather_all(silu_rows, "seq")
    ada_grad = ada_product(silu_all, columns)
    latent_2 = swap(latent_2, "seq", 2)
    latent_3 = swap(latent_3, "seq", 3)
    last_far, cond_rows, fc1_parts, latent_2, latent_3, sums = fence(
        last_far, cond_rows, fc1_parts, latent_2, latent_3, sums
    )

    last_parts = fold(
        last_cut[2],
        last_x,
        last_y,
        *last_far,
        (plain_cuts(0, 3 * model, seq_count), plain_cuts(3 * model, model, seq_count)),
        "last_fold",
    )
    sums = sums + swap(sums, "seq", 2)
    condition_grad = cond_end(grow(cond_rows, "seq", 2))
    gather_parts = lambda parts: sum(
        (swap(parts[k], "seq", k) if k else parts[0]).astype(F32) for k in range(seq_count)
    )
    fc1_grad = gather_parts(fc1_parts)
    fc1_grad = jnp.where(
        parity == 1,
        jnp.concatenate([fc1_grad[:, unit_rows:], fc1_grad[:, :unit_rows]], axis=1),
        fc1_grad,
    )
    qkv_grad = gather_parts(last_parts[:seq_count])
    out_grad = gather_parts(last_parts[seq_count:])
    latents_grad = put_slices((latent_grads[0], latent_1, latent_2, latent_3), F32)
    ada_bias_grad, fc1_bias_grad, kept_total = split_sums(sums)
    return (
        block_out,
        latents_grad,
        condition_grad,
        ada_grad,
        ada_bias_grad,
        qkv_grad,
        out_grad,
        fc1_grad,
        fc1_bias_grad,
        fc2_grad,
        kept_total,
    )


def solution(mesh):
    placed = (
        P("dp", "seq", None),
        P("dp", None),
        P("dp", "seq"),
        P("dp", "seq"),
        P("dp", None),
        P(),
        P("dp", None),
        P("dp", None),
        P("dp", None),
        P(),
        P("dp", None),
        P("dp", "seq", None),
    )
    return jax.shard_map(
        body,
        mesh=mesh,
        in_specs=placed,
        out_specs=(
            P("dp", "seq", None),
            P("dp", "seq", None),
            P("dp", None),
            P("dp", "seq"),
            P(),
            P("dp", "seq"),
            P("dp", "seq"),
            P("dp", "seq"),
            P(),
            P("dp", "seq"),
            P(),
        ),
        check_vma=False,
    )
```

time: 653 us -> 539 us (0.83)
  waiting for transfers between devices: 314 us -> 213 us
  starting transfers between devices: 96 us -> 84.8 us
  local copies, waits for them, and re-layouts: 62.5 us -> 54 us
    ppermute x101 -> x99, waiting for transfers between devices: 314 us -> 213 us  [swap(): lax.ppermute(value, axis, [(i, i ^ step) for i in range(lax.axis_size(axi...]
    ppermute x101 -> x99, starting transfers between devices: 96 us -> 84.8 us  [swap(): lax.ppermute(value, axis, [(i, i ^ step) for i in range(lax.axis_size(axi...]
    unnamed x135 -> x159, local copies, waits for them, and re-layouts: 9.19 us -> 17.9 us
    dynamic_slice x8 -> x2, local copies, waits for them, and re-layouts: 11.9 us -> 3.18 us  [whole_slice(): return lax.dynamic_slice_in_dim(blocks_in, (seq_at ^ k) * group, group, 0)]
    reshape x6 -> x5, local copies, waits for them, and re-layouts: 8.81 us -> 1.93 us  [the longest x1 1.21 us: body(): corners = chip_sum.reshape(2, 2, group, 6 * model)]
    pallas_call x4 -> x7, Pallas kernels: 31.5 us -> 36.5 us  [the longest x3 29.5 us: outer_pair(): pl.pallas_call(functools.partial(outer_kernel, rows, used, sides), out_sh...]
  transfers between devices with their start and end apart: 101 -> 99, of which waited for: 47 -> 45; matrix products, arithmetic and copies ran while one was open for 13% -> 13% of each run, Pallas kernels for 11% -> 22%
where the time goes in v2:
time: 539 us; the launch traced here: 528 us
  waiting for transfers between devices  213 us (40%)
  Pallas kernels  137 us (25%)
  starting transfers between devices  84.8 us (16%)
  local copies, waits for them, and re-layouts  54 us (10%)
  other arithmetic  31.7 us (6%)
    ppermute x99, waiting for transfers between devices, swap(): lax.ppermute(value, axis, [(i, i ^ step) for i in range(lax.axis_size(axi...  213 us
    pallas_call x8, Pallas kernels, call(): pl.pallas_call(kernel, out_shape=outs, in_specs=specs, out_specs=jax.tree...  100 us
    ppermute x99, starting transfers between devices, swap(): lax.ppermute(value, axis, [(i, i ^ step) for i in range(lax.axis_size(axi...  84.8 us
    pallas_call x3, Pallas kernels, outer_pair(): pl.pallas_call(functools.partial(outer_kernel, rows, used, sides), out_sh...  29.5 us
    unnamed x159, local copies, waits for them, and re-layouts  17.9 us
  transfers between devices with their start and end apart: 99, of which 45 were waited for; matrix products, arithmetic and copies ran while one was open for 13% of the time, Pallas kernels for 22%

profile of v2, /device:TPU:8, one launch (start us, length us, event | category | flops | bytes accessed | tf_op | source)
XLA Modules:
  0.0 528.4 jit_solution(6639103530610978895)
XLA Ops:
  10.2 2.6 collective-permute-start.3
  21.3 2.6 collective-permute-start.8
  25.2 8.7 %collective-permute-done.7.refs_5_.refs_11_ = bf16[2,64,1152]{2,1,0:T(8,128)(2,1)S(1)} collective-permute-done((bf16[2,64,1152]{2,1,0:T(8,128)(2,1)S(1)}, bf16[2,64,1152]{2,1,0:T(8,128)(2,1)S(1)}, u32[]{:S(2)}, u32[]{:S(2)}) %collective-permute-start.7) | collective-permute-done | bytes 294944 | tf_op jit(solution)/shard_map/ppermute | solution.py:32
  33.9 3.0 collective-permute-done.8.refs_6_.refs_12_
  37.0 10.0 %collective-permute-done.5.refs_10_.refs_8_.refs_21_.refs_12_ = bf16[144,4608]{1,0:T(8,128)(2,1)S(1)} collective-permute-done((bf16[144,4608]{1,0:T(8,128)(2,1)S(1)}, bf16[144,4608]{1,0:T(8,128)(2,1)S(1)}, u32[]{:S(2)}, u32[]{:S(2)}) %collective-permute-start.5) | collective-permute-done | bytes 1327136 | tf_op jit(solution)/shard_map/ppermute | solution.py:32
  55.1 2.9 collective-permute-done.13
  67.0 2.7 collective-permute-start.19
  71.3 8.9 %collective-permute-done.19.refs_7_.refs_13_ = bf16[2,64,1152]{2,1,0:T(8,128)(2,1)S(1)} collective-permute-done((bf16[2,64,1152]{2,1,0:T(8,128)(2,1)}, bf16[2,64,1152]{2,1,0:T(8,128)(2,1)S(1)}, u32[]{:S(2)}, u32[]{:S(2)}) %collective-permute-start.19) | collective-permute-done | bytes 294944 | tf_op jit(solution)/shard_map/ppermute | solution.py:32
  83.8 2.9 fusion.refs_3_.refs_5_
  87.3 2.3 constant_dynamic-slice_fusion
  89.5 2.1 collective-permute-start.24
  93.2 10.2 %enter.1 = (bf16[320,1152]{1,0:T(8,128)(2,1)}, bf16[320,3456]{1,0:T(8,128)(2,1)}, bf16[320,640]{1,0:T(8,128)(2,1)}, bf16[320,640]{1,0:T(8,128)(2,1)}) custom-call(s32[10]{0:T(128)} %stack.112.refs_0_.refs_1_, s32[2,1,256]{2,1,0:T(1,128)} %broadcast_in_dim_reshape.9.refs_1_.refs_0_, f32[2,6,1152]{2,1,0:T(8,128)} %maximum_add_fusion.refs_2_.refs_4_.refs_1_.refs_8_, ...), custom_call_target="tpu_custom_call" | custom-call | tf_op jit(solution)/shard_map/enter/pallas_call | solution.py:131
  103.4 7.8 %collective-permute-done.20.refs_6_.refs_11_ = bf16[144,4608]{1,0:T(8,128)(2,1)} collective-permute-done((bf16[144,4608]{1,0:T(8,128)(2,1)S(1)}, bf16[144,4608]{1,0:T(8,128)(2,1)}, u32[]{:S(2)}, u32[]{:S(2)}) %collective-permute-start.20) | collective-permute-done | bytes 1327136 | tf_op jit(solution)/shard_map/ppermute | solution.py:32
  117.4 11.7 %attend.1 = (bf16[320,640]{1,0:T(8,128)(2,1)}, bf16[320,640]{1,0:T(8,128)(2,1)}, f32[320,1152]{1,0:T(8,128)}, f32[320,1152]{1,0:T(8,128)}, bf16[320,1152]{1,0:T(...) custom-call(s32[10]{0:T(128)} %stack.112.refs_0_.refs_1_, s32[2]{0:T(128)} %get-tuple-element.562.refs_1_.refs_0_, ...), custom_call_target="tpu_custom_call" | custom-call | tf_op jit(solution)/shard_map/attend/pallas_call | solution.py:131
  138.2 13.8 %first.1 = (bf16[320,2304]{1,0:T(8,128)(2,1)}, bf16[320,2304]{1,0:T(8,128)(2,1)}, bf16[320,2304]{1,0:T(8,128)(2,1)}, bf16[320,2304]{1,0:T(8,128)(2,1)}) custom-call(s32[10]{0:T(128)} %stack.112.refs_0_.refs_1_, s32[1]{0:T(128)} %bitcast.41.refs_1_.refs_2_, bf16[320,1152]{1,0:T(8,128)(2,1)} %get-tuple-element.302.refs_2_, f32[1,4608]{1,0:T(1,128)} %reshape.307.refs_3_, ...), custom_call_target="tpu_custom_call" | custom-call | tf_op jit(solution)/shard_map/first/pallas_call | solution.py:131
  152.1 10.4 %collective-permute-done.31.refs_16_ = bf16[576,1152]{1,0:T(8,128)(2,1)S(1)} collective-permute-done((bf16[576,1152]{1,0:T(8,128)(2,1)}, bf16[576,1152]{1,0:T(8,128)(2,1)S(1)}, u32[]{:S(2)}, u32[]{:S(2)}) %collective-permute-start.31) | collective-permute-done | bytes 1327136 | tf_op jit(solution)/shard_map/ppermute | solution.py:32
  163.5 2.8 cotangent.1
  174.0 9.7 %fc2_grad.1 = (bf16[2,288,1152]{2,1,0:T(8,128)(2,1)}, bf16[2,288,1152]{2,1,0:T(8,128)(2,1)}, bf16[576,1152]{1,0:T(8,128)(2,1)}, bf16[288,1152]{1,0:T(8,128)(2,1)}, bf16[288,1152]{1,0:T(8,128)(2,1)}) custom-call(s32[4]{0:T(128)} %pad_add_fusion.2.refs_0_, bf16[320,2304]{1,0:T(8,128)(2,1)} %get-tuple-element.315.refs_1_, ...), custom_call_target="tpu_custom_call" | custom-call | tf_op jit(solution)/shard_map/fc2_grad/pallas_call | solution.py:548
  183.8 5.0 collective-permute-done.36.refs_20_
  195.4 18.3 %second.1 = (bf16[2,64,1152]{2,1,0:T(8,128)(2,1)}, bf16[2,64,1152]{2,1,0:T(8,128)(2,1)}, bf16[2,64,1152]{2,1,0:T(8,128)(2,1)}, bf16[2,64,1152]{2,1,0:T(8,128)(2,...) custom-call(s32[10]{0:T(128)} %stack.241.refs_0_, ...), custom_call_target="tpu_custom_call" | custom-call | tf_op jit(solution)/shard_map/second/pallas_call | solution.py:131
  213.7 6.2 %collective-permute-done.43 = bf16[2,288,1152]{2,1,0:T(8,128)(2,1)S(1)} collective-permute-done((bf16[2,288,1152]{2,1,0:T(8,128)(2,1)}, bf16[2,288,1152]{2,1,0:T(8,128)(2,1)S(1)}, u32[]{:S(2)}, u32[]{:S(2)}) %collective-permute-start.43) | collective-permute-done | bytes 1327136 | tf_op jit(solution)/shard_map/ppermute | solution.py:32
  221.5 2.1 fusion.7
  229.1 16.3 %hidden_back.1 = (f32[320,1152]{1,0:T(8,128)}, bf16[320,1152]{1,0:T(8,128)(2,1)}, bf16[320,1152]{1,0:T(8,128)(2,1)}, f32[2,3,1152]{2,1,0:T(4,128)}) custom-call(s32[10]{0:T(128)} %stack.112.refs_0_.refs_1_, s32[10]{0:T(128)} %stack.112.refs_0_.refs_1_, s32[1]{0:T(128)} %bitcast.41.refs_1_.refs_2_, bf16[320,2304]{1,0:T(8,128)(2,1)} %get-tuple-element.353.refs_3_, ...), custom_call_target="tpu_custom_call" | custom-call | tf_op jit(solution)/shard_map/hidden_back/pallas_call | solution.py:131
  247.0 9.7 %fc1_grad.1 = (bf16[2,80,4608]{2,1,0:T(8,128)(2,1)}, bf16[2,64,4608]{2,1,0:T(8,128)(2,1)}, bf16[144,4608]{1,0:T(8,128)(2,1)}, bf16[64,4608]{1,0:T(8,128)(2,1)}, bf16[80,4608]{1,0:T(8,128)(2,1)}) custom-call(s32[4]{0:T(128)} %pad_add_fusion.2.refs_0_, bf16[320,640]{1,0:T(8,128)(2,1)} %get-tuple-element.358.refs_1_, bf16[320,640]{1,0:T(8,128)(2,1)} %copy-done.51, ...), custom_call_target="tpu_custom_call" | custom-call | tf_op jit(solution)/shard_map/fc1_grad/pallas_call | solution.py:548
  256.8 15.3 %attend_back.1.refs_1_.refs_5_ = bf16[320,3456]{1,0:T(8,128)(2,1)} custom-call(s32[2]{0:T(128)} %get-tuple-element.562.refs_1_.refs_0_, bf16[320,3456]{1,0:T(8,128)(2,1)} %get-tuple-element.296.refs_2_.refs_1_, bf16[320,1152]{1,0:T(8,128)(2,1)} %get-tuple-element.379.refs_2_), custom_call_target="tpu_custom_call" | custom-call | tf_op jit(solution)/shard_map/attend_back/pallas_call | solution.py:131
  273.8 2.2 collective-permute-done.87
  284.7 12.0 %leave.1 = (bf16[2,64,1152]{2,1,0:T(8,128)(2,1)}, bf16[2,64,1152]{2,1,0:T(8,128)(2,1)}, bf16[2,64,1152]{2,1,0:T(8,128)(2,1)}, bf16[2,64,1152]{2,1,0:T(8,128)(2,1)}, f32[2,2,1152]{2,1,0:T(2,128)}) custom-call(s32[10]{0:T(128)} %stack.112.refs_0_.refs_1_, bf16[320,3456]{1,0:T(8,128)(2,1)} %attend_back.1.refs_1_.refs_5_, ...), custom_call_target="tpu_custom_call" | custom-call | tf_op jit(solution)/shard_map/leave/pallas_call | solution.py:131
  307.2 10.5 %collective-permute-done.55 = bf16[576,288]{1,0:T(8,128)(2,1)S(1)} collective-permute-done((bf16[576,288]{1,0:T(8,128)(2,1)}, bf16[576,288]{1,0:T(8,128)(2,1)S(1)}, u32[]{:S(2)}, u32[]{:S(2)}) %collective-permute-start.55) | collective-permute-done | bytes 331808 | tf_op jit(solution)/shard_map/ppermute | solution.py:32
  325.5 10.1 %last_grad.1 = (bf16[2,80,4608]{2,1,0:T(8,128)(2,1)}, bf16[2,64,4608]{2,1,0:T(8,128)(2,1)}, bf16[144,4608]{1,0:T(8,128)(2,1)}, bf16[64,4608]{1,0:T(8,128)(2,1)}, bf16[80,4608]{1,0:T(8,128)(2,1)}) custom-call(s32[4]{0:T(128)} %pad_add_fusion.2.refs_0_, bf16[320,640]{1,0:T(8,128)(2,1)} %get-tuple-element.399.refs_1_, ...), custom_call_target="tpu_custom_call" | custom-call | tf_op jit(solution)/shard_map/last_grad/pallas_call | solution.py:548
  335.7 4.2 collective-permute-done.63
  339.9 2.9 collective-permute-done.61.refs_4_
  363.8 21.5 %collective-permute-done.75 = bf16[2,64,1152]{2,1,0:T(8,128)(2,1)S(1)} collective-permute-done((bf16[2,64,1152]{2,1,0:T(8,128)(2,1)S(1)}, bf16[2,64,1152]{2,1,0:T(8,128)(2,1)S(1)}, u32[]{:S(2)}, u32[]{:S(2)}) %collective-permute-start.75) | collective-permute-done | bytes 294944 | tf_op jit(solution)/shard_map/ppermute | solution.py:32
  385.3 2.4 collective-permute-done.72
  387.7 10.9 %collective-permute-done.73 = bf16[576,288]{1,0:T(8,128)(2,1)S(1)} collective-permute-done((bf16[576,288]{1,0:T(8,128)(2,1)S(1)}, bf16[576,288]{1,0:T(8,128)(2,1)S(1)}, u32[]{:S(2)}, u32[]{:S(2)}) %collective-permute-start.73) | collective-permute-done | bytes 331808 | tf_op jit(solution)/shard_map/ppermute | solution.py:32
  404.4 4.1 collective-permute-done.78
  409.7 2.9 collective-permute-done.79
  412.6 2.7 collective-permute-done.80
  417.0 2.1 fusion.9
  430.1 13.2 %collective-permute-done.84 = bf16[2,64,1152]{2,1,0:T(8,128)(2,1)S(1)} collective-permute-done((bf16[2,64,1152]{2,1,0:T(8,128)(2,1)}, bf16[2,64,1152]{2,1,0:T(8,128)(2,1)S(1)}, u32[]{:S(2)}, u32[]{:S(2)}) %collective-permute-start.84) | collective-permute-done | bytes 294944 | tf_op jit(solution)/shard_map/ppermute | solution.py:32
  443.3 7.8 %collective-permute-done.85 = bf16[2,64,1152]{2,1,0:T(8,128)(2,1)S(1)} collective-permute-done((bf16[2,64,1152]{2,1,0:T(8,128)(2,1)}, bf16[2,64,1152]{2,1,0:T(8,128)(2,1)S(1)}, u32[]{:S(2)}, u32[]{:S(2)}) %collective-permute-start.85) | collective-permute-done | bytes 294944 | tf_op jit(solution)/shard_map/ppermute | solution.py:32
  451.1 3.9 last_fold.1
  462.3 8.4 %collective-permute-done.86 = f32[2,2,1152]{2,1,0:T(2,128)S(1)} collective-permute-done((f32[2,2,1152]{2,1,0:T(2,128)S(1)}, f32[2,2,1152]{2,1,0:T(2,128)S(1)}, u32[]{:S(2)}, u32[]{:S(2)}) %collective-permute-start.86) | collective-permute-done | bytes 18464 | tf_op jit(solution)/shard_map/ppermute | solution.py:32
  472.8 3.2 collective-permute-done.89
  481.5 3.7 collective-permute-start.96
  488.5 4.4 collective-permute-done.91
  493.0 20.5 %collective-permute-done.92 = bf16[144,864]{1,0:T(8,128)(2,1)S(1)} collective-permute-done((bf16[144,864]{1,0:T(8,128)(2,1)}, bf16[144,864]{1,0:T(8,128)(2,1)S(1)}, u32[]{:S(2)}, u32[]{:S(2)}) %collective-permute-start.92) | collective-permute-done | bytes 248864 | tf_op jit(solution)/shard_map/ppermute | solution.py:32
  515.4 2.4 collective-permute-done.97
  517.9 7.7 %collective-permute-done.98 = bf16[144,1152]{1,0:T(8,128)(2,1)S(1)} collective-permute-done((bf16[144,1152]{1,0:T(8,128)(2,1)S(1)}, bf16[144,1152]{1,0:T(8,128)(2,1)S(1)}, u32[]{:S(2)}, u32[]{:S(2)}) %collective-permute-start.98) | collective-permute-done | bytes 331808 | tf_op jit(solution)/shard_map/ppermute | solution.py:32
  (469 shorter events, 171.7 us)
Async XLA Ops:
  15.5 31.5 %collective-permute-start.5 = (bf16[144,4608]{1,0:T(8,128)(2,1)S(1)}, bf16[144,4608]{1,0:T(8,128)(2,1)S(1)}, u32[]{:S(2)}, u32[]{:S(2)}) collective-permute-start(bf16[144,4608]{1,0:T(8,128)(2,1)S(1)} %constant_dynamic-update-slice_fusion.refs_8_.refs_6_.refs_19_.refs_10_), channel_id=1, source_target_pairs={{0,8},{4,12},{8,0},{12,4},{16,24},{20,28},{24,16},{28,20},{1,9},{5... | collective-permute-start | bytes 3981320 | tf_op jit(solution)/shard_map/ppermute | solution.py:32
  17.0 31.3 %collective-permute-start.6 = (bf16[144,4608]{1,0:T(8,128)(2,1)S(1)}, bf16[144,4608]{1,0:T(8,128)(2,1)}, u32[]{:S(2)}, u32[]{:S(2)}) collective-permute-start(bf16[144,4608]{1,0:T(8,128)(2,1)S(1)} %constant_dynamic-update-slice_fusion.refs_8_.refs_6_.refs_19_.refs_10_), channel_id=1, source_target_pairs={{0,16},{4,20},{8,24},{12,28},{16,0},{20,4},{24,8},{28,12},{1,17},{... | collective-permute-start | bytes 3981320 | tf_op jit(solution)/shard_map/ppermute | solution.py:32
  81.4 29.8 %collective-permute-start.20 = (bf16[144,4608]{1,0:T(8,128)(2,1)S(1)}, bf16[144,4608]{1,0:T(8,128)(2,1)}, u32[]{:S(2)}, u32[]{:S(2)}) collective-permute-start(bf16[144,4608]{1,0:T(8,128)(2,1)S(1)} %reorder.1.refs_4_.refs_9_), channel_id=1, source_target_pairs={{0,8},{4,12},{8,0},{12,4},{16,24},{20,28},{24,16},{28,20},{1,9},{5... | collective-permute-start | bytes 3981320 | tf_op jit(solution)/shard_map/ppermute | solution.py:32
  82.6 29.1 %collective-permute-start.21 = (bf16[144,4608]{1,0:T(8,128)(2,1)S(1)}, bf16[144,4608]{1,0:T(8,128)(2,1)}, u32[]{:S(2)}, u32[]{:S(2)}) collective-permute-start(bf16[144,4608]{1,0:T(8,128)(2,1)S(1)} %reorder.1.refs_4_.refs_9_), channel_id=1, source_target_pairs={{0,16},{4,20},{8,24},{12,28},{16,0},{20,4},{24,8},{28,12},{1,17},{... | collective-permute-start | bytes 3981320 | tf_op jit(solution)/shard_map/ppermute | solution.py:32
  87.3 30.1 %collective-permute-start.29 = (bf16[144,4608]{1,0:T(8,128)(2,1)S(1)}, bf16[144,4608]{1,0:T(8,128)(2,1)}, u32[]{:S(2)}, u32[]{:S(2)}) collective-permute-start(bf16[144,4608]{1,0:T(8,128)(2,1)S(1)} %reorder.1.refs_4_.refs_9_), channel_id=1, source_target_pairs={{0,4},{4,0},{8,12},{12,8},{16,20},{20,16},{24,28},{28,24},{1,5},{5... | collective-permute-start | bytes 3981320 | tf_op jit(solution)/shard_map/ppermute | solution.py:32
  111.7 20.2 %collective-permute-start.27 = (bf16[144,4608]{1,0:T(8,128)(2,1)}, bf16[144,4608]{1,0:T(8,128)(2,1)}, u32[]{:S(2)}, u32[]{:S(2)}) collective-permute-start(bf16[144,4608]{1,0:T(8,128)(2,1)} %collective-permute-done.20.refs_6_.refs_11_), channel_id=1, source_target_pairs={{0,4},{4,0},{8,12},{12,8},{16,20},{20,16},{24,28},{28,24},{1,5},{5... | collective-permute-start | bytes 3981320 | tf_op jit(solution)/shard_map/ppermute | solution.py:32
  111.7 20.2 %collective-permute-start.28 = (bf16[144,4608]{1,0:T(8,128)(2,1)}, bf16[144,4608]{1,0:T(8,128)(2,1)}, u32[]{:S(2)}, u32[]{:S(2)}) collective-permute-start(bf16[144,4608]{1,0:T(8,128)(2,1)} %collective-permute-done.21.refs_8_.refs_13_), channel_id=1, source_target_pairs={{0,4},{4,0},{8,12},{12,8},{16,20},{20,16},{24,28},{28,24},{1,5},{5... | collective-permute-start | bytes 3981320 | tf_op jit(solution)/shard_map/ppermute | solution.py:32
  113.4 18.6 %collective-permute-start.25 = (bf16[80,4608]{1,0:T(8,128)(2,1)S(1)}, bf16[80,4608]{1,0:T(8,128)(2,1)}, u32[]{:S(2)}, u32[]{:S(2)}) collective-permute-start(bf16[80,4608]{1,0:T(8,128)(2,1)S(1)} %slice.183), channel_id=1, source_target_pairs={{0,8},{4,12},{8,0},{12,4},{16,24},{20,28},{24,16},{28,20},{1,9},{5... | collective-permute-start | bytes 2211848 | tf_op jit(solution)/shard_map/ppermute | solution.py:32
  132.0 30.5 %collective-permute-start.31 = (bf16[576,1152]{1,0:T(8,128)(2,1)}, bf16[576,1152]{1,0:T(8,128)(2,1)S(1)}, u32[]{:S(2)}, u32[]{:S(2)}) collective-permute-start(bf16[576,1152]{1,0:T(8,128)(2,1)} %refs_14_), channel_id=1, source_target_pairs={{0,8},{4,12},{8,0},{12,4},{16,24},{20,28},{24,16},{28,20},{1,9},{5... | collective-permute-start | bytes 3981320 | tf_op jit(solution)/shard_map/ppermute | solution.py:32
  133.3 30.2 %collective-permute-start.32 = (bf16[576,1152]{1,0:T(8,128)(2,1)}, bf16[576,1152]{1,0:T(8,128)(2,1)}, u32[]{:S(2)}, u32[]{:S(2)}) collective-permute-start(bf16[576,1152]{1,0:T(8,128)(2,1)} %refs_14_), channel_id=1, source_target_pairs={{0,16},{4,20},{8,24},{12,28},{16,0},{20,4},{24,8},{28,12},{1,17},{... | collective-permute-start | bytes 3981320 | tf_op jit(solution)/shard_map/ppermute | solution.py:32
  166.8 22.4 %collective-permute-start.38 = (bf16[576,1152]{1,0:T(8,128)(2,1)S(1)}, bf16[576,1152]{1,0:T(8,128)(2,1)}, u32[]{:S(2)}, u32[]{:S(2)}) collective-permute-start(bf16[576,1152]{1,0:T(8,128)(2,1)S(1)} %collective-permute-done.31.refs_16_), channel_id=1, source_target_pairs={{0,4},{4,0},{8,12},{12,8},{16,20},{20,16},{24,28},{28,24},{1,5},{5... | collective-permute-start | bytes 3981320 | tf_op jit(solution)/shard_map/ppermute | solution.py:32
  167.3 21.9 %collective-permute-start.39 = (bf16[576,1152]{1,0:T(8,128)(2,1)}, bf16[576,1152]{1,0:T(8,128)(2,1)}, u32[]{:S(2)}, u32[]{:S(2)}) collective-permute-start(bf16[576,1152]{1,0:T(8,128)(2,1)} %collective-permute-done.32.refs_18_), channel_id=1, source_target_pairs={{0,4},{4,0},{8,12},{12,8},{16,20},{20,16},{24,28},{28,24},{1,5},{5... | collective-permute-start | bytes 3981320 | tf_op jit(solution)/shard_map/ppermute | solution.py:32
  171.1 17.6 %collective-permute-start.36 = (bf16[288,1152]{1,0:T(8,128)(2,1)}, bf16[288,1152]{1,0:T(8,128)(2,1)}, u32[]{:S(2)}, u32[]{:S(2)}) collective-permute-start(bf16[288,1152]{1,0:T(8,128)(2,1)} %slice.185), channel_id=1, source_target_pairs={{0,8},{4,12},{8,0},{12,4},{16,24},{20,28},{24,16},{28,20},{1,9},{5... | collective-permute-start | bytes 1990664 | tf_op jit(solution)/shard_map/ppermute | solution.py:32
  171.9 17.4 %collective-permute-start.37 = (bf16[288,1152]{1,0:T(8,128)(2,1)}, bf16[288,1152]{1,0:T(8,128)(2,1)}, u32[]{:S(2)}, u32[]{:S(2)}) collective-permute-start(bf16[288,1152]{1,0:T(8,128)(2,1)} %slice.186), channel_id=1, source_target_pairs={{0,16},{4,20},{8,24},{12,28},{16,0},{20,4},{24,8},{28,12},{1,17},{... | collective-permute-start | bytes 1990664 | tf_op jit(solution)/shard_map/ppermute | solution.py:32
  189.2 30.6 %collective-permute-start.43 = (bf16[2,288,1152]{2,1,0:T(8,128)(2,1)}, bf16[2,288,1152]{2,1,0:T(8,128)(2,1)S(1)}, u32[]{:S(2)}, u32[]{:S(2)}) collective-permute-start(bf16[2,288,1152]{2,1,0:T(8,128)(2,1)} %get-tuple-element.327), channel_id=1, source_target_pairs={{0,8},{4,12},{8,0},{12,4},{16,24},{20,28},{24,16},{28,20},{1,9},{5... | collective-permute-start | bytes 3981320 | tf_op jit(solution)/shard_map/ppermute | solution.py:32
  190.5 30.5 %collective-permute-start.44 = (bf16[2,288,1152]{2,1,0:T(8,128)(2,1)}, bf16[2,288,1152]{2,1,0:T(8,128)(2,1)}, u32[]{:S(2)}, u32[]{:S(2)}) collective-permute-start(bf16[2,288,1152]{2,1,0:T(8,128)(2,1)} %get-tuple-element.328), channel_id=1, source_target_pairs={{0,16},{4,20},{8,24},{12,28},{16,0},{20,4},{24,8},{28,12},{1,17},{... | collective-permute-start | bytes 3981320 | tf_op jit(solution)/shard_map/ppermute | solution.py:32
  221.0 24.4 %collective-permute-start.50 = (bf16[320,2304]{1,0:T(8,128)(2,1)}, bf16[320,2304]{1,0:T(8,128)(2,1)S(1)}, u32[]{:S(2)}, u32[]{:S(2)}) collective-permute-start(bf16[320,2304]{1,0:T(8,128)(2,1)} %get-tuple-element.354.refs_4_.refs_5_), channel_id=1, source_target_pairs={{0,4},{4,0},{8,12},{12,8},{16,20},{20,16},{24,28},{28,24},{1,5},{5... | collective-permute-start | bytes 4423688 | tf_op jit(solution)/shard_map/ppermute | solution.py:32
  221.0 24.4 %collective-permute-start.51 = (bf16[320,2304]{1,0:T(8,128)(2,1)}, bf16[320,2304]{1,0:T(8,128)(2,1)S(1)}, u32[]{:S(2)}, u32[]{:S(2)}) collective-permute-start(bf16[320,2304]{1,0:T(8,128)(2,1)} %get-tuple-element.353.refs_3_), channel_id=1, source_target_pairs={{0,4},{4,0},{8,12},{12,8},{16,20},{20,16},{24,28},{28,24},{1,5},{5... | collective-permute-start | bytes 4423688 | tf_op jit(solution)/shard_map/ppermute | solution.py:32
  223.6 33.2 %collective-permute-start.48 = (bf16[288,1152]{1,0:T(8,128)(2,1)}, bf16[288,1152]{1,0:T(8,128)(2,1)S(1)}, u32[]{:S(2)}, u32[]{:S(2)}) collective-permute-start(bf16[288,1152]{1,0:T(8,128)(2,1)} %fusion.7), channel_id=1, source_target_pairs={{0,8},{4,12},{8,0},{12,4},{16,24},{20,28},{24,16},{28,20},{1,9},{5... | collective-permute-start | bytes 1990664 | tf_op jit(solution)/shard_map/ppermute | solution.py:32
  225.4 31.4 %collective-permute-start.47 = (bf16[288,1152]{1,0:T(8,128)(2,1)}, bf16[288,1152]{1,0:T(8,128)(2,1)S(1)}, u32[]{:S(2)}, u32[]{:S(2)}) collective-permute-start(bf16[288,1152]{1,0:T(8,128)(2,1)} %fusion.8), channel_id=1, source_target_pairs={{0,16},{4,20},{8,24},{12,28},{16,0},{20,4},{24,8},{28,12},{1,17},{... | collective-permute-start | bytes 1990664 | tf_op jit(solution)/shard_map/ppermute | solution.py:32
  227.1 29.6 %collective-permute-start.52 = (bf16[2,64,1152]{2,1,0:T(8,128)(2,1)}, bf16[2,64,1152]{2,1,0:T(8,128)(2,1)S(1)}, u32[]{:S(2)}, u32[]{:S(2)}) collective-permute-start(bf16[2,64,1152]{2,1,0:T(8,128)(2,1)} %get-tuple-element.365), channel_id=1, source_target_pairs={{0,1},{1,0},{2,3},{3,2},{4,5},{5,4},{6,7},{7,6},{8,9},{9,8},{10,11... | collective-permute-start | bytes 884744 | tf_op jit(solution)/shard_map/ppermute | solution.py:32
  272.2 45.6 %collective-permute-start.60 = (bf16[320,3456]{1,0:T(8,128)(2,1)}, bf16[320,3456]{1,0:T(8,128)(2,1)}, u32[]{:S(2)}, u32[]{:S(2)}) collective-permute-start(bf16[320,3456]{1,0:T(8,128)(2,1)} %attend_back.1.refs_1_.refs_5_), channel_id=1, source_target_pairs={{0,4},{4,0},{8,12},{12,8},{16,20},{20,16},{24,28},{28,24},{1,5},{5... | collective-permute-start | bytes 6635528 | tf_op jit(solution)/shard_map/ppermute | solution.py:32
  277.5 40.2 %collective-permute-start.53 = (bf16[2,80,4608]{2,1,0:T(8,128)(2,1)}, bf16[2,80,4608]{2,1,0:T(8,128)(2,1)}, u32[]{:S(2)}, u32[]{:S(2)}) collective-permute-start(bf16[2,80,4608]{2,1,0:T(8,128)(2,1)} %get-tuple-element.369), channel_id=1, source_target_pairs={{0,8},{4,12},{8,0},{12,4},{16,24},{20,28},{24,16},{28,20},{1,9},{5... | collective-permute-start | bytes 4423688 | tf_op jit(solution)/shard_map/ppermute | solution.py:32
  278.7 39.0 %collective-permute-start.54 = (bf16[2,64,4608]{2,1,0:T(8,128)(2,1)}, bf16[2,64,4608]{2,1,0:T(8,128)(2,1)}, u32[]{:S(2)}, u32[]{:S(2)}) collective-permute-start(bf16[2,64,4608]{2,1,0:T(8,128)(2,1)} %get-tuple-element.370), channel_id=1, source_target_pairs={{0,16},{4,20},{8,24},{12,28},{16,0},{20,4},{24,8},{28,12},{1,17},{... | collective-permute-start | bytes 3538952 | tf_op jit(solution)/shard_map/ppermute | solution.py:32
  280.7 37.1 %collective-permute-start.57 = (bf16[320,1152]{1,0:T(8,128)(2,1)}, bf16[320,1152]{1,0:T(8,128)(2,1)}, u32[]{:S(2)}, u32[]{:S(2)}) collective-permute-start(bf16[320,1152]{1,0:T(8,128)(2,1)} %get-tuple-element.385.refs_7_), channel_id=1, source_target_pairs={{0,4},{4,0},{8,12},{12,8},{16,20},{20,16},{24,28},{28,24},{1,5},{5... | collective-permute-start | bytes 2211848 | tf_op jit(solution)/shard_map/ppermute | solution.py:32
  280.7 24.4 %collective-permute-start.56 = (bf16[2,64,1152]{2,1,0:T(8,128)(2,1)}, bf16[2,64,1152]{2,1,0:T(8,128)(2,1)}, u32[]{:S(2)}, u32[]{:S(2)}) collective-permute-start(bf16[2,64,1152]{2,1,0:T(8,128)(2,1)} %get-tuple-element.377), channel_id=1, source_target_pairs={{0,2},{1,3},{2,0},{3,1},{4,6},{5,7},{6,4},{7,5},{8,10},{9,11},{10,... | collective-permute-start | bytes 884744 | tf_op jit(solution)/shard_map/ppermute | solution.py:32
  317.7 17.8 %collective-permute-start.65 = (bf16[1,2,6912]{2,1,0:T(2,128)(2,1)S(1)}, bf16[1,2,6912]{2,1,0:T(2,128)(2,1)S(1)}, u32[]{:S(2)}, u32[]{:S(2)}) collective-permute-start(bf16[1,2,6912]{2,1,0:T(2,128)(2,1)S(1)} %convert_element_type.179), channel_id=1, source_target_pairs={{0,4},{4,0},{8,12},{12,8},{16,20},{20,16},{24,28},{28,24},{1,5},{5... | collective-permute-start | bytes 82952 | tf_op jit(solution)/shard_map/ppermute | solution.py:32
  317.8 17.8 %collective-permute-start.64 = (f32[11521]{0:T(1024)S(1)}, f32[11521]{0:T(1024)S(1)}, u32[]{:S(2)}, u32[]{:S(2)}) collective-permute-start(f32[11521]{0:T(1024)S(1)} %pad_maximum_fusion.7), channel_id=1, source_target_pairs={{0,4},{4,0},{8,12},{12,8},{16,20},{20,16},{24,28},{28,24},{1,5},{5... | collective-permute-start | bytes 138260 | tf_op jit(solution)/shard_map/ppermute | solution.py:32
  320.7 19.2 %collective-permute-start.62 = (bf16[64,4608]{1,0:T(8,128)(2,1)S(1)}, bf16[64,4608]{1,0:T(8,128)(2,1)S(1)}, u32[]{:S(2)}, u32[]{:S(2)}) collective-permute-start(bf16[64,4608]{1,0:T(8,128)(2,1)S(1)} %fusion.10), channel_id=1, source_target_pairs={{0,8},{4,12},{8,0},{12,4},{16,24},{20,28},{24,16},{28,20},{1,9},{5... | collective-permute-start | bytes 1769480 | tf_op jit(solution)/shard_map/ppermute | solution.py:32
  324.6 18.3 %collective-permute-start.61 = (bf16[80,4608]{1,0:T(8,128)(2,1)S(1)}, bf16[80,4608]{1,0:T(8,128)(2,1)S(1)}, u32[]{:S(2)}, u32[]{:S(2)}) collective-permute-start(bf16[80,4608]{1,0:T(8,128)(2,1)S(1)} %fusion.6), channel_id=1, source_target_pairs={{0,16},{4,20},{8,24},{12,28},{16,0},{20,4},{24,8},{28,12},{1,17},{... | collective-permute-start | bytes 2211848 | tf_op jit(solution)/shard_map/ppermute | solution.py:32
  355.0 43.6 %collective-permute-start.70 = (bf16[2,80,4608]{2,1,0:T(8,128)(2,1)S(1)}, bf16[2,80,4608]{2,1,0:T(8,128)(2,1)S(1)}, u32[]{:S(2)}, u32[]{:S(2)}) collective-permute-start(bf16[2,80,4608]{2,1,0:T(8,128)(2,1)S(1)} %copy-done.70), channel_id=1, source_target_pairs={{0,8},{4,12},{8,0},{12,4},{16,24},{20,28},{24,16},{28,20},{1,9},{5... | collective-permute-start | bytes 4423688 | tf_op jit(solution)/shard_map/ppermute | solution.py:32
  356.0 42.6 %collective-permute-start.71 = (bf16[2,64,4608]{2,1,0:T(8,128)(2,1)S(1)}, bf16[2,64,4608]{2,1,0:T(8,128)(2,1)S(1)}, u32[]{:S(2)}, u32[]{:S(2)}) collective-permute-start(bf16[2,64,4608]{2,1,0:T(8,128)(2,1)S(1)} %copy-done.71), channel_id=1, source_target_pairs={{0,16},{4,20},{8,24},{12,28},{16,0},{20,4},{24,8},{28,12},{1,17},{... | collective-permute-start | bytes 3538952 | tf_op jit(solution)/shard_map/ppermute | solution.py:32
  357.3 30.4 %collective-permute-start.72 = (bf16[576,288]{1,0:T(8,128)(2,1)S(1)}, bf16[576,288]{1,0:T(8,128)(2,1)S(1)}, u32[]{:S(2)}, u32[]{:S(2)}) collective-permute-start(bf16[576,288]{1,0:T(8,128)(2,1)S(1)} %copy-done.18), channel_id=1, source_target_pairs={{0,2},{1,3},{2,0},{3,1},{4,6},{5,7},{6,4},{7,5},{8,10},{9,11},{10,... | collective-permute-start | bytes 995336 | tf_op jit(solution)/shard_map/ppermute | solution.py:32
  359.9 38.7 %collective-permute-start.73 = (bf16[576,288]{1,0:T(8,128)(2,1)S(1)}, bf16[576,288]{1,0:T(8,128)(2,1)S(1)}, u32[]{:S(2)}, u32[]{:S(2)}) collective-permute-start(bf16[576,288]{1,0:T(8,128)(2,1)S(1)} %copy-done.16), channel_id=1, source_target_pairs={{0,3},{1,2},{2,1},{3,0},{4,7},{5,6},{6,5},{7,4},{8,11},{9,10},{10,... | collective-permute-start | bytes 995336 | tf_op jit(solution)/shard_map/ppermute | solution.py:32
  361.7 23.5 %collective-permute-start.75 = (bf16[2,64,1152]{2,1,0:T(8,128)(2,1)S(1)}, bf16[2,64,1152]{2,1,0:T(8,128)(2,1)S(1)}, u32[]{:S(2)}, u32[]{:S(2)}) collective-permute-start(bf16[2,64,1152]{2,1,0:T(8,128)(2,1)S(1)} %copy-done.73), channel_id=1, source_target_pairs={{0,1},{1,0},{2,3},{3,2},{4,5},{5,4},{6,7},{7,6},{8,9},{9,8},{10,11... | collective-permute-start | bytes 884744 | tf_op jit(solution)/shard_map/ppermute | solution.py:32
  385.3 41.2 %collective-permute-start.88 = (bf16[2,8,2,144]{3,1,2,0:T(8,128)(2,1)}, bf16[2,8,2,144]{3,1,2,0:T(8,128)(2,1)}, u32[]{:S(2)}, u32[]{:S(2)}) collective-permute-start(bf16[2,8,2,144]{3,1,2,0:T(8,128)(2,1)} %pad_maximum_fusion.13), channel_id=1, source_target_pairs={{0,2},{1,3},{2,0},{3,1},{4,6},{5,7},{6,4},{7,5},{8,10},{9,11},{10,... | collective-permute-start | bytes 27656 | tf_op jit(solution)/shard_map/ppermute | solution.py:32
  420.2 30.9 %collective-permute-start.81 = (bf16[80,4608]{1,0:T(8,128)(2,1)}, bf16[80,4608]{1,0:T(8,128)(2,1)}, u32[]{:S(2)}, u32[]{:S(2)}) collective-permute-start(bf16[80,4608]{1,0:T(8,128)(2,1)} %fusion.5), channel_id=1, source_target_pairs={{0,16},{4,20},{8,24},{12,28},{16,0},{20,4},{24,8},{28,12},{1,17},{... | collective-permute-start | bytes 2211848 | tf_op jit(solution)/shard_map/ppermute | solution.py:32
  421.7 29.4 %collective-permute-start.82 = (bf16[64,4608]{1,0:T(8,128)(2,1)}, bf16[64,4608]{1,0:T(8,128)(2,1)}, u32[]{:S(2)}, u32[]{:S(2)}) collective-permute-start(bf16[64,4608]{1,0:T(8,128)(2,1)} %fusion.9), channel_id=1, source_target_pairs={{0,8},{4,12},{8,0},{12,4},{16,24},{20,28},{24,16},{28,20},{1,9},{5... | collective-permute-start | bytes 1769480 | tf_op jit(solution)/shard_map/ppermute | solution.py:32
  426.2 17.1 %collective-permute-start.84 = (bf16[2,64,1152]{2,1,0:T(8,128)(2,1)}, bf16[2,64,1152]{2,1,0:T(8,128)(2,1)S(1)}, u32[]{:S(2)}, u32[]{:S(2)}) collective-permute-start(bf16[2,64,1152]{2,1,0:T(8,128)(2,1)} %get-tuple-element.479), channel_id=1, source_target_pairs={{0,2},{1,3},{2,0},{3,1},{4,6},{5,7},{6,4},{7,5},{8,10},{9,11},{10,... | collective-permute-start | bytes 884744 | tf_op jit(solution)/shard_map/ppermute | solution.py:32
  426.5 24.6 %collective-permute-start.85 = (bf16[2,64,1152]{2,1,0:T(8,128)(2,1)}, bf16[2,64,1152]{2,1,0:T(8,128)(2,1)S(1)}, u32[]{:S(2)}, u32[]{:S(2)}) collective-permute-start(bf16[2,64,1152]{2,1,0:T(8,128)(2,1)} %get-tuple-element.480), channel_id=1, source_target_pairs={{0,3},{1,2},{2,1},{3,0},{4,7},{5,6},{6,5},{7,4},{8,11},{9,10},{10,... | collective-permute-start | bytes 884744 | tf_op jit(solution)/shard_map/ppermute | solution.py:32
  455.0 21.0 %collective-permute-start.93 = (bf16[144,288]{1,0:T(8,128)(2,1)}, bf16[144,288]{1,0:T(8,128)(2,1)}, u32[]{:S(2)}, u32[]{:S(2)}) collective-permute-start(bf16[144,288]{1,0:T(8,128)(2,1)} %get-tuple-element.496), channel_id=1, source_target_pairs={{0,1},{1,0},{2,3},{3,2},{4,5},{5,4},{6,7},{7,6},{8,9},{9,8},{10,11... | collective-permute-start | bytes 248840 | tf_op jit(solution)/shard_map/ppermute | solution.py:32
  455.1 26.4 %collective-permute-start.94 = (bf16[144,288]{1,0:T(8,128)(2,1)}, bf16[144,288]{1,0:T(8,128)(2,1)}, u32[]{:S(2)}, u32[]{:S(2)}) collective-permute-start(bf16[144,288]{1,0:T(8,128)(2,1)} %get-tuple-element.497), channel_id=1, source_target_pairs={{0,2},{1,3},{2,0},{3,1},{4,6},{5,7},{6,4},{7,5},{8,10},{9,11},{10,... | collective-permute-start | bytes 248840 | tf_op jit(solution)/shard_map/ppermute | solution.py:32
  457.1 28.1 %collective-permute-start.95 = (bf16[144,288]{1,0:T(8,128)(2,1)S(1)}, bf16[144,288]{1,0:T(8,128)(2,1)}, u32[]{:S(2)}, u32[]{:S(2)}) collective-permute-start(bf16[144,288]{1,0:T(8,128)(2,1)S(1)} %get-tuple-element.498), channel_id=1, source_target_pairs={{0,3},{1,2},{2,1},{3,0},{4,7},{5,6},{6,5},{7,4},{8,11},{9,10},{10,... | collective-permute-start | bytes 248840 | tf_op jit(solution)/shard_map/ppermute | solution.py:32
  458.6 26.6 %collective-permute-start.90 = (bf16[144,864]{1,0:T(8,128)(2,1)}, bf16[144,864]{1,0:T(8,128)(2,1)}, u32[]{:S(2)}, u32[]{:S(2)}) collective-permute-start(bf16[144,864]{1,0:T(8,128)(2,1)} %get-tuple-element.492), channel_id=1, source_target_pairs={{0,1},{1,0},{2,3},{3,2},{4,5},{5,4},{6,7},{7,6},{8,9},{9,8},{10,11... | collective-permute-start | bytes 746504 | tf_op jit(solution)/shard_map/ppermute | solution.py:32
  476.1 37.4 %collective-permute-start.92 = (bf16[144,864]{1,0:T(8,128)(2,1)}, bf16[144,864]{1,0:T(8,128)(2,1)S(1)}, u32[]{:S(2)}, u32[]{:S(2)}) collective-permute-start(bf16[144,864]{1,0:T(8,128)(2,1)} %copy-done.25), channel_id=1, source_target_pairs={{0,3},{1,2},{2,1},{3,0},{4,7},{5,6},{6,5},{7,4},{8,11},{9,10},{10,... | collective-permute-start | bytes 746504 | tf_op jit(solution)/shard_map/ppermute | solution.py:32
  481.5 33.9 %collective-permute-start.96 = (bf16[144,1152]{1,0:T(8,128)(2,1)S(1)}, bf16[144,1152]{1,0:T(8,128)(2,1)S(1)}, u32[]{:S(2)}, u32[]{:S(2)}) collective-permute-start(bf16[144,1152]{1,0:T(8,128)(2,1)S(1)} %copy-done.24), channel_id=1, source_target_pairs={{0,1},{1,0},{2,3},{3,2},{4,5},{5,4},{6,7},{7,6},{8,9},{9,8},{10,11... | collective-permute-start | bytes 995336 | tf_op jit(solution)/shard_map/ppermute | solution.py:32
  485.2 32.7 %collective-permute-start.97 = (bf16[144,1152]{1,0:T(8,128)(2,1)S(1)}, bf16[144,1152]{1,0:T(8,128)(2,1)S(1)}, u32[]{:S(2)}, u32[]{:S(2)}) collective-permute-start(bf16[144,1152]{1,0:T(8,128)(2,1)S(1)} %copy-done.22), channel_id=1, source_target_pairs={{0,2},{1,3},{2,0},{3,1},{4,6},{5,7},{6,4},{7,5},{8,10},{9,11},{10,... | collective-permute-start | bytes 995336 | tf_op jit(solution)/shard_map/ppermute | solution.py:32
  485.2 40.3 %collective-permute-start.98 = (bf16[144,1152]{1,0:T(8,128)(2,1)S(1)}, bf16[144,1152]{1,0:T(8,128)(2,1)S(1)}, u32[]{:S(2)}, u32[]{:S(2)}) collective-permute-start(bf16[144,1152]{1,0:T(8,128)(2,1)S(1)} %copy-done.20), channel_id=1, source_target_pairs={{0,3},{1,2},{2,1},{3,0},{4,7},{5,6},{6,5},{7,4},{8,11},{9,10},{10,... | collective-permute-start | bytes 995336 | tf_op jit(solution)/shard_map/ppermute | solution.py:32
  (126 other events, 1087.3 us)
